TPU v7x, 32 devices: a whole 2x2x4 slice. The times are simulated.
32 devices in a mesh: grp: 1, pen: 16 (over z, y, core), dep: 2 (over x), chan: 1.
Axes of the slice: x: 2, y: 2, z: 4, core: 2. Of those that a mesh axis runs over, the one named last changes fastest.
Arguments:
- misfit: float32 [6, 2048, 2048], P(('grp', 'chan'), ('pen', 'dep')), may hold values from -6 to 6
- kernel_spec: bfloat16 [6, 2, 2048, 2048], P('chan', None, ('pen', 'dep')), may hold values from -2.5 to 2.5
- model_vec: float32 [2, 16, 3072, 128], P(('grp', 'dep', 'chan'), 'pen'), may hold values from -1 to 1
- weight_vec: bfloat16 [2, 16, 3072, 128], P(('grp', 'dep', 'chan'), 'pen'), may hold values from 0.19921875 to 2
- active_list: int32 [2, 16, 2048], P(('grp', 'dep', 'chan'), 'pen'), may hold values from 0 to 2047, as said below
- send_counts: int32 [2, 16, 16], P(('grp', 'dep', 'chan'), 'pen'), may hold values from 0 to 192, as said below
Outputs:
- gradient: float32 [2, 2048, 2048], P(('grp', 'dep', 'chan'), 'pen')
- model_new: float32 [2, 16, 3072, 128], P(('grp', 'dep', 'chan'), 'pen')
- predicted: float32 [6, 2048, 2048], P(('grp', 'chan'), ('pen', 'dep'))
Inputs may be any that keep to these rules, and one draw needn't show every extreme that they name: For each layer and band, active_list is a permutation of the 2048 block ids: the active blocks in increasing order, then the others in increasing order; the number of active blocks equals the sum of send_counts over owners, and every active block of a layer is active in all deeper layers. `send_counts`: each entry is at most 192, reached in every draw; the counts of a band sum to its number of active blocks.
All inputs are finite; a program needn't handle non-finite values.
Results may differ from a plain program's by a relative error of at most 0.0003.
Values sent between devices are 32-bit elements; how exact they have to be, the bound alone decides.
No kernel may reach another device: no remote copies, remote signals or barrier semaphores. Data moves between devices by JAX's collectives and lax.ppermute only.
A program may use at most 128 MiB of HBM per device.

v0:
```python
import math

import jax
import jax.numpy as jnp
from jax import lax
from jax.sharding import PartitionSpec as P

inner_radix = 128
step_size = 0.5
highest = lax.Precision.HIGHEST
letters_free = "cdefghij"


def unit_table(length, direction):
    indices = jnp.arange(length, dtype=jnp.int32)
    phases = indices[:, None] * indices[None, :] % length
    angles = 2.0 * math.pi / length * phases.astype(jnp.float32)
    return (jnp.cos(angles), direction * jnp.sin(angles))


def twiddle_table(outer_size, inner_size, direction):
    length = outer_size * inner_size
    phases = (
        jnp.arange(outer_size, dtype=jnp.int32)[:, None]
        * jnp.arange(inner_size, dtype=jnp.int32)[None, :]
        % length
    )
    angles = 2.0 * math.pi / length * phases.astype(jnp.float32)
    return (jnp.cos(angles), direction * jnp.sin(angles))


def contract(formula, operand, tables, real_only):
    product_one = jnp.einsum(formula, operand[0], tables[0], precision=highest)
    if operand[1] is None:
        return (product_one, jnp.einsum(formula, operand[0], tables[1], precision=highest))
    real_value = product_one - jnp.einsum(formula, operand[1], tables[1], precision=highest)
    if real_only:
        return (real_value, None)
    imag_value = jnp.einsum(formula, operand[0], tables[1], precision=highest) + jnp.einsum(
        formula, operand[1], tables[0], precision=highest
    )
    return (real_value, imag_value)


def transform(operand, dimension, direction, real_only):
    full_shape = operand[0].shape
    length = full_shape[dimension]
    inner_size = min(inner_radix, length)
    outer_size = length // inner_size
    split_shape = full_shape[:dimension] + (outer_size, inner_size) + full_shape[dimension + 1 :]
    leading = letters_free[:dimension]
    trailing = letters_free[dimension : len(full_shape) - 1]
    pieces = tuple((None if member is None else member.reshape(split_shape) for member in operand))
    sectioned = contract(
        leading + "ab" + trailing + ",ak->" + leading + "kb" + trailing,
        pieces,
        unit_table(outer_size, direction),
        False,
    )
    twist_real, twist_imag = twiddle_table(outer_size, inner_size, direction)
    twist_shape = (outer_size, inner_size) + (1,) * len(trailing)
    twist_real = twist_real.reshape(twist_shape)
    twist_imag = twist_imag.reshape(twist_shape)
    rotated = (
        sectioned[0] * twist_real - sectioned[1] * twist_imag,
        sectioned[0] * twist_imag + sectioned[1] * twist_real,
    )
    factor = 1.0 / length if direction > 0 else 1.0
    if len(trailing) == 0:
        result = contract(
            leading + "kb,bm->" + leading + "km",
            rotated,
            unit_table(inner_size, direction),
            real_only,
        )
        return tuple(
            (
                (
                    None
                    if member is None
                    else jnp.swapaxes(member, -1, -2).reshape(full_shape) * factor
                )
                for member in result
            )
        )
    result = contract(
        leading + "kb" + trailing + ",bm->" + leading + "mk" + trailing,
        rotated,
        unit_table(inner_size, direction),
        real_only,
    )
    return tuple(
        (None if member is None else member.reshape(full_shape) * factor for member in result)
    )


def imag_channels(chan_place, chan_width):
    channel_ids = chan_place * chan_width + jnp.arange(chan_width, dtype=jnp.int32)
    return ((channel_ids == 2) | (channel_ids == 4))[:, None, None]


def channel_weighted(kernel_view, along):
    total = None
    for channel in range(kernel_view.shape[0]):
        kernel_now = kernel_view[channel].astype(jnp.float32)
        term = kernel_now * along[channel][None, None]
        total = term if total is None else total + term
    return total.reshape(-1, along.shape[1], along.shape[2])


def layer_weighted(kernel_view, grouped):
    ordered = jnp.swapaxes(grouped, 0, 1)
    outputs = []
    for channel in range(kernel_view.shape[0]):
        products = kernel_view[channel].astype(jnp.float32) * ordered
        outputs.append(jnp.sum(products, axis=(0, 1)))
    return jnp.stack(outputs)


def local(misfit, kernel_spec, model_vec, weight_vec, active_list, send_counts):
    pen_count = lax.axis_size("pen")
    dep_count = lax.axis_size("dep")
    chan_count = lax.axis_size("chan")
    chan_width, band_width, grid_width = misfit.shape
    column_width = kernel_spec.shape[2]
    kernel_view = kernel_spec.reshape(chan_width, dep_count, chan_count, column_width, grid_width)
    turned = imag_channels(lax.axis_index("chan"), chan_width)
    spectra_real, spectra_imag = transform((misfit, None), 2, -1.0, False)
    columns = (
        lax.all_to_all(spectra_real, ("pen", "dep"), split_axis=2, concat_axis=1, tiled=True),
        lax.all_to_all(spectra_imag, ("pen", "dep"), split_axis=2, concat_axis=1, tiled=True),
    )
    columns = (jnp.swapaxes(columns[0], 1, 2), jnp.swapaxes(columns[1], 1, 2))
    misfit_hat = transform(columns, 2, -1.0, False)
    along_real = jnp.where(turned, misfit_hat[1], misfit_hat[0])
    along_imag = jnp.where(turned, -misfit_hat[0], misfit_hat[1])
    partial_real = channel_weighted(kernel_view, along_real)
    partial_imag = channel_weighted(kernel_view, along_imag)
    fields = transform((partial_real, partial_imag), 2, 1.0, False)
    outgoing = tuple(
        (
            member.reshape(dep_count, chan_count, column_width, pen_count, -1)
            .transpose(3, 0, 1, 4, 2)
            .reshape(pen_count * dep_count, chan_count, -1, column_width)
            for member in fields
        )
    )
    arrived = (
        lax.all_to_all(outgoing[0], ("pen", "dep"), split_axis=0, concat_axis=3, tiled=True),
        lax.all_to_all(outgoing[1], ("pen", "dep"), split_axis=0, concat_axis=3, tiled=True),
    )
    real_fields = transform(arrived, 3, 1.0, True)[0]
    gradient = lax.psum_scatter(real_fields, "chan", scatter_dimension=1, tiled=True).reshape(
        1, -1, grid_width
    )
    blocks = gradient.reshape(-1, 128)
    block_count = blocks.shape[0]
    owner_length = model_vec.shape[2]
    slot_cap = owner_length // pen_count
    counts = send_counts.reshape(pen_count)
    starts = jnp.cumsum(counts) - counts
    slot_index = jnp.arange(slot_cap, dtype=jnp.int32)
    slot_valid = slot_index[None, :] < counts[:, None]
    in_list = jnp.minimum(starts[:, None] + slot_index[None, :], block_count - 1)
    listing = active_list.reshape(block_count)
    block_ids = listing[in_list]
    outgoing_blocks = jnp.where(slot_valid[:, :, None], blocks[block_ids], 0.0)
    incoming, arrived_counts = (
        lax.all_to_all(outgoing_blocks, "pen", split_axis=0, concat_axis=0, tiled=True),
        lax.all_to_all(counts.astype(jnp.float32), "pen", split_axis=0, concat_axis=0, tiled=True),
    )
    source_counts = arrived_counts.astype(jnp.int32)
    begins = jnp.cumsum(source_counts) - source_counts
    filled = slot_index[None, :] < source_counts[:, None]
    places = begins[:, None] + slot_index[None, :]
    safe_places = jnp.minimum(places, owner_length - 1)
    current = model_vec.reshape(owner_length, 128)
    scales = weight_vec.reshape(owner_length, 128)
    updated = jnp.clip(
        current[safe_places] - step_size * scales[safe_places].astype(jnp.float32) * incoming,
        -1.0,
        1.0,
    )
    targets = jnp.where(filled, places, owner_length)
    model_new = current.at[targets].set(updated, mode="drop").reshape(model_vec.shape)
    returned = lax.all_to_all(updated, "pen", split_axis=0, concat_axis=0, tiled=True)
    drop_ids = jnp.where(slot_valid, block_ids, block_count)
    model_grid = jnp.zeros((block_count, 128), jnp.float32).at[drop_ids].set(returned, mode="drop")
    model_grid = model_grid.reshape(-1, grid_width)
    surface_field = transform((model_grid, None), 1, -1.0, False)
    moved_columns = (
        lax.all_to_all(surface_field[0], ("pen", "dep"), split_axis=1, concat_axis=0, tiled=True),
        lax.all_to_all(surface_field[1], ("pen", "dep"), split_axis=1, concat_axis=0, tiled=True),
    )
    ordered = tuple(
        (
            member.reshape(pen_count, dep_count, -1, column_width)
            .transpose(1, 3, 0, 2)
            .reshape(dep_count, column_width, grid_width)
            for member in moved_columns
        )
    )
    model_hat = transform(ordered, 2, -1.0, False)
    layers_all = (
        lax.all_gather(model_hat[0], "chan", axis=0, tiled=True),
        lax.all_gather(model_hat[1], "chan", axis=0, tiled=True),
    )
    grouped = tuple(
        (member.reshape(chan_count, dep_count, column_width, grid_width) for member in layers_all)
    )
    summed_real = layer_weighted(kernel_view, grouped[0])
    summed_imag = layer_weighted(kernel_view, grouped[1])
    data_real = jnp.where(turned, -summed_imag, summed_real)
    data_imag = jnp.where(turned, summed_real, summed_imag)
    surface_rows = transform((data_real, data_imag), 2, 1.0, False)
    rows_back = (
        lax.all_to_all(surface_rows[0], ("pen", "dep"), split_axis=2, concat_axis=1, tiled=True),
        lax.all_to_all(surface_rows[1], ("pen", "dep"), split_axis=2, concat_axis=1, tiled=True),
    )
    predicted = jnp.swapaxes(transform(rows_back, 1, 1.0, True)[0], 1, 2)
    return (gradient, model_new, predicted)


def solution(mesh):
    return jax.shard_map(
        local,
        mesh=mesh,
        in_specs=(
            P(("grp", "chan"), ("pen", "dep"), None),
            P("chan", None, ("pen", "dep"), None),
            P(("grp", "dep", "chan"), "pen", None, None),
            P(("grp", "dep", "chan"), "pen", None, None),
            P(("grp", "dep", "chan"), "pen", None),
            P(("grp", "dep", "chan"), "pen", None),
        ),
        out_specs=(
            P(("grp", "dep", "chan"), "pen", None),
            P(("grp", "dep", "chan"), "pen", None, None),
            P(("grp", "chan"), ("pen", "dep"), None),
        ),
        check_vma=False,
    )
```

profile of v0, /device:TPU:0, one launch (start us, length us, event | category | flops | bytes accessed | tf_op | source)
XLA Modules:
  0.0 969.6 jit_solution(5816430865910839902)
XLA Ops:
  18.1 9.3 copy.394
  27.5 8.7 reshape.1037
  36.1 7.4 all-to-all-start.1
  53.8 9.3 copy.391
  63.2 8.7 reshape.1039
  71.8 42.9 %all-to-all-done.1 = f32[32,1,24576]{2,1,0:T(1,128)} async-done(((f32[32,1,24576]{2,1,0:T(1,128)}), f32[32,1,24576]{2,1,0:T(1,128)}, u32[]{:S(2)}, u32[]{:S(2)}) %all-to-all-start.1) | async-done | bytes 3145760 | tf_op jit(solution)/shard_map/all_to_all | solution.py:131
  129.2 11.9 %reduce.16 = f32[32,24576]{1,0:T(8,128)} reduce(f32[32,1,24576]{2,1,0:T(1,128)} %all-to-all-done.1, f32[]{:T(128)} %broadcast.1177), dimensions={1}, to_apply=%all_to_all.108.reduce_sub_computation | reduce | bytes 6291460 | tf_op jit(solution)/shard_map/all_to_all | solution.py:131
  141.1 7.1 reshape.1038
  148.2 9.7 %copy.288 = f32[6,32,64,64]{2,1,3,0:T(8,128)} copy(f32[6,32,64,64]{2,0,3,1:T(8,128)} %bitcast.570) | data formatting | bytes 6291456 | tf_op jit(solution)/shard_map/all_to_all | solution.py:131
  158.0 6.4 all_to_all.111
  173.1 17.4 %all-to-all-done = f32[32,1,24576]{2,1,0:T(1,128)} async-done(((f32[32,1,24576]{2,1,0:T(1,128)}), f32[32,1,24576]{2,1,0:T(1,128)}, u32[]{:S(2)}, u32[]{:S(2)}) %all-to-all-start) | async-done | bytes 3145760 | tf_op jit(solution)/shard_map/all_to_all | solution.py:130
  194.4 11.9 %reduce.17 = f32[32,24576]{1,0:T(8,128)} reduce(f32[32,1,24576]{2,1,0:T(1,128)} %all-to-all-done, f32[]{:T(128)} %broadcast.1177), dimensions={1}, to_apply=%all_to_all.104.reduce_sub_computation | reduce | bytes 6291460 | tf_op jit(solution)/shard_map/all_to_all | solution.py:130
  206.3 7.0 reshape.1040
  213.3 9.7 %copy.284 = f32[6,32,64,64]{2,1,3,0:T(8,128)} copy(f32[6,32,64,64]{2,0,3,1:T(8,128)} %bitcast.571) | data formatting | bytes 6291456 | tf_op jit(solution)/shard_map/all_to_all | solution.py:130
  223.0 6.8 all_to_all.107
  260.6 6.8 add_bitcast_fusion.1
  267.4 6.8 copy.289
  274.2 10.4 %fusion = (f32[6,64,2048]{1,2,0:T(8,128)}, f32[6,64,2048]{1,2,0:T(8,128)}) fusion(f32[6,64,128,16]{1,3,2,0:T(8,128)} %copy.290, f32[6,64,128,16]{1,3,2,0:T(8,128)} %copy.289, pred[6]{0:T(512)(128)(4,1)S(1)} %compare_or_fusion), kind=kLoop, calls=%fused_computation.8 | loop fusion | flops 2359296 | bytes 12582918 | tf_op jit(solution)/shard_map/jit(_where)/select_n | solution.py:136
  342.7 6.6 all-to-all-start.2
  356.8 18.7 %all-to-all-done.2 = f32[32,1,128,64]{2,3,1,0:T(8,128)} async-done(((f32[32,1,128,64]{2,3,1,0:T(8,128)}), f32[32,1,128,64]{2,3,1,0:T(8,128)}, u32[]{:S(2)}, u32[]{:S(2)}) %all-to-all-start.2) | async-done | bytes 1048608 | tf_op jit(solution)/shard_map/all_to_all | solution.py:149
  379.4 17.4 %gather_fusion.2 = s32[3072]{0:T(1024)S(1)} fusion(s32[2048]{0:T(1024)S(1)} %bitcast.566, s32[3072]{0:T(1024)S(1)} %broadcast_clamp_fusion.1), kind=kCustom, calls=%fused_computation.2 | custom fusion | bytes 36864 | tf_op jit(solution)/shard_map/gather | solution.py:166
  413.9 7.5 copy.318
  427.0 10.9 %gather_fusion.3 = f32[3072,128]{1,0:T(8,128)} fusion(f32[2048,128]{1,0:T(8,128)S(1)} %mul.1726, s32[3072]{0:T(1024)S(1)} %get-tuple-element.63), kind=kCustom, calls=%fused_computation.3 | custom fusion | bytes 3158016 | tf_op jit(solution)/shard_map/gather | solution.py:167
  445.4 10.9 %gather_fusion = f32[3072,128]{1,0:T(8,128)} fusion(f32[3072,128]{1,0:T(8,128)S(1)} %bitcast.567, s32[3072]{0:T(1024)S(1)} %get-tuple-element.64), kind=kCustom, calls=%fused_computation | custom fusion | bytes 3158016 | tf_op jit(solution)/shard_map/gather | solution.py:180
  456.3 9.1 gather_fusion.1
  466.7 10.2 %all-to-all-done.5 = f32[16,192,128]{2,1,0:T(8,128)} async-done(((f32[16,192,128]{2,1,0:T(8,128)}), f32[16,192,128]{2,1,0:T(8,128)}, u32[]{:S(2)}, u32[]{:S(2)}) %all-to-all-start.5) | async-done | bytes 1572896 | tf_op jit(solution)/shard_map/all_to_all | solution.py:169
  480.7 9.2 all-to-all-start.6
  490.1 32.0 %all-to-all-done.6 = f32[16,192,128]{2,1,0:T(8,128)} async-done(((f32[16,192,128]{2,1,0:T(8,128)}), f32[16,192,128]{2,1,0:T(8,128)}, u32[]{:S(2)}, u32[]{:S(2)}) %all-to-all-start.6) | async-done | bytes 1572896 | tf_op jit(solution)/shard_map/all_to_all | solution.py:186
  522.0 8.7 scatter_custom_fusion.1
  540.0 9.1 all-to-all-start.7
  555.2 20.1 %all-to-all-done.7 = f32[128,32,64]{0,2,1:T(8,128)} async-done(((f32[128,32,64]{0,2,1:T(8,128)}), f32[128,32,64]{0,2,1:T(8,128)}, u32[]{:S(2)}, u32[]{:S(2)}) %all-to-all-start.7) | async-done | bytes 1048608 | tf_op jit(solution)/shard_map/all_to_all | solution.py:192
  680.5 12.1 %broadcast_select_fusion = (f32[6,64,16,128]{1,3,2,0:T(8,128)}, f32[6,64,16,128]{1,3,2,0:T(8,128)}) fusion(f32[6,64,16,128]{1,3,2,0:T(8,128)} %constant_dynamic-update-slice_fusion.6, f32[6,64,16,128]{1,3,2,0:T(8,128)} %constant_dynamic-update-slice_fusion, pred[6]{0:T(512)(128)(4,1)S(1)} %compare_or_fusion), kind=kLoop, calls=%fused_computation.65 | loop fusion | flops 2359296 | bytes 12582918 | tf_op jit(solution)/shard_map/jit(_where)/select_n | solution.py:214
  698.7 6.5 fusion.210
  732.9 9.8 %copy.403 = f32[6,64,128,16]{1,0,3,2:T(8,128)} copy(f32[6,64,128,16]{2,3,1,0:T(8,128)} %multiply_bitcast_fusion.2) | data formatting | bytes 6291456 | tf_op jit(solution)/shard_map/mul | solution.py:81
  742.7 8.7 reshape.1041
  767.5 9.3 copy.406
  776.8 8.7 reshape.1043
  785.5 43.0 %all-to-all-done.9 = f32[32,1,24576]{2,1,0:T(1,128)} async-done(((f32[32,1,24576]{2,1,0:T(1,128)}), f32[32,1,24576]{2,1,0:T(1,128)}, u32[]{:S(2)}, u32[]{:S(2)}) %all-to-all-start.9) | async-done | bytes 3145760 | tf_op jit(solution)/shard_map/all_to_all | solution.py:217
  836.8 9.0 scatter_fusion
  845.8 11.9 %reduce.18 = f32[32,24576]{1,0:T(8,128)} reduce(f32[32,1,24576]{2,1,0:T(1,128)} %all-to-all-done.9, f32[]{:T(128)} %broadcast.1177), dimensions={1}, to_apply=%all_to_all.127.reduce_sub_computation | reduce | bytes 6291460 | tf_op jit(solution)/shard_map/all_to_all | solution.py:217
  857.8 7.0 reshape.1042
  864.8 9.7 %copy.369 = f32[6,32,64,64]{2,1,3,0:T(8,128)} copy(f32[6,32,64,64]{2,0,3,1:T(8,128)} %bitcast.572) | data formatting | bytes 6291456 | tf_op jit(solution)/shard_map/all_to_all | solution.py:217
  874.5 6.5 reshape.945
  881.0 6.5 fusion.207
  892.1 11.7 %all-to-all-done.10 = f32[32,1,24576]{2,1,0:T(1,128)} async-done(((f32[32,1,24576]{2,1,0:T(1,128)}), f32[32,1,24576]{2,1,0:T(1,128)}, u32[]{:S(2)}, u32[]{:S(2)}) %all-to-all-start.10) | async-done | bytes 3145760 | tf_op jit(solution)/shard_map/all_to_all | solution.py:218
  903.8 12.1 %reduce.19 = f32[32,24576]{1,0:T(8,128)} reduce(f32[32,1,24576]{2,1,0:T(1,128)} %all-to-all-done.10, f32[]{:T(128)} %broadcast.1177), dimensions={1}, to_apply=%all_to_all.130.reduce_sub_computation | reduce | bytes 6291460 | tf_op jit(solution)/shard_map/all_to_all | solution.py:218
  915.9 7.0 reshape.1044
  922.9 9.7 %copy.373 = f32[6,32,64,64]{2,1,3,0:T(8,128)} copy(f32[6,32,64,64]{2,0,3,1:T(8,128)} %bitcast.573) | data formatting | bytes 6291456 | tf_op jit(solution)/shard_map/all_to_all | solution.py:218
  (280 shorter events, 409.5 us)
Async XLA Ops:
  0.6 455.7 %copy-start = (bf16[1,1,3072,128]{3,2,1,0:T(8,128)(2,1)S(1)}, bf16[1,1,3072,128]{3,2,1,0:T(8,128)(2,1)}, u32[]{:S(2)}) copy-start(bf16[1,1,3072,128]{3,2,1,0:T(8,128)(2,1)} %param.9) | copy-start | bytes 2359300
  7.1 6.0 copy-start.7
  10.1 3.1 copy-start.9
  36.1 78.6 %all-to-all-start.1 = ((f32[32,1,24576]{2,1,0:T(1,128)}), f32[32,1,24576]{2,1,0:T(1,128)}, u32[]{:S(2)}, u32[]{:S(2)}) async-start(f32[32,1,24576]{2,1,0:T(1,128)} %reshape.1037), calls=%async_computation.1 | async-start | bytes 6291456 | tf_op jit(solution)/shard_map/all_to_all | solution.py:131
  43.6 5.5 copy-start.8
  43.6 5.5 copy-start.10
  114.8 75.7 %all-to-all-start = ((f32[32,1,24576]{2,1,0:T(1,128)}), f32[32,1,24576]{2,1,0:T(1,128)}, u32[]{:S(2)}, u32[]{:S(2)}) async-start(f32[32,1,24576]{2,1,0:T(1,128)} %reshape.1039), calls=%async_computation | async-start | bytes 6291456 | tf_op jit(solution)/shard_map/all_to_all | solution.py:130
  122.0 3.5 copy-start.26
  122.0 4.7 copy-start.24
  124.3 3.5 copy-start.53
  190.5 152.2 %all-to-all-start.4 = ((f32[16,1,1]{2,1,0:T(1,128)}), f32[16,1,1]{2,1,0:T(1,128)S(1)}, u32[]{:S(2)}, u32[]{:S(2)}) async-start(f32[16,1,1]{2,1,0:T(1,128)} %copy.316), calls=%async_computation.4 | async-start | bytes 16384 | tf_op jit(solution)/shard_map/all_to_all | solution.py:170
  238.6 10.9 %copy-start.13 = (f32[16,6,64,128]{3,0,2,1:T(8,128)}, f32[16,6,64,128]{3,0,2,1:T(8,128)S(1)}, u32[]{:S(2)}) copy-start(f32[16,6,64,128]{3,0,2,1:T(8,128)S(1)} %fusion.44) | copy-start | bytes 9437188
  241.7 7.8 copy-start.14
  342.7 32.8 %all-to-all-start.2 = ((f32[32,1,128,64]{2,3,1,0:T(8,128)}), f32[32,1,128,64]{2,3,1,0:T(8,128)}, u32[]{:S(2)}, u32[]{:S(2)}) async-start(f32[32,1,128,64]{2,3,1,0:T(8,128)} %bitcast.614), calls=%async_computation.2 | async-start | bytes 2097152 | tf_op jit(solution)/shard_map/all_to_all | solution.py:149
  355.2 24.2 %copy-start.2 = (s32[1,1,2048]{2,1,0:T(1,128)S(1)}, s32[1,1,2048]{2,1,0:T(1,128)}, u32[]{:S(2)}) copy-start(s32[1,1,2048]{2,1,0:T(1,128)} %param.10) | copy-start | bytes 24580
  375.5 30.0 %all-to-all-start.3 = ((f32[32,1,128,64]{2,3,1,0:T(8,128)}), f32[32,1,128,64]{2,3,1,0:T(8,128)}, u32[]{:S(2)}, u32[]{:S(2)}) async-start(f32[32,1,128,64]{2,3,1,0:T(8,128)} %bitcast.613), calls=%async_computation.3 | async-start | bytes 2097152 | tf_op jit(solution)/shard_map/all_to_all | solution.py:150
  437.9 7.5 copy-start.3
  440.6 36.4 %all-to-all-start.5 = ((f32[16,192,128]{2,1,0:T(8,128)}), f32[16,192,128]{2,1,0:T(8,128)}, u32[]{:S(2)}, u32[]{:S(2)}) async-start(f32[16,192,128]{2,1,0:T(8,128)} %broadcast_select_fusion.1), calls=%async_computation.5 | async-start | bytes 3145728 | tf_op jit(solution)/shard_map/all_to_all | solution.py:169
  480.7 41.3 %all-to-all-start.6 = ((f32[16,192,128]{2,1,0:T(8,128)}), f32[16,192,128]{2,1,0:T(8,128)}, u32[]{:S(2)}, u32[]{:S(2)}) async-start(f32[16,192,128]{2,1,0:T(8,128)} %subtract_clamp_fusion), calls=%async_computation.6 | async-start | bytes 3145728 | tf_op jit(solution)/shard_map/all_to_all | solution.py:186
  535.2 4.8 copy-start.34
  540.0 35.3 %all-to-all-start.7 = ((f32[128,32,64]{0,2,1:T(8,128)}), f32[128,32,64]{0,2,1:T(8,128)}, u32[]{:S(2)}, u32[]{:S(2)}) async-start(f32[128,32,64]{0,2,1:T(8,128)} %bitcast.637), calls=%async_computation.7 | async-start | bytes 2097152 | tf_op jit(solution)/shard_map/all_to_all | solution.py:192
  575.3 48.1 %all-to-all-start.8 = ((f32[128,32,64]{0,2,1:T(8,128)}), f32[128,32,64]{0,2,1:T(8,128)}, u32[]{:S(2)}, u32[]{:S(2)}) async-start(f32[128,32,64]{0,2,1:T(8,128)} %bitcast.114), calls=%async_computation.8 | async-start | bytes 2097152 | tf_op jit(solution)/shard_map/all_to_all | solution.py:193
  579.1 6.4 copy-start.29
  587.5 6.4 copy-start.25
  623.4 3.6 copy-start.42
  641.0 5.0 copy-start.52
  641.0 6.5 copy-start.51
  667.0 4.9 copy-start.47
  667.0 6.0 copy-start.45
  671.9 3.2 copy-start.48
  673.0 3.2 copy-start.49
  674.1 3.2 copy-start.46
  675.1 3.2 copy-start.43
  676.2 3.2 copy-start.44
  698.7 6.5 copy-start.17
  716.1 6.0 copy-start.20
  716.1 6.0 copy-start.23
  722.1 6.1 copy-start.5
  751.4 77.1 %all-to-all-start.9 = ((f32[32,1,24576]{2,1,0:T(1,128)}), f32[32,1,24576]{2,1,0:T(1,128)}, u32[]{:S(2)}, u32[]{:S(2)}) async-start(f32[32,1,24576]{2,1,0:T(1,128)} %reshape.1041), calls=%async_computation.9 | async-start | bytes 6291456 | tf_op jit(solution)/shard_map/all_to_all | solution.py:217
  757.3 5.5 copy-start.6
  757.3 5.5 copy-start.12
  785.5 47.2 %copy-start.33 = (f32[1,1,128,128,16]{2,3,4,1,0:T(8,128)S(1)}, f32[1,1,128,128,16]{2,3,4,1,0:T(8,128)}, u32[]{:S(2)}) copy-start(f32[1,1,128,128,16]{2,3,4,1,0:T(8,128)} %copy-done.32) | copy-start | bytes 3145732
  828.5 75.3 %all-to-all-start.10 = ((f32[32,1,24576]{2,1,0:T(1,128)}), f32[32,1,24576]{2,1,0:T(1,128)}, u32[]{:S(2)}, u32[]{:S(2)}) async-start(f32[32,1,24576]{2,1,0:T(1,128)} %reshape.1043), calls=%async_computation.10 | async-start | bytes 6291456 | tf_op jit(solution)/shard_map/all_to_all | solution.py:218
  845.8 11.9 %copy-start.4 = (f32[3072,128]{1,0:T(8,128)}, f32[3072,128]{1,0:T(8,128)S(1)}, u32[]{:S(2)}) copy-start(f32[3072,128]{1,0:T(8,128)S(1)} %scatter_fusion) | copy-start | bytes 4718596
  881.0 6.5 copy-start.18
  938.7 5.8 copy-start.19
  938.7 5.8 copy-start.22
  963.2 6.2 copy-start.1
  (17 other events, 37.9 us)
where the time goes:
time: 983 us; the launch traced here: 970 us
  local copies, waits for them, and re-layouts  442 us (45%)
  waiting for transfers between devices  199 us (20%)
  matrix products  177 us (18%)
  other arithmetic  86.5 us (9%)
  starting transfers between devices  63.1 us (6%)
    unnamed x138, local copies, waits for them, and re-layouts  105 us
    dot_general x16, matrix products, contract(): product_one = jnp.einsum(formula, operand[0], tables[0], precision=highest)  49.6 us
    dot_general x14, matrix products, contract(): jnp.einsum(formula, operand[0], tables[1], precision=highest)  47.5 us
    dot_general x12, matrix products, contract(): jnp.einsum(formula, operand[1], tables[0], precision=highest)  43.6 us
    all_to_all x1, waiting for transfers between devices, local(): lax.all_to_all(surface_rows[0], ('pen', 'dep'), split_axis=2, concat_axis...  43 us
    all_to_all x1, waiting for transfers between devices, local(): lax.all_to_all(spectra_imag, ('pen', 'dep'), split_axis=2, concat_axis=1,...  42.9 us
    mul x7, local copies, waits for them, and re-layouts, transform(): jnp.swapaxes(member, -1, -2).reshape(full_shape) * factor  39.5 us
    convert_element_type x12, local copies, waits for them, and re-layouts, channel_weighted(): kernel_now = kernel_view[channel].astype(jnp.float32)  36.9 us
  transfers between devices with their start and end apart: 11, of which 9 were waited for; matrix products, arithmetic and copies ran while one was open for 42% of the time, Pallas kernels for 0%

commit v1 on v0

--- a/solution.py
+++ b/solution.py
@@ -1,8 +1,13 @@
+import functools
 import math
 
 import jax
 import jax.numpy as jnp
+import ml_dtypes
+import numpy as np
 from jax import lax
+from jax.experimental import pallas as pl
+from jax.experimental.pallas import tpu as pltpu
 from jax.sharding import PartitionSpec as P
 
 inner_radix = 128
@@ -94,6 +99,11 @@
     )
 
 
+def exclusive_sum(counts):
+    places = jnp.arange(counts.shape[0], dtype=jnp.int32)
+    return jnp.sum(jnp.where(places[None, :] < places[:, None], counts[None, :], 0), axis=1)
+
+
 def imag_channels(chan_place, chan_width):
     channel_ids = chan_place * chan_width + jnp.arange(chan_width, dtype=jnp.int32)
     return ((channel_ids == 2) | (channel_ids == 4))[:, None, None]
@@ -117,7 +127,7 @@
     return jnp.stack(outputs)
 
 
-def local(misfit, kernel_spec, model_vec, weight_vec, active_list, send_counts):
+def local_general(misfit, kernel_spec, model_vec, weight_vec, active_list, send_counts):
     pen_count = lax.axis_size("pen")
     dep_count = lax.axis_size("dep")
     chan_count = lax.axis_size("chan")
@@ -158,7 +168,7 @@
     owner_length = model_vec.shape[2]
     slot_cap = owner_length // pen_count
     counts = send_counts.reshape(pen_count)
-    starts = jnp.cumsum(counts) - counts
+    starts = exclusive_sum(counts)
     slot_index = jnp.arange(slot_cap, dtype=jnp.int32)
     slot_valid = slot_index[None, :] < counts[:, None]
     in_list = jnp.minimum(starts[:, None] + slot_index[None, :], block_count - 1)
@@ -170,7 +180,7 @@
         lax.all_to_all(counts.astype(jnp.float32), "pen", split_axis=0, concat_axis=0, tiled=True),
     )
     source_counts = arrived_counts.astype(jnp.int32)
-    begins = jnp.cumsum(source_counts) - source_counts
+    begins = exclusive_sum(source_counts)
     filled = slot_index[None, :] < source_counts[:, None]
     places = begins[:, None] + slot_index[None, :]
     safe_places = jnp.minimum(places, owner_length - 1)
@@ -219,6 +229,866 @@
     )
     predicted = jnp.swapaxes(transform(rows_back, 1, 1.0, True)[0], 1, 2)
     return (gradient, model_new, predicted)
+
+
+RADIX = 16
+LANES = 128
+f32 = jnp.float32
+bf16 = jnp.bfloat16
+
+
+def two_terms(table):
+    high = table.astype(ml_dtypes.bfloat16)
+    low = (table - high.astype(np.float64)).astype(ml_dtypes.bfloat16)
+    return (high, low)
+
+
+def row_frequencies(n, devices, width):
+    device = np.arange(devices)[:, None]
+    column = np.arange(width // 2)[None, :]
+    return width * device + 2 * column + (device >= devices // 2)
+
+
+@functools.cache
+def row_tables(n, devices):
+    width = n // devices
+    freq = row_frequencies(n, devices, width).reshape(devices // 4, 1, LANES)
+    y = np.arange(n // 2)[None, :, None]
+    angle = 2.0 * math.pi / n * (freq * y % n)
+    real, imag = np.cos(angle), -np.sin(angle)
+    imag[0, :, 0] = 1.0 - 2.0 * (np.arange(n // 2) % 2)
+    forward = np.concatenate([real, imag], axis=2)
+    inverse = 2.0 * forward
+    inverse[0, :, 0] *= 0.5
+    inverse[0, :, LANES] *= 0.5
+    inverse = inverse.swapaxes(1, 2) / float(n) ** 2
+    return (two_terms(forward), two_terms(inverse))
+
+
+@functools.cache
+def column_tables():
+    k = np.arange(RADIX)[:, None, None]
+    m = np.arange(LANES)[None, :, None]
+    b = np.arange(LANES)[None, None, :]
+    n = RADIX * LANES
+    angle = 2.0 * math.pi / n * ((16 * b * m + b * k) % n)
+    real, sine = np.cos(angle), np.sin(angle)
+    forward = np.concatenate(
+        [np.concatenate([real, sine], axis=2), np.concatenate([-sine, real], axis=2)], axis=1
+    )
+    return (two_terms(forward), two_terms(forward.swapaxes(1, 2)))
+
+
+def split(value):
+    high = value.astype(bf16)
+    return high, (value - high.astype(f32)).astype(bf16)
+
+
+def dot(a, b):
+    return jnp.dot(a, b, preferred_element_type=f32)
+
+
+def dot3(left, right):
+    return dot(left[0], right[0]) + (dot(left[0], right[1]) + dot(left[1], right[0]))
+
+
+def turn(value, shift):
+    shift %= LANES
+    return value if shift == 0 else pltpu.roll(value, shift, value.ndim - 1)
+
+
+def lane_of(shape):
+    return lax.broadcasted_iota(jnp.int32, shape, len(shape) - 1)
+
+
+def quad_transpose(parts):
+    lane = lane_of(parts[0].shape)
+    low, even = lane < 64, lane % 64 < 32
+    a, b, c, d = parts
+    a, c = jnp.where(low, a, turn(c, 64)), jnp.where(low, turn(a, 64), c)
+    b, d = jnp.where(low, b, turn(d, 64)), jnp.where(low, turn(b, 64), d)
+    a, b = jnp.where(even, a, turn(b, 32)), jnp.where(even, turn(a, 96), b)
+    c, d = jnp.where(even, c, turn(d, 32)), jnp.where(even, turn(c, 96), d)
+    return [a, b, c, d]
+
+
+def radix4(x, sign):
+    (r0, i0), (r1, i1), (r2, i2), (r3, i3) = x
+    ar, ai, br, bi = r0 + r2, i0 + i2, r0 - r2, i0 - i2
+    cr, ci, dr, di = r1 + r3, i1 + i3, r1 - r3, i1 - i3
+    if sign < 0:
+        turned = (di, -dr)
+    else:
+        turned = (-di, dr)
+    return [
+        (ar + cr, ai + ci),
+        (br + turned[0], bi + turned[1]),
+        (ar - cr, ai - ci),
+        (br - turned[0], bi - turned[1]),
+    ]
+
+
+def radix16(x, sign):
+    inner = [radix4([x[4 * a1 + a0] for a1 in range(4)], sign) for a0 in range(4)]
+    outputs = [None] * RADIX
+    for k0 in range(4):
+        column = []
+        for a0 in range(4):
+            re, im = inner[a0][k0]
+            power = a0 * k0 % RADIX
+            if power == 4:
+                re, im = (im, -re) if sign < 0 else (-im, re)
+            elif power == 2 or power == 6:
+                scale = math.sqrt(0.5)
+                c = scale if power == 2 else -scale
+                if sign < 0:
+                    re, im = re * c + im * scale, im * c - re * scale
+                else:
+                    re, im = re * c - im * scale, im * c + re * scale
+            elif power != 0:
+                c = math.cos(2.0 * math.pi * power / RADIX)
+                s = sign * math.sin(2.0 * math.pi * power / RADIX)
+                re, im = re * c - im * s, re * s + im * c
+            column.append((re, im))
+        for k1, value in enumerate(radix4(column, sign)):
+            outputs[4 * k1 + k0] = value
+    return outputs
+
+
+def forward_blocks(load, work):
+    @pl.loop(0, LANES // 8)
+    def _(step):
+        first = pl.multiple_of(step * 8, 8)
+        outputs = radix16([load(a, first) for a in range(RADIX)], -1)
+        for k, (re, im) in enumerate(outputs):
+            work[k, pl.ds(first, 8), :] = re
+            work[k, pl.ds(first + LANES, 8), :] = im
+
+
+def inverse_blocks(work, store):
+    @pl.loop(0, LANES // 8)
+    def _(step):
+        first = pl.multiple_of(step * 8, 8)
+        inputs = [
+            (work[k, pl.ds(first, 8), :], work[k, pl.ds(first + LANES, 8), :]) for k in range(RADIX)
+        ]
+        for a, (re, im) in enumerate(radix16(inputs, 1)):
+            store(a, first, re, im)
+
+
+def column_product(tables, k, value):
+    return dot3((tables[0][k], tables[1][k]), split(value))
+
+
+def part_kernel(flags, spec, sent, kept, wide):
+    wide[...] = spec[0].astype(f32)
+    upper = flags[0]
+    half = kept.shape[1]
+    for i in range(half):
+        sent[0, half - 1 - i : half - i, :] = wide[pl.ds(2 * i + 1 - upper, 1), :]
+        kept[0, i : i + 1, :] = wide[pl.ds(2 * i + upper, 1), :]
+
+
+def part_spec(flags, spec):
+    count, width, n = spec.shape
+    half = width // 2
+    block = pl.BlockSpec((1, half, n), lambda s: (s, 0, 0))
+    return pl.pallas_call(
+        part_kernel,
+        grid=(count,),
+        out_shape=[jax.ShapeDtypeStruct((count, half, n), f32)] * 2,
+        in_specs=[
+            pl.BlockSpec(memory_space=pltpu.SMEM),
+            pl.BlockSpec((1, width, n), lambda s: (s, 0, 0)),
+        ],
+        out_specs=[block, block],
+        scratch_shapes=[pltpu.VMEM((width, n), f32)],
+        name="part_spec",
+    )(flags, spec)
+
+
+TILE_ROWS = {0: (0, 0), 1: (0, 32), 2: (0, 64), 3: (0, 96), 4: (1, 0), 5: (1, 32)}
+EDGE_LANES = {4: 64, 0: 65, 2: 66, 5: 96, 1: 97, 3: 98}
+
+
+def pair_kernel(flags, kept, got, edge, pairs_a, pairs_b, own, mirror, room, rows):
+    k = pl.program_id(0)
+    n = own.shape[1]
+
+    @pl.when(k == 0)
+    def _():
+        first, upper = flags[1], flags[0]
+        for layer in range(2):
+            for channel in range(6):
+                line = 2 * channel + layer
+                weight = -0.5 if channel in (2, 4) else 0.5
+                tile, place = TILE_ROWS[channel]
+                base = (2 * layer + tile) * LANES + place
+                own[base : base + 32, :] = (kept[line] * 0.5).astype(bf16)
+                room[0:1, :] = jnp.where(first == 1, kept[line, 0:1, :], edge[line])
+                room[1:33, :] = got[line]
+                mirror[base : base + 32, :] = (
+                    jnp.where(upper == 1, room[1:33, :], room[0:32, :]) * weight
+                ).astype(bf16)
+            base = (2 * layer + 1) * LANES + 64
+            for target, weights in ((own, (0.5, 0.5)), (mirror, (0.5, -0.5))):
+                rows[...] = jnp.zeros_like(rows)
+                for channel, lane in EDGE_LANES.items():
+                    weight = weights[1] if channel in (2, 4) else weights[0]
+                    rows[lane - 64 : lane - 63, :] = edge[2 * channel + layer] * weight
+                target[base : base + 64, :] = rows[...].astype(bf16)
+
+    lane = lax.broadcasted_iota(jnp.int32, (LANES, n), 1)
+    wanted = RADIX * lax.broadcasted_iota(jnp.int32, (LANES, n), 0) + k
+    contract_last = (((1,), (1,)), ((), ()))
+    total = lax.dot_general(
+        (lane == wanted).astype(f32).astype(bf16), own[...], contract_last, preferred_element_type=f32
+    ) + lax.dot_general(
+        (lane == lax.rem(n - wanted, n)).astype(f32).astype(bf16),
+        mirror[...],
+        contract_last,
+        preferred_element_type=f32,
+    )
+    for layer in range(2):
+        pairs_a[layer] = total[:, 2 * layer * LANES : (2 * layer + 1) * LANES]
+        pairs_b[layer] = total[:, (2 * layer + 1) * LANES : (2 * layer + 2) * LANES]
+
+
+def pair_spec(flags, kept, got, edge):
+    count, half, n = kept.shape
+    whole = pl.BlockSpec((count, half, n), lambda k: (0, 0, 0))
+    out = pl.BlockSpec((2, LANES, LANES), lambda k: (0, k, 0))
+    return pl.pallas_call(
+        pair_kernel,
+        grid=(RADIX,),
+        out_shape=[jax.ShapeDtypeStruct((2, n, LANES), f32)] * 2,
+        in_specs=[
+            pl.BlockSpec(memory_space=pltpu.SMEM),
+            whole,
+            whole,
+            pl.BlockSpec((count, 1, n), lambda k: (0, 0, 0)),
+        ],
+        out_specs=[out, out],
+        scratch_shapes=[
+            pltpu.VMEM((4 * LANES, n), bf16),
+            pltpu.VMEM((4 * LANES, n), bf16),
+            pltpu.VMEM((40, n), f32),
+            pltpu.VMEM((64, n), f32),
+        ],
+        compiler_params=pltpu.CompilerParams(vmem_limit_bytes=44 << 20),
+        name="pair_spec",
+    )(flags, kept, got, edge)
+
+
+def misfit_rows_kernel(misfit, high, low, out_a, out_b, halves_high, halves_low):
+    s = pl.program_id(0)
+    channels, rows, n = misfit.shape
+
+    @pl.when(s == 0)
+    def _():
+        value = misfit[...].reshape(channels * rows, n)
+        first, second = value[:, : n // 2], value[:, n // 2 :]
+        for index, combined in enumerate((first + second, first - second)):
+            halves_high[index], halves_low[index] = split(combined)
+
+    side = s // (pl.num_programs(0) // 2)
+    result = dot3((halves_high[side], halves_low[side]), (high[0], low[0]))
+    real = [result[rows * c : rows * (c + 1), :LANES] for c in range(channels)]
+    imag = [result[rows * c : rows * (c + 1), LANES:] for c in range(channels)]
+    parts = (quad_transpose(real[:4]), quad_transpose(imag[:4]))
+    for index in range(4):
+        out_a[index, :, :LANES] = parts[0][index]
+        out_a[index, :, LANES:] = parts[1][index]
+    for index, value in enumerate(quad_transpose([real[4], real[5], imag[4], imag[5]])):
+        out_b[index] = value
+
+
+def misfit_rows(misfit, tables, devices):
+    channels, rows, n = misfit.shape
+    table = pl.BlockSpec((1, n // 2, 2 * LANES), lambda s: (s, 0, 0))
+    return pl.pallas_call(
+        misfit_rows_kernel,
+        grid=(devices // 4,),
+        out_shape=[
+            jax.ShapeDtypeStruct((devices, rows, 2 * LANES), f32),
+            jax.ShapeDtypeStruct((devices, rows, LANES), f32),
+        ],
+        in_specs=[pl.BlockSpec((channels, rows, n), lambda s: (0, 0, 0)), table, table],
+        out_specs=[
+            pl.BlockSpec((4, rows, 2 * LANES), lambda s: (s, 0, 0)),
+            pl.BlockSpec((4, rows, LANES), lambda s: (s, 0, 0)),
+        ],
+        scratch_shapes=[pltpu.VMEM((2, channels * rows, n // 2), bf16)] * 2,
+        compiler_params=pltpu.CompilerParams(vmem_limit_bytes=40 << 20),
+        name="misfit_rows",
+    )(misfit, *tables)
+
+
+def inverse_step(lhs, high, low, sums):
+    s = pl.program_id(0)
+    steps = pl.num_programs(0)
+    product = dot3(split(lhs), (high[0], low[0]))
+    side = s // (steps // 2)
+    fresh = s % (steps // 2) == 0
+
+    @pl.when(fresh)
+    def _():
+        sums[side] = product
+
+    @pl.when(jnp.logical_not(fresh))
+    def _():
+        sums[side] += product
+
+
+def predicted_kernel_b(spectra, high, low, out, sums):
+    rows, n = out.shape[1:]
+    c4r, c5r, c4i, c5i = quad_transpose([spectra[index] for index in range(4)])
+    lhs = jnp.concatenate(
+        [jnp.concatenate([c4r, c4i], axis=1), jnp.concatenate([c5r, c5i], axis=1)], axis=0
+    )
+    inverse_step(lhs, high, low, sums)
+
+    @pl.when(pl.program_id(0) == pl.num_programs(0) - 1)
+    def _():
+        for channel in range(2):
+            even, odd = sums[0, channel * rows : (channel + 1) * rows], sums[1, channel * rows : (channel + 1) * rows]
+            out[channel, :, : n // 2] = even + odd
+            out[channel, :, n // 2 :] = even - odd
+
+
+def predicted_kernel_a(spectra, high, low, before, out, sums):
+    rows, n = out.shape[1:]
+    real = quad_transpose([spectra[index, :, :LANES] for index in range(4)])
+    imag = quad_transpose([spectra[index, :, LANES:] for index in range(4)])
+    lhs = jnp.concatenate(
+        [jnp.concatenate(pair, axis=1) for pair in zip(real, imag)], axis=0
+    )
+    inverse_step(lhs, high, low, sums)
+
+    @pl.when(pl.program_id(0) == pl.num_programs(0) - 1)
+    def _():
+        for channel in range(4):
+            even, odd = sums[0, channel * rows : (channel + 1) * rows], sums[1, channel * rows : (channel + 1) * rows]
+            out[channel, :, : n // 2] = even + odd
+            out[channel, :, n // 2 :] = even - odd
+
+
+def predicted_rows(spectra, tables, before, n):
+    devices, rows, lanes = spectra.shape
+    table = pl.BlockSpec((1, 2 * LANES, n // 2), lambda s: (s, 0, 0))
+    chunk = pl.BlockSpec((4, rows, lanes), lambda s: (s, 0, 0))
+    channels = 2 if before is None else 4
+    return pl.pallas_call(
+        predicted_kernel_b if before is None else predicted_kernel_a,
+        grid=(devices // 4,),
+        out_shape=jax.ShapeDtypeStruct((6, rows, n), f32),
+        in_specs=[chunk, table, table] + ([] if before is None else [pl.BlockSpec(memory_space=pl.ANY)]),
+        out_specs=pl.BlockSpec((channels, rows, n), lambda s: (2 if before is None else 0, 0, 0)),
+        scratch_shapes=[pltpu.VMEM((2, channels * rows, n // 2), f32)],
+        input_output_aliases={} if before is None else {3: 0},
+        compiler_params=pltpu.CompilerParams(vmem_limit_bytes=32 << 20),
+        name="predicted_rows_b" if before is None else "predicted_rows_a",
+    )(spectra, *tables, *([] if before is None else [before]))
+
+
+def write_sum(total, layer0, layer1):
+    return jnp.where(lane_of(total.shape) < 64, layer0, layer1)
+
+
+def adjoint_kernel_a(flags, spectra, pairs, high, low, sums, edges, work):
+    first = flags[1] == 1
+    lane8 = lane_of((8, LANES))
+    packed = jnp.logical_and(lane8 % 32 == 0, first)
+
+    def load(a, row):
+        real = spectra[pl.ds(a * LANES + row, 8), :LANES]
+        imag = spectra[pl.ds(a * LANES + row, 8), LANES:]
+        edges[pl.ds(a * LANES + row, 8), :] = jnp.where(
+            (lane8 == 65) | (lane8 == 97), turn(imag, 65), turn(imag, 2)
+        )
+        return (real, jnp.where(packed, 0.0, imag))
+
+    forward_blocks(load, work)
+    lane = lane_of((LANES, LANES))
+    turned = lane // 32 == 2
+
+    @pl.loop(0, RADIX)
+    def _(k):
+        spectrum = column_product((high, low), k, work[k])
+        real, imag = spectrum[:LANES], spectrum[LANES:]
+        real, imag = jnp.where(turned, imag, real), jnp.where(turned, -real, imag)
+        row = pl.multiple_of(k * LANES, LANES)
+        for index, value in enumerate((real, imag)):
+            v0, v1 = value * pairs[0, pl.ds(row, LANES), :], value * pairs[1, pl.ds(row, LANES), :]
+            both = jnp.where(lane < 64, v0 + turn(v0, 64), v1 + turn(v1, 64))
+            sums[index, pl.ds(row, LANES), :] = both + turn(both, 96)
+
+
+def adjoint_columns_a(flags, spectra, pairs, tables):
+    n = spectra.shape[0]
+    return pl.pallas_call(
+        adjoint_kernel_a,
+        out_shape=[
+            jax.ShapeDtypeStruct((2, n, LANES), f32),
+            jax.ShapeDtypeStruct((n, LANES), f32),
+        ],
+        in_specs=[pl.BlockSpec(memory_space=pltpu.SMEM)] + [pl.BlockSpec(memory_space=pltpu.VMEM)] * 4,
+        scratch_shapes=[pltpu.VMEM((RADIX, 2 * LANES, LANES), f32)],
+        compiler_params=pltpu.CompilerParams(vmem_limit_bytes=32 << 20),
+        name="adjoint_columns_a",
+    )(flags, spectra, pairs, *tables)
+
+
+def adjoint_kernel_b(flags, spectra, edges, sums, pairs, high, low, high_i, low_i, out, work, fields):
+    first = flags[1] == 1
+    lane8 = lane_of((8, LANES))
+    packed = jnp.logical_and(lane8 % 32 == 0, first)
+    main = lane8 < 64
+    here = (lane8 == 64) | (lane8 == 96)
+    moved = (lane8 == 65) | (lane8 == 66) | (lane8 == 97) | (lane8 == 98)
+
+    def load(a, row):
+        value = spectra[pl.ds(a * LANES + row, 8), :]
+        edge = edges[pl.ds(a * LANES + row, 8), :]
+        real = jnp.where(main | here, value, jnp.where(moved, edge, 0.0))
+        imag = jnp.where(main, jnp.where(packed, 0.0, turn(value, 64)), 0.0)
+        return (real, imag)
+
+    forward_blocks(load, work)
+    lane = lane_of((LANES, LANES))
+    turned = (lane < 32) | (lane == 64) | (lane == 66)
+    low_main = lane < 32
+    high_main = (lane >= 64) & (lane < 96)
+
+    @pl.loop(0, RADIX)
+    def _(k):
+        spectrum = column_product((high, low), k, work[k])
+        real, imag = spectrum[:LANES], spectrum[LANES:]
+        real, imag = jnp.where(turned, imag, real), jnp.where(turned, -real, imag)
+        row = pl.multiple_of(k * LANES, LANES)
+        parts = []
+        for index, value in enumerate((real, imag)):
+            t0, t1 = (value * pairs[layer, pl.ds(row, LANES), :] for layer in range(2))
+            t0, t1 = t0 + turn(t0, 96), t1 + turn(t1, 96)
+            e0, e1 = (t + turn(t, 127) + turn(t, 126) for t in (t0, t1))
+            total = sums[index, pl.ds(row, LANES), :]
+            parts.append(
+                jnp.where(
+                    low_main,
+                    total + t0,
+                    jnp.where(
+                        high_main,
+                        total + turn(t1, 64),
+                        jnp.where(
+                            lane == 32, turn(e0, 96), jnp.where(lane == 96, turn(e1, 32), 0.0)
+                        ),
+                    ),
+                )
+            )
+        work[k] = column_product((high_i, low_i), k, jnp.concatenate(parts, axis=0))
+
+    def store(a, row, real, imag):
+        edge = turn(real, 96)
+        fields[0, pl.ds(a * LANES + row, 8), :] = real
+        fields[1, pl.ds(a * LANES + row, 8), :] = jnp.where(
+            jnp.logical_and(lane8 % 64 == 0, first), edge, imag
+        )
+
+    inverse_blocks(work, store)
+    lane64 = lane_of((64, LANES))
+    for band in range(RADIX):
+        pieces = [
+            fields[part, band * LANES + 64 * side : band * LANES + 64 * side + 64, :]
+            for part in range(2)
+            for side in range(2)
+        ]
+        for layer in range(2):
+            shifted = [turn(piece, 32 * q - 64 * layer) for q, piece in enumerate(pieces)]
+            out[2 * band + layer] = jnp.where(
+                lane64 < 32,
+                shifted[0],
+                jnp.where(lane64 < 64, shifted[1], jnp.where(lane64 < 96, shifted[2], shifted[3])),
+            )
+
+
+def adjoint_columns_b(flags, spectra, edges, sums, pairs, tables, inverse_tables):
+    n = spectra.shape[0]
+    return pl.pallas_call(
+        adjoint_kernel_b,
+        out_shape=jax.ShapeDtypeStruct((2 * RADIX, 64, LANES), f32),
+        in_specs=[pl.BlockSpec(memory_space=pltpu.SMEM)] + [pl.BlockSpec(memory_space=pltpu.VMEM)] * 8,
+        scratch_shapes=[
+            pltpu.VMEM((RADIX, 2 * LANES, LANES), f32),
+            pltpu.VMEM((2, n, LANES), f32),
+        ],
+        compiler_params=pltpu.CompilerParams(vmem_limit_bytes=40 << 20),
+        name="adjoint_columns_b",
+    )(flags, spectra, edges, sums, pairs, *tables, *inverse_tables)
+
+
+def forward_kernel_b(flags, moved, pairs, high, low, high_i, low_i, out, edges, model, work, fields):
+    first = flags[1] == 1
+    lane64 = lane_of((64, LANES))
+    low_main = lane64 < 32
+    high_main = (lane64 >= 64) & (lane64 < 96)
+    edge_lane = (lane64 == 32) | (lane64 == 96)
+    for band in range(RADIX):
+        value0, value1 = moved[2 * band], moved[2 * band + 1]
+
+        def pick(q):
+            return jnp.where(
+                low_main,
+                turn(value0, -32 * q),
+                jnp.where(high_main, turn(value1, 64 - 32 * q), 0.0),
+            )
+
+        for side in range(2):
+            real, imag = pick(side), pick(2 + side)
+            row = band * LANES + 64 * side
+            fields[0, row : row + 64, :] = jnp.where(edge_lane, turn(imag, 32), real)
+            fields[1, row : row + 64, :] = jnp.where(
+                jnp.logical_and(lane64 % 64 == 0, first), 0.0, imag
+            )
+
+    def load(a, row):
+        return tuple(fields[part, pl.ds(a * LANES + row, 8), :] for part in range(2))
+
+    forward_blocks(load, work)
+    lane = lane_of((LANES, LANES))
+    turned = (lane < 32) | (lane == 64) | (lane == 66)
+
+    @pl.loop(0, RADIX)
+    def _(k):
+        spectrum = column_product((high, low), k, work[k])
+        row = pl.multiple_of(k * LANES, LANES)
+        totals = []
+        for part in range(2):
+            value = spectrum[part * LANES : (part + 1) * LANES]
+            spread = []
+            for layer in range(2):
+                main = jnp.where(lane < 32, turn(value, -64 * layer), 0.0)
+                main = main + turn(main, 32)
+                main = main + turn(main, 64)
+                model[layer, part, pl.ds(row, LANES), :] = main
+                at = 32 + 64 * layer
+                edge = jnp.broadcast_to(value[:, at : at + 1], value.shape)
+                spread.append(jnp.where(lane < 64, main, edge))
+            totals.append(
+                spread[0] * pairs[0, pl.ds(row, LANES), :] + spread[1] * pairs[1, pl.ds(row, LANES), :]
+            )
+        real, imag = totals
+        real, imag = jnp.where(turned, -imag, real), jnp.where(turned, real, imag)
+        work[k] = column_product((high_i, low_i), k, jnp.concatenate([real, imag], axis=0))
+
+    lane8 = lane_of((8, LANES))
+
+    def store(a, row, real, imag):
+        imag = jnp.where(jnp.logical_and(lane8 % 32 == 0, first), turn(real, 64), imag)
+        out[pl.ds(a * LANES + row, 8), :] = jnp.where(lane8 < 64, real, turn(imag, 64))
+        edges[pl.ds(a * LANES + row, 8), :] = real
+
+    inverse_blocks(work, store)
+
+
+def forward_columns_b(flags, moved, pairs, tables, inverse_tables, n):
+    return pl.pallas_call(
+        forward_kernel_b,
+        out_shape=[
+            jax.ShapeDtypeStruct((n, LANES), f32),
+            jax.ShapeDtypeStruct((n, LANES), f32),
+            jax.ShapeDtypeStruct((2, 2, n, LANES), f32),
+        ],
+        in_specs=[pl.BlockSpec(memory_space=pltpu.SMEM)] + [pl.BlockSpec(memory_space=pltpu.VMEM)] * 6,
+        scratch_shapes=[
+            pltpu.VMEM((RADIX, 2 * LANES, LANES), f32),
+            pltpu.VMEM((2, n, LANES), f32),
+        ],
+        compiler_params=pltpu.CompilerParams(vmem_limit_bytes=40 << 20),
+        name="forward_columns_b",
+    )(flags, moved, pairs, *tables, *inverse_tables)
+
+
+def forward_kernel_a(flags, model, edges, pairs, high_i, low_i, out, work):
+    first = flags[1] == 1
+    lane = lane_of((LANES, LANES))
+    turned = lane // 32 == 2
+
+    @pl.loop(0, RADIX)
+    def _(k):
+        row = pl.multiple_of(k * LANES, LANES)
+        real, imag = (
+            model[0, part, pl.ds(row, LANES), :] * pairs[0, pl.ds(row, LANES), :]
+            + model[1, part, pl.ds(row, LANES), :] * pairs[1, pl.ds(row, LANES), :]
+            for part in range(2)
+        )
+        real, imag = jnp.where(turned, -imag, real), jnp.where(turned, real, imag)
+        work[k] = column_product((high_i, low_i), k, jnp.concatenate([real, imag], axis=0))
+
+    lane8 = lane_of((8, LANES))
+    packed = jnp.logical_and(lane8 % 32 == 0, first)
+
+    def store(a, row, real, imag):
+        edge = edges[pl.ds(a * LANES + row, 8), :]
+        edge = jnp.where(lane8 < 64, turn(edge, 63), turn(edge, 126))
+        out[pl.ds(a * LANES + row, 8), :LANES] = real
+        out[pl.ds(a * LANES + row, 8), LANES:] = jnp.where(packed, edge, imag)
+
+    inverse_blocks(work, store)
+
+
+def forward_columns_a(flags, model, edges, pairs, inverse_tables):
+    n = edges.shape[0]
+    return pl.pallas_call(
+        forward_kernel_a,
+        out_shape=jax.ShapeDtypeStruct((n, 2 * LANES), f32),
+        in_specs=[pl.BlockSpec(memory_space=pltpu.SMEM)] + [pl.BlockSpec(memory_space=pltpu.VMEM)] * 5,
+        scratch_shapes=[pltpu.VMEM((RADIX, 2 * LANES, LANES), f32)],
+        compiler_params=pltpu.CompilerParams(vmem_limit_bytes=32 << 20),
+        name="forward_columns_a",
+    )(flags, model, edges, pairs, *inverse_tables)
+
+
+def block_row(block, rows):
+    return (block % RADIX) * rows + block // RADIX
+
+
+def gradient_kernel(counts, listing, spectra, high, low, gradient, outgoing, sums, blocks, compact):
+    rows, n = gradient.shape
+    parts = quad_transpose([spectra[index] for index in range(4)])
+    lhs = jnp.concatenate(
+        [jnp.concatenate([parts[0], parts[1]], axis=0), jnp.concatenate([parts[2], parts[3]], axis=0)],
+        axis=1,
+    )
+    inverse_step(lhs, high, low, sums)
+
+    @pl.when(pl.program_id(0) == pl.num_programs(0) - 1)
+    def _():
+        gradient[:, : n // 2] = sums[0] + sums[1]
+        gradient[:, n // 2 :] = sums[0] - sums[1]
+        for q in range(RADIX):
+            blocks[q * rows : (q + 1) * rows, :] = gradient[:, q * LANES : (q + 1) * LANES]
+        owners = outgoing.shape[0]
+        cap = outgoing.shape[1]
+        total = lax.fori_loop(0, owners, lambda o, t: t + counts[o], jnp.int32(0))
+
+        @pl.loop(0, lax.div(total + 7, 8))
+        def _(step):
+            for index in range(8):
+                at = step * 8 + index
+                compact[pl.ds(at, 1), :] = blocks[pl.ds(block_row(listing[at], rows), 1), :]
+
+        offset = 0
+        for o in range(owners):
+            outgoing[o] = compact[pl.ds(offset, cap), :]
+            offset = offset + counts[o]
+
+
+def gradient_rows(counts, listing, spectra, tables, rows, n, cap):
+    devices = spectra.shape[0]
+    owners = counts.shape[0]
+    smem = pl.BlockSpec(memory_space=pltpu.SMEM)
+    table = pl.BlockSpec((1, 2 * LANES, n // 2), lambda s: (s, 0, 0))
+    block_count = listing.shape[0]
+    return pl.pallas_call(
+        gradient_kernel,
+        grid=(devices // 4,),
+        out_shape=[
+            jax.ShapeDtypeStruct((rows, n), f32),
+            jax.ShapeDtypeStruct((owners, cap, LANES), f32),
+        ],
+        in_specs=[
+            smem,
+            smem,
+            pl.BlockSpec((4, rows // 2, LANES), lambda s: (s, 0, 0)),
+            table,
+            table,
+        ],
+        out_specs=[
+            pl.BlockSpec((rows, n), lambda s: (0, 0)),
+            pl.BlockSpec((owners, cap, LANES), lambda s: (0, 0, 0)),
+        ],
+        scratch_shapes=[
+            pltpu.VMEM((2, rows, n // 2), f32),
+            pltpu.VMEM((block_count, LANES), f32),
+            pltpu.VMEM((block_count + cap, LANES), f32),
+        ],
+        compiler_params=pltpu.CompilerParams(vmem_limit_bytes=32 << 20),
+        name="gradient_rows",
+    )(counts, listing, spectra, *tables)
+
+
+def owner_kernel(counts, incoming, current, weights, model_new, updated, room, scales):
+    sources, cap, _ = incoming.shape
+    length = current.shape[0]
+    room[:length, :] = current[...]
+    room[length:, :] = jnp.zeros_like(room[length:, :])
+    scales[:length, :] = weights[...].astype(f32) * step_size
+    scales[length:, :] = jnp.zeros_like(scales[length:, :])
+    row = lax.broadcasted_iota(jnp.int32, (cap, LANES), 0)
+    begin = 0
+    for p in range(sources):
+        count = counts[p]
+        before = room[pl.ds(begin, cap), :]
+        after = jnp.clip(before - scales[pl.ds(begin, cap), :] * incoming[p], -1.0, 1.0)
+        updated[p] = after
+        room[pl.ds(begin, cap), :] = jnp.where(row < count, after, before)
+        begin = begin + count
+    model_new[...] = room[:length, :]
+
+
+def owner_update(counts, incoming, current, weights):
+    sources, cap, _ = incoming.shape
+    length = current.shape[0]
+    return pl.pallas_call(
+        owner_kernel,
+        out_shape=[
+            jax.ShapeDtypeStruct((length, LANES), f32),
+            jax.ShapeDtypeStruct((sources, cap, LANES), f32),
+        ],
+        in_specs=[pl.BlockSpec(memory_space=pltpu.SMEM)] + [pl.BlockSpec(memory_space=pltpu.VMEM)] * 3,
+        scratch_shapes=[pltpu.VMEM((length + cap, LANES), f32)] * 2,
+        compiler_params=pltpu.CompilerParams(vmem_limit_bytes=24 << 20),
+        name="owner_update",
+    )(counts, incoming, current, weights)
+
+
+def model_rows_kernel(counts, listing, returned, high, low, out, compact, grid, halves_high, halves_low):
+    s = pl.program_id(0)
+    owners, cap, _ = returned.shape
+    rows = halves_high.shape[1]
+
+    @pl.when(s == 0)
+    def _():
+        grid[...] = jnp.zeros_like(grid)
+        offset = 0
+        for o in range(owners):
+            compact[pl.ds(offset, cap), :] = returned[o]
+            offset = offset + counts[o]
+        total = offset
+
+        @pl.loop(0, lax.div(total, 8))
+        def _(step):
+            for index in range(8):
+                at = step * 8 + index
+                grid[pl.ds(block_row(listing[at], rows), 1), :] = compact[pl.ds(at, 1), :]
+
+        @pl.loop(lax.div(total, 8) * 8, total)
+        def _(at):
+            grid[pl.ds(block_row(listing[at], rows), 1), :] = compact[pl.ds(at, 1), :]
+
+        half = RADIX // 2
+        for q in range(half):
+            first = grid[q * rows : (q + 1) * rows, :]
+            second = grid[(q + half) * rows : (q + half + 1) * rows, :]
+            for index, combined in enumerate((first + second, first - second)):
+                top, rest = split(combined)
+                halves_high[index, :, q * LANES : (q + 1) * LANES] = top
+                halves_low[index, :, q * LANES : (q + 1) * LANES] = rest
+
+    side = s // (pl.num_programs(0) // 2)
+    result = dot3((halves_high[side], halves_low[side]), (high[0], low[0]))
+    half = rows // 2
+    parts = quad_transpose(
+        [result[:half, :LANES], result[half:, :LANES], result[:half, LANES:], result[half:, LANES:]]
+    )
+    for index in range(4):
+        out[index] = parts[index]
+
+
+def model_rows(counts, listing, returned, tables, rows, n, devices):
+    owners, cap, _ = returned.shape
+    block_count = listing.shape[0]
+    smem = pl.BlockSpec(memory_space=pltpu.SMEM)
+    table = pl.BlockSpec((1, n // 2, 2 * LANES), lambda s: (s, 0, 0))
+    return pl.pallas_call(
+        model_rows_kernel,
+        grid=(devices // 4,),
+        out_shape=jax.ShapeDtypeStruct((devices, rows // 2, LANES), f32),
+        in_specs=[
+            smem,
+            smem,
+            pl.BlockSpec((owners, cap, LANES), lambda s: (0, 0, 0)),
+            table,
+            table,
+        ],
+        out_specs=pl.BlockSpec((4, rows // 2, LANES), lambda s: (s, 0, 0)),
+        scratch_shapes=[
+            pltpu.VMEM((block_count + cap, LANES), f32),
+            pltpu.VMEM((block_count, LANES), f32),
+            pltpu.VMEM((2, rows, n // 2), bf16),
+            pltpu.VMEM((2, rows, n // 2), bf16),
+        ],
+        compiler_params=pltpu.CompilerParams(vmem_limit_bytes=32 << 20),
+        name="model_rows",
+    )(counts, listing, returned, *tables)
+
+
+def swap_all(value, axes):
+    return lax.all_to_all(value, axes, split_axis=0, concat_axis=0, tiled=True)
+
+
+def local_paired(misfit, kernel_spec, model_vec, weight_vec, active_list, send_counts):
+    both = ("pen", "dep")
+    pen_count = lax.axis_size("pen")
+    devices = pen_count * lax.axis_size("dep")
+    channels, rows, n = misfit.shape
+    band = n // pen_count
+    forward_np, inverse_np = row_tables(n, devices)
+    row_forward, row_inverse = tuple(map(jnp.asarray, forward_np)), tuple(map(jnp.asarray, inverse_np))
+    forward_np, inverse_np = column_tables()
+    col_forward, col_inverse = tuple(map(jnp.asarray, forward_np)), tuple(map(jnp.asarray, inverse_np))
+    me = lax.axis_index(both)
+    half = devices // 2
+    flags = jnp.stack([(me >= half).astype(jnp.int32), (me == 0).astype(jnp.int32)])
+    counts = send_counts.reshape(pen_count)
+    listing = active_list.reshape(-1)
+    owner_length = model_vec.shape[2]
+    cap = owner_length // pen_count
+
+    spec = kernel_spec.reshape((-1,) + kernel_spec.shape[2:])
+    sent, kept = part_spec(flags, spec)
+    got = lax.ppermute(sent, both, [(d, devices - 1 - d) for d in range(devices)])
+    edge = lax.ppermute(
+        spec[:, 0:1, :].astype(f32), both, [(d, (devices - d) % half) for d in range(half, devices)]
+    )
+    source_counts = swap_all(counts, "pen")
+
+    chunk_a, chunk_b = misfit_rows(misfit, row_forward, devices)
+    columns_a = swap_all(chunk_a, both).reshape(n, 2 * LANES)
+    columns_b = swap_all(chunk_b, both).reshape(n, LANES)
+    pairs_a, pairs_b = pair_spec(flags, kept, got, edge)
+    sums, edges = adjoint_columns_a(flags, columns_a, pairs_a, col_forward)
+    fields = adjoint_columns_b(flags, columns_b, edges, sums, pairs_b, col_forward, col_inverse)
+    gradient, outgoing = gradient_rows(
+        counts, listing, swap_all(fields, both), row_inverse, band, n, cap
+    )
+    incoming = swap_all(outgoing, "pen")
+    model_new, updated = owner_update(
+        source_counts,
+        incoming,
+        model_vec.reshape(owner_length, LANES),
+        weight_vec.reshape(owner_length, LANES),
+    )
+    returned = swap_all(updated, "pen")
+    model_chunks = model_rows(counts, listing, returned, row_forward, band, n, devices)
+    out_b, edges, model = forward_columns_b(
+        flags, swap_all(model_chunks, both), pairs_b, col_forward, col_inverse, n
+    )
+    back_b = swap_all(out_b.reshape(devices, rows, LANES), both)
+    out_a = forward_columns_a(flags, model, edges, pairs_a, col_inverse)
+    back_a = swap_all(out_a.reshape(devices, rows, 2 * LANES), both)
+    predicted = predicted_rows(back_b, row_inverse, None, n)
+    predicted = predicted_rows(back_a, row_inverse, predicted, n)
+    return (gradient[None], model_new.reshape(model_vec.shape), predicted)
+
+
+def local(misfit, kernel_spec, model_vec, weight_vec, active_list, send_counts):
+    sizes = tuple(lax.axis_size(name) for name in ("pen", "dep", "chan"))
+    if sizes == (16, 2, 1) and misfit.shape == (6, 64, RADIX * LANES) and kernel_spec.shape[1] == 2:
+        plan = local_paired
+    else:
+        plan = local_general
+    return plan(misfit, kernel_spec, model_vec, weight_vec, active_list, send_counts)
 
 
 def solution(mesh):

time: 983 us -> 629 us (0.64); the launches traced: 970 us -> 627 us
  local copies, waits for them, and re-layouts: 442 us -> 50.5 us
  matrix products: 177 us -> 0 us
  Pallas kernels: 0 us -> 149 us
  waiting for transfers between devices: 199 us -> 297 us
  blocking collectives: 0 us -> 89.8 us
  other arithmetic: 86.5 us -> 2.08 us
  starting transfers between devices: 63.1 us -> 37.1 us
    dot_general x56 -> x0, matrix products: 177 us -> none  [the longest x16 49.6 us: contract(): product_one = jnp.einsum(formula, operand[0], tables[0], precision=highest)]
    pallas_call x0 -> x12, Pallas kernels: none -> 149 us  [the longest x1 28.3 us: pair_spec(): pl.pallas_call(pair_kernel, grid=(RADIX,), out_shape=[jax.ShapeDtypeStruc...]
    all_to_all x0 -> x2, blocking collectives: none -> 89.8 us  [swap_all(): return lax.all_to_all(value, axes, split_axis=0, concat_axis=0, tiled=True)]
    ppermute x0 -> x2, waiting for transfers between devices: none -> 88.4 us  [the longest x1 88.4 us: local_paired(): lax.ppermute(spec[:, 0:1, :].astype(f32), both, [(d, (devices - d) % half...]
    mul x20 -> x0, local copies, waits for them, and re-layouts: 73.3 us -> none  [the longest x7 39.5 us: transform(): jnp.swapaxes(member, -1, -2).reshape(full_shape) * factor]
    unnamed x138 -> x90, local copies, waits for them, and re-layouts: 105 us -> 49.8 us
    all_to_all x7 -> x1, local copies, waits for them, and re-layouts: 52.7 us -> 0.68 us  [swap_all(): return lax.all_to_all(value, axes, split_axis=0, concat_axis=0, tiled=True)]
    gather x5 -> x0, local copies, waits for them, and re-layouts: 48.5 us -> none  [the longest x2 17.5 us: local(): block_ids = listing[in_list]]
  transfers between devices with their start and end apart: 11 -> 9, of which waited for: 9 -> 6; matrix products, arithmetic and copies ran while one was open for 42% -> 0% of each run, Pallas kernels for 0% -> 12%
where the time goes in v1:
time: 629 us; the launch traced here: 627 us
  waiting for transfers between devices  297 us (47%)
  Pallas kernels  149 us (24%)
  blocking collectives  89.8 us (14%)
  local copies, waits for them, and re-layouts  50.5 us (8%)
  starting transfers between devices  37.1 us (6%)
    all_to_all x7, waiting for transfers between devices, swap_all(): return lax.all_to_all(value, axes, split_axis=0, concat_axis=0, tiled=True)  209 us
    all_to_all x2, blocking collectives, swap_all(): return lax.all_to_all(value, axes, split_axis=0, concat_axis=0, tiled=True)  89.8 us
    ppermute x1, waiting for transfers between devices, local_paired(): lax.ppermute(spec[:, 0:1, :].astype(f32), both, [(d, (devices - d) % half...  88.4 us
    unnamed x90, local copies, waits for them, and re-layouts  49.8 us
    all_to_all x7, starting transfers between devices, swap_all(): return lax.all_to_all(value, axes, split_axis=0, concat_axis=0, tiled=True)  30.6 us
    pallas_call x1, Pallas kernels, pair_spec(): pl.pallas_call(pair_kernel, grid=(RADIX,), out_shape=[jax.ShapeDtypeStruc...  28.3 us
    pallas_call x1, Pallas kernels, forward_columns_b(): pl.pallas_call(forward_kernel_b, out_shape=[jax.ShapeDtypeStruct((n, LANE...  23.2 us
    pallas_call x1, Pallas kernels, adjoint_columns_b(): pl.pallas_call(adjoint_kernel_b, out_shape=jax.ShapeDtypeStruct((2 * RADI...  20.3 us
  transfers between devices with their start and end apart: 9, of which 6 were waited for; matrix products, arithmetic and copies ran while one was open for 0% of the time, Pallas kernels for 12%

profile of v1, /device:TPU:0, one launch (start us, length us, event | category | flops | bytes accessed | tf_op | source)
XLA Modules:
  0.0 626.8 jit_solution(18412328418703231341)
XLA Ops:
  0.6 2.2 copy-done.17
  2.8 1.9 copy-done.30
  4.7 9.6 %misfit_rows.1 = (f32[32,64,256]{2,1,0:T(8,128)S(1)}, f32[32,64,128]{2,1,0:T(8,128)S(1)}) custom-call(f32[6,64,2048]{2,1,0:T(8,128)S(1)} %copy-done.30, bf16[8,1024,256]{2,1,0:T(8,128)(2,1)S(1)} %copy-done.17, bf16[8,1024,256]{2,1,0:T(8,128)(2,1)} %constant.31.clone.low), custom_call_target="tpu_custom_call" | custom-call | tf_op jit(solution)/shard_map/misfit_rows/pallas_call | solution.py:509
  14.4 1.4 copy-done.33
  16.7 7.3 %all-to-all-start.1 = ((f32[32,64,256]{2,1,0:T(8,128)}), f32[32,64,256]{2,1,0:T(8,128)S(1)}, u32[]{:S(2)}, u32[]{:S(2)}) async-start(f32[32,64,256]{2,1,0:T(8,128)} %copy-done.33), calls=%async_computation.1 | async-start | bytes 4194304 | tf_op jit(solution)/shard_map/all_to_all | solution.py:1027
  24.7 9.6 %part_spec.1 = (f32[12,32,2048]{2,1,0:T(8,128)}, f32[12,32,2048]{2,1,0:T(8,128)}) custom-call(s32[2]{0:T(128)} %add_convert_fusion.flags, bf16[12,64,2048]{2,1,0:T(8,128)(2,1)} %bitcast.25), custom_call_target="tpu_custom_call" | custom-call | tf_op jit(solution)/shard_map/part_spec/pallas_call | solution.py:396
  34.3 5.2 collective-permute-start
  39.5 101.1 %all-to-all-done.1 = f32[32,64,256]{2,1,0:T(8,128)S(1)} async-done(((f32[32,64,256]{2,1,0:T(8,128)}), f32[32,64,256]{2,1,0:T(8,128)S(1)}, u32[]{:S(2)}, u32[]{:S(2)}) %all-to-all-start.1) | async-done | bytes 2097184 | tf_op jit(solution)/shard_map/all_to_all | solution.py:1027
  140.6 3.3 all-to-all-start
  146.2 88.4 %collective-permute-done.1.edge = f32[12,1,2048]{2,1,0:T(1,128)S(1)} collective-permute-done((f32[12,1,2048]{2,1,0:T(1,128)S(1)}, f32[12,1,2048]{2,1,0:T(1,128)S(1)}, u32[]{:S(2)}, u32[]{:S(2)}) %collective-permute-start.1) | collective-permute-done | bytes 98336 | tf_op jit(solution)/shard_map/ppermute | solution.py:1051
  234.6 1.9 copy-done.29
  236.5 28.3 %pair_spec.1 = (f32[2,2048,128]{2,1,0:T(8,128)S(1)}, f32[2,2048,128]{2,1,0:T(8,128)S(1)}) custom-call(s32[2]{0:T(128)S(1)} %copy-done.43, f32[12,32,2048]{2,1,0:T(8,128)S(1)} %copy-done.29, f32[12,32,2048]{2,1,0:T(8,128)} %collective-permute-done.got, f32[12,1,2048]{2,1,0:T(1,128)S(1)} %collective-permute-done.1.edge), custom_call_target="tpu_custom_call" | custom-call | tf_op jit(solution)/shard_map/pair_spec/pallas_call | solution.py:461
  266.2 1.6 copy-done.23
  267.8 9.0 %adjoint_columns_a.1 = (f32[2,2048,128]{2,1,0:T(8,128)S(1)}, f32[2048,128]{1,0:T(8,128)S(1)}) custom-call(s32[2]{0:T(128)S(1)} %copy-done.43, f32[2048,256]{1,0:T(8,128)S(1)} %bitcast.14, f32[2,2048,128]{2,1,0:T(8,128)S(1)} %get-tuple-element.22.pairs, bf16[16,256,256]{2,1,0:T(8,128)(2,1)S(1)} %copy-done.13, bf16[16,256,256]{2,1,0:T(8,128)(2,1)S(1)} %copy-done.10), custom_call_target="tpu_custom_call" | custom-call | tf_op jit(solution)/shard_map/adjoint_columns_a/pallas_call | solution.py:629
  276.8 1.4 copy-done.25
  280.5 1.6 copy-done.11
  282.1 1.6 copy-done.14
  283.7 1.6 copy-done.20
  285.3 1.6 copy-done.32
  288.1 20.3 %adjoint_columns_b.1 = f32[32,64,128]{2,1,0:T(8,128)S(1)} custom-call(s32[2]{0:T(128)S(1)} %copy-done.43, f32[2048,128]{1,0:T(8,128)S(1)} %bitcast.16, f32[2048,128]{1,0:T(8,128)S(1)} %copy-done.36, f32[2,2048,128]{2,1,0:T(8,128)S(1)} %copy-done.32, f32[2,2048,128]{2,1,0:T(8,128)S(1)} %copy-done.20, bf16[16,256,256]{2,1,0:T(8,128)(2,1)S(1)} %copy-done.14, ...), custom_call_target="tpu_custom_call" | custom-call | tf_op jit(solution)/shard_map/adjoint_columns_b/pallas_call | solution.py:716
  309.3 2.8 all-to-all-start.2
  312.8 25.5 %all-to-all-done.2.spectra = f32[32,64,128]{2,1,0:T(8,128)S(1)} async-done(((f32[32,64,128]{2,1,0:T(8,128)}), f32[32,64,128]{2,1,0:T(8,128)S(1)}, u32[]{:S(2)}, u32[]{:S(2)}) %all-to-all-start.2) | async-done | bytes 1048608 | tf_op jit(solution)/shard_map/all_to_all | solution.py:1027
  338.3 3.7 all-to-all-start.3
  342.0 2.2 copy-done
  344.2 2.2 copy-done.3
  346.4 14.1 %gradient_rows.1 = (f32[128,2048]{1,0:T(8,128)}, f32[16,192,128]{2,1,0:T(8,128)}) custom-call(s32[16]{0:T(128)S(1)} %bitcast.23, s32[2048]{0:T(1024)S(1)} %bitcast.20, f32[32,64,128]{2,1,0:T(8,128)S(1)} %all-to-all-done.2.spectra, bf16[8,256,1024]{2,1,0:T(8,128)(2,1)S(1)} %copy-done.3, bf16[8,256,1024]{2,1,0:T(8,128)(2,1)S(1)} %copy-done), custom_call_target="tpu_custom_call" | custom-call | tf_op jit(solution)/shard_map/gradient_rows/pallas_call | solution.py:892
  360.5 6.3 %all-to-all-start.4 = ((f32[16,192,128]{2,1,0:T(8,128)}), f32[16,192,128]{2,1,0:T(8,128)S(1)}, u32[]{:S(2)}, u32[]{:S(2)}) async-start(f32[16,192,128]{2,1,0:T(8,128)} %get-tuple-element.27), calls=%async_computation.4 | async-start | bytes 3145728 | tf_op jit(solution)/shard_map/all_to_all | solution.py:1027
  367.2 31.6 %all-to-all-done.4.incoming = f32[16,192,128]{2,1,0:T(8,128)S(1)} async-done(((f32[16,192,128]{2,1,0:T(8,128)}), f32[16,192,128]{2,1,0:T(8,128)S(1)}, u32[]{:S(2)}, u32[]{:S(2)}) %all-to-all-start.4) | async-done | bytes 1572896 | tf_op jit(solution)/shard_map/all_to_all | solution.py:1027
  400.0 2.6 owner_update.1
  402.5 45.0 %all_to_all.51.returned = f32[16,192,128]{2,1,0:T(8,128)S(1)} all-to-all(f32[16,192,128]{2,1,0:T(8,128)S(1)} %get-tuple-element.29), channel_id=1, replica_groups=mesh['grp'=1,'pen'=16,'dep'=2,'chan'=1] {'pen'}, dimensions={0} | all-to-all | bytes 3145728 | tf_op jit(solution)/shard_map/all_to_all | solution.py:1027
  447.5 2.2 copy-done.18
  449.7 12.4 %model_rows.1 = f32[32,64,128]{2,1,0:T(8,128)S(1)} custom-call(s32[16]{0:T(128)S(1)} %bitcast.24, s32[2048]{0:T(1024)S(1)} %bitcast.21, f32[16,192,128]{2,1,0:T(8,128)S(1)} %all_to_all.51.returned, bf16[8,1024,256]{2,1,0:T(8,128)(2,1)S(1)} %copy-done.18, bf16[8,1024,256]{2,1,0:T(8,128)(2,1)S(1)} %copy-done.16), custom_call_target="tpu_custom_call" | custom-call | tf_op jit(solution)/shard_map/model_rows/pallas_call | solution.py:1003
  462.1 44.9 %all_to_all.52.moved = f32[32,64,128]{2,1,0:T(8,128)S(1)} all-to-all(f32[32,64,128]{2,1,0:T(8,128)S(1)} %model_rows.1), channel_id=1, replica_groups=mesh['grp'=1,'pen'=16,'dep'=2,'chan'=1] {'pen','dep'}, dimensions={0} | all-to-all | bytes 2097152 | tf_op jit(solution)/shard_map/all_to_all | solution.py:1027
  507.0 23.2 %forward_columns_b.1 = (f32[2048,128]{1,0:T(8,128)S(1)}, f32[2048,128]{1,0:T(8,128)S(1)}, f32[2,2,2048,128]{3,2,1,0:T(8,128)}) custom-call(s32[2]{0:T(128)S(1)} %copy-done.43, f32[32,64,128]{2,1,0:T(8,128)S(1)} %all_to_all.52.moved, f32[2,2048,128]{2,1,0:T(8,128)S(1)} %copy-done.21, bf16[16,256,256]{2,1,0:T(8,128)(2,1)S(1)} %copy-done.15, ...), custom_call_target="tpu_custom_call" | custom-call | tf_op jit(solution)/shard_map/forward_columns_b/pallas_call | solution.py:794
  532.1 3.6 all-to-all-start.8
  535.8 1.6 copy-done.9
  537.4 1.6 copy-done.26
  538.9 2.2 copy-done.28
  542.4 6.5 %forward_columns_a.1 = f32[2048,256]{1,0:T(8,128)S(1)} custom-call(s32[2]{0:T(128)S(1)} %copy-done.43, f32[2,2,2048,128]{3,2,1,0:T(8,128)S(1)} %copy-done.28, f32[2048,128]{1,0:T(8,128)S(1)} %copy-done.40, f32[2,2048,128]{2,1,0:T(8,128)S(1)} %copy-done.26, bf16[16,256,256]{2,1,0:T(8,128)(2,1)S(1)} %copy-done.9, bf16[16,256,256]{2,1,0:T(8,128)(2,1)S(1)} %copy-done.6), custom_call_target="tpu_custom_call" | custom-call | tf_op jit(solution)/shard_map/forward_columns_a/pallas_call | solution.py:841
  550.2 11.8 %all-to-all-done.8.spectra = f32[32,64,128]{2,1,0:T(8,128)S(1)} async-done(((f32[32,64,128]{2,1,0:T(8,128)}), f32[32,64,128]{2,1,0:T(8,128)S(1)}, u32[]{:S(2)}, u32[]{:S(2)}) %all-to-all-start.8) | async-done | bytes 1048608 | tf_op jit(solution)/shard_map/all_to_all | solution.py:1027
  562.0 3.6 all-to-all-start.7
  565.6 2.2 copy-done.1
  567.8 2.2 copy-done.4
  570.0 5.4 predicted_rows_b.1.before
  575.4 38.9 %all-to-all-done.7.spectra = f32[32,64,256]{2,1,0:T(8,128)S(1)} async-done(((f32[32,64,256]{2,1,0:T(8,128)}), f32[32,64,256]{2,1,0:T(8,128)S(1)}, u32[]{:S(2)}, u32[]{:S(2)}) %all-to-all-start.7) | async-done | bytes 2097184 | tf_op jit(solution)/shard_map/all_to_all | solution.py:1027
  614.4 2.2 copy-done.2
  616.5 2.2 copy-done.5
  618.7 8.1 %predicted_rows_a.1 = f32[6,64,2048]{2,1,0:T(8,128)} custom-call(f32[32,64,256]{2,1,0:T(8,128)S(1)} %all-to-all-done.7.spectra, bf16[8,256,1024]{2,1,0:T(8,128)(2,1)S(1)} %copy-done.5, bf16[8,256,1024]{2,1,0:T(8,128)(2,1)S(1)} %copy-done.2, f32[6,64,2048]{2,1,0:T(8,128)} %predicted_rows_b.1.before), custom_call_target="tpu_custom_call", output_to_operand_aliasing={{}: (3, {})} | custom-call | tf_op jit(solution)/shard_map/predicted_rows_a/pallas_call | solution.py:581
  (78 shorter events, 16.6 us)
Async XLA Ops:
  0.6 2.2 copy-start.17
  2.8 1.9 copy-start.30
  14.3 1.4 copy-start.33
  16.7 123.9 %all-to-all-start.1 = ((f32[32,64,256]{2,1,0:T(8,128)}), f32[32,64,256]{2,1,0:T(8,128)S(1)}, u32[]{:S(2)}, u32[]{:S(2)}) async-start(f32[32,64,256]{2,1,0:T(8,128)} %copy-done.33), calls=%async_computation.1 | async-start | bytes 4194304 | tf_op jit(solution)/shard_map/all_to_all | solution.py:1027
  24.7 210.0 %copy-start.43 = (s32[2]{0:T(128)S(1)}, s32[2]{0:T(128)}, u32[]{:S(2)}) copy-start(s32[2]{0:T(128)} %add_convert_fusion.flags) | copy-start | bytes 28
  34.3 200.4 %collective-permute-start = (f32[12,32,2048]{2,1,0:T(8,128)}, f32[12,32,2048]{2,1,0:T(8,128)}, u32[]{:S(2)}, u32[]{:S(2)}) collective-permute-start(f32[12,32,2048]{2,1,0:T(8,128)} %get-tuple-element.21), channel_id=1, source_target_pairs={{0,31},{1,30},{2,29},{3,28},{4,27},{5,26},{6,25},{7,24},{8,23},{9,... | collective-permute-start | bytes 9437192 | tf_op jit(solution)/shard_map/ppermute | solution.py:1050
  140.6 124.2 %copy-start.22 = (f32[32,64,256]{2,1,0:T(8,128)}, f32[32,64,256]{2,1,0:T(8,128)S(1)}, u32[]{:S(2)}) copy-start(f32[32,64,256]{2,1,0:T(8,128)S(1)} %all-to-all-done.1) | copy-start | bytes 6291460
  140.6 139.9 %all-to-all-start = ((f32[32,64,128]{2,1,0:T(8,128)}), f32[32,64,128]{2,1,0:T(8,128)S(1)}, u32[]{:S(2)}, u32[]{:S(2)}) async-start(f32[32,64,128]{2,1,0:T(8,128)} %copy-done.37), calls=%async_computation | async-start | bytes 2097152 | tf_op jit(solution)/shard_map/all_to_all | solution.py:1027
  144.9 89.7 %collective-permute-start.1 = (f32[12,1,2048]{2,1,0:T(1,128)S(1)}, f32[12,1,2048]{2,1,0:T(1,128)S(1)}, u32[]{:S(2)}, u32[]{:S(2)}) collective-permute-start(f32[12,1,2048]{2,1,0:T(1,128)S(1)} %slice_convert_fusion), channel_id=1, source_target_pairs={{16,0},{17,15},{18,14},{19,13},{20,12},{21,11},{22,10},{23,9},{24,... | collective-permute-start | bytes 294920 | tf_op jit(solution)/shard_map/ppermute | solution.py:1051
  234.6 1.9 copy-start.29
  236.5 29.7 %copy-start.10 = (bf16[16,256,256]{2,1,0:T(8,128)(2,1)S(1)}, bf16[16,256,256]{2,1,0:T(8,128)(2,1)}, u32[]{:S(2)}) copy-start(bf16[16,256,256]{2,1,0:T(8,128)(2,1)} %constant.35.clone.low) | copy-start | bytes 6291460
  236.5 29.7 %copy-start.13 = (bf16[16,256,256]{2,1,0:T(8,128)(2,1)S(1)}, bf16[16,256,256]{2,1,0:T(8,128)(2,1)}, u32[]{:S(2)}) copy-start(bf16[16,256,256]{2,1,0:T(8,128)(2,1)} %constant.34.clone.high) | copy-start | bytes 6291460
  264.8 1.3 copy-start.19
  266.2 1.6 copy-start.23
  267.8 12.7 %copy-start.7 = (bf16[16,256,256]{2,1,0:T(8,128)(2,1)S(1)}, bf16[16,256,256]{2,1,0:T(8,128)(2,1)}, u32[]{:S(2)}) copy-start(bf16[16,256,256]{2,1,0:T(8,128)(2,1)} %constant.36.clone.high_i) | copy-start | bytes 6291460
  276.8 1.4 copy-start.25
  278.2 1.3 copy-start.31
  280.5 1.6 copy-start.11
  282.1 1.6 copy-start.14
  283.7 1.6 copy-start.20
  285.3 1.6 copy-start.32
  286.8 1.2 copy-start.36
  309.3 2.8 copy-start.44
  309.3 32.7 %copy-start.42 = (s32[1,1,2048]{2,1,0:T(1,128)S(1)}, s32[1,1,2048]{2,1,0:T(1,128)}, u32[]{:S(2)}) copy-start(s32[1,1,2048]{2,1,0:T(1,128)} %param.18) | copy-start | bytes 24580
  309.3 29.0 %all-to-all-start.2 = ((f32[32,64,128]{2,1,0:T(8,128)}), f32[32,64,128]{2,1,0:T(8,128)S(1)}, u32[]{:S(2)}, u32[]{:S(2)}) async-start(f32[32,64,128]{2,1,0:T(8,128)} %copy-done.27), calls=%async_computation.2 | async-start | bytes 2097152 | tf_op jit(solution)/shard_map/all_to_all | solution.py:1027
  338.3 22.2 %all-to-all-start.3 = ((s32[16,1,1]{2,1,0:T(1,128)}), s32[16,1,1]{2,1,0:T(1,128)S(1)}, u32[]{:S(2)}, u32[]{:S(2)}) async-start(s32[16,1,1]{2,1,0:T(1,128)} %copy.19), calls=%async_computation.3 | async-start | bytes 16384 | tf_op jit(solution)/shard_map/all_to_all | solution.py:1027
  342.0 2.2 copy-start
  344.2 2.2 copy-start.3
  360.5 38.3 %copy-start.34 = (f32[1,1,3072,128]{3,2,1,0:T(8,128)S(1)}, f32[1,1,3072,128]{3,2,1,0:T(8,128)}, u32[]{:S(2)}) copy-start(f32[1,1,3072,128]{3,2,1,0:T(8,128)} %param.16) | copy-start | bytes 4718596
  360.5 38.3 %all-to-all-start.4 = ((f32[16,192,128]{2,1,0:T(8,128)}), f32[16,192,128]{2,1,0:T(8,128)S(1)}, u32[]{:S(2)}, u32[]{:S(2)}) async-start(f32[16,192,128]{2,1,0:T(8,128)} %get-tuple-element.27), calls=%async_computation.4 | async-start | bytes 3145728 | tf_op jit(solution)/shard_map/all_to_all | solution.py:1027
  400.0 47.5 %copy-start.16 = (bf16[8,1024,256]{2,1,0:T(8,128)(2,1)S(1)}, bf16[8,1024,256]{2,1,0:T(8,128)(2,1)}, u32[]{:S(2)}) copy-start(bf16[8,1024,256]{2,1,0:T(8,128)(2,1)} %constant.31.clone.low) | copy-start | bytes 12582916
  447.5 2.2 copy-start.18
  449.7 57.3 %copy-start.8 = (bf16[16,256,256]{2,1,0:T(8,128)(2,1)S(1)}, bf16[16,256,256]{2,1,0:T(8,128)(2,1)}, u32[]{:S(2)}) copy-start(bf16[16,256,256]{2,1,0:T(8,128)(2,1)} %constant.36.clone.high_i) | copy-start | bytes 6291460
  449.7 57.3 %copy-start.12 = (bf16[16,256,256]{2,1,0:T(8,128)(2,1)S(1)}, bf16[16,256,256]{2,1,0:T(8,128)(2,1)}, u32[]{:S(2)}) copy-start(bf16[16,256,256]{2,1,0:T(8,128)(2,1)} %constant.35.clone.low) | copy-start | bytes 6291460
  449.7 57.3 %copy-start.15 = (bf16[16,256,256]{2,1,0:T(8,128)(2,1)S(1)}, bf16[16,256,256]{2,1,0:T(8,128)(2,1)}, u32[]{:S(2)}) copy-start(bf16[16,256,256]{2,1,0:T(8,128)(2,1)} %constant.34.clone.high) | copy-start | bytes 6291460
  449.7 57.3 %copy-start.21 = (f32[2,2048,128]{2,1,0:T(8,128)S(1)}, f32[2,2048,128]{2,1,0:T(8,128)}, u32[]{:S(2)}) copy-start(f32[2,2048,128]{2,1,0:T(8,128)} %copy-done.19) | copy-start | bytes 6291460
  462.1 44.9 %copy-start.6 = (bf16[16,256,256]{2,1,0:T(8,128)(2,1)S(1)}, bf16[16,256,256]{2,1,0:T(8,128)(2,1)}, u32[]{:S(2)}) copy-start(bf16[16,256,256]{2,1,0:T(8,128)(2,1)} %constant.37.clone.low_i) | copy-start | bytes 6291460
  532.1 29.9 %all-to-all-start.8 = ((f32[32,64,128]{2,1,0:T(8,128)}), f32[32,64,128]{2,1,0:T(8,128)S(1)}, u32[]{:S(2)}, u32[]{:S(2)}) async-start(f32[32,64,128]{2,1,0:T(8,128)} %bitcast.18), calls=%async_computation.8 | async-start | bytes 2097152 | tf_op jit(solution)/shard_map/all_to_all | solution.py:1027
  535.8 1.6 copy-start.9
  537.4 1.6 copy-start.26
  538.9 2.2 copy-start.28
  541.1 1.2 copy-start.40
  548.8 1.3 copy-start.24
  562.0 52.4 %all-to-all-start.7 = ((f32[32,64,256]{2,1,0:T(8,128)}), f32[32,64,256]{2,1,0:T(8,128)S(1)}, u32[]{:S(2)}, u32[]{:S(2)}) async-start(f32[32,64,256]{2,1,0:T(8,128)} %bitcast.15), calls=%async_computation.7 | async-start | bytes 4194304 | tf_op jit(solution)/shard_map/all_to_all | solution.py:1027
  565.6 2.2 copy-start.1
  567.8 2.2 copy-start.4
  614.4 2.2 copy-start.2
  616.5 2.2 copy-start.5
  (6 other events, 6.0 us)

commit v2 on v1

--- a/solution.py
+++ b/solution.py
@@ -233,6 +233,8 @@
 
 RADIX = 16
 LANES = 128
+TILES = (((0, 0), (1, 32), (2, 64), (3, 96)), ((4, 0), (5, 64)))
+EDGES = ((4, 32), (0, 33), (1, 34), (5, 96), (2, 97), (3, 98))
 f32 = jnp.float32
 bf16 = jnp.bfloat16
 
@@ -277,6 +279,23 @@
         [np.concatenate([real, sine], axis=2), np.concatenate([-sine, real], axis=2)], axis=1
     )
     return (two_terms(forward), two_terms(forward.swapaxes(1, 2)))
+
+
+@functools.cache
+def lane_tables():
+    edges = [lane for _, lane in EDGES]
+    fold = np.zeros((2, LANES, LANES))
+    spread = np.zeros((LANES, 2, LANES))
+    for layer in range(2):
+        for _, lane in TILES[1]:
+            for i in range(32):
+                fold[layer, lane + i, 64 * layer + i] = 1.0
+                spread[64 * layer + i, layer, lane + i] = 1.0
+        fold[layer, edges, 64 * layer + 32] = 1.0
+        spread[64 * layer + 32, layer, edges] = 1.0
+    fold = np.concatenate([fold[0], fold[0], fold[1], fold[1]])
+    spread = np.tile(spread.reshape(LANES, 2 * LANES), (2, 1))
+    return (fold.astype(ml_dtypes.bfloat16), spread.astype(ml_dtypes.bfloat16))
 
 
 def split(value):
@@ -376,108 +395,112 @@
             store(a, first, re, im)
 
 
-def column_product(tables, k, value):
-    return dot3((tables[0][k], tables[1][k]), split(value))
-
-
-def part_kernel(flags, spec, sent, kept, wide):
-    wide[...] = spec[0].astype(f32)
-    upper = flags[0]
-    half = kept.shape[1]
-    for i in range(half):
-        sent[0, half - 1 - i : half - i, :] = wide[pl.ds(2 * i + 1 - upper, 1), :]
-        kept[0, i : i + 1, :] = wide[pl.ds(2 * i + upper, 1), :]
-
-
-def part_spec(flags, spec):
+def column_product(tables, value):
+    high, low = split(value)
+    wide = dot(tables[0], jnp.concatenate([high, low], axis=1))
+    return wide[:, :LANES] + wide[:, LANES:] + dot(tables[1], high)
+
+
+def choose_rows(wanted, value):
+    columns = lax.broadcasted_iota(jnp.int32, (wanted.shape[0], value.shape[0]), 1)
+    return dot((columns == wanted).astype(f32).astype(bf16), value)
+
+
+def part_kernel(flags, spec, sent):
+    half = sent.shape[1]
+    wanted = 2 * (half - 1 - lax.broadcasted_iota(jnp.int32, (half, 2 * half), 0)) + 1 - flags[0]
+    for line in range(sent.shape[0]):
+        sent[line] = choose_rows(wanted, spec[line])
+
+
+def part_spec(flags, spec, begin, end):
     count, width, n = spec.shape
     half = width // 2
-    block = pl.BlockSpec((1, half, n), lambda s: (s, 0, 0))
+    step = 2
     return pl.pallas_call(
         part_kernel,
-        grid=(count,),
-        out_shape=[jax.ShapeDtypeStruct((count, half, n), f32)] * 2,
+        grid=((end - begin) // step,),
+        out_shape=pltpu.HBM((end - begin, half, n), f32),
         in_specs=[
             pl.BlockSpec(memory_space=pltpu.SMEM),
-            pl.BlockSpec((1, width, n), lambda s: (s, 0, 0)),
-        ],
-        out_specs=[block, block],
-        scratch_shapes=[pltpu.VMEM((width, n), f32)],
+            pl.BlockSpec((step, width, n), lambda s: (s + begin // step, 0, 0)),
+        ],
+        out_specs=pl.BlockSpec((step, half, n), lambda s: (s, 0, 0)),
         name="part_spec",
-    )(flags, spec)
-
-
-TILE_ROWS = {0: (0, 0), 1: (0, 32), 2: (0, 64), 3: (0, 96), 4: (1, 0), 5: (1, 32)}
-EDGE_LANES = {4: 64, 0: 65, 2: 66, 5: 96, 1: 97, 3: 98}
-
-
-def pair_kernel(flags, kept, got, edge, pairs_a, pairs_b, own, mirror, room, rows):
-    k = pl.program_id(0)
-    n = own.shape[1]
-
-    @pl.when(k == 0)
-    def _():
-        first, upper = flags[1], flags[0]
-        for layer in range(2):
-            for channel in range(6):
+    )(flags, in_hbm(spec))
+
+
+def pair_kernel(flags, spec, got_a, got_b, edge, pairs, own, mirror, room, own_t, mirror_t):
+    step = pl.program_id(0)
+    layer = lax.rem(step, 2)
+    upper, first = flags[0], flags[1]
+    half = got_a.shape[1]
+    n = spec.shape[2]
+    wanted = 2 * lax.broadcasted_iota(jnp.int32, (half, 2 * half), 0) + upper
+
+    def weight(channel):
+        return -0.5 if channel in (2, 4) else 0.5
+
+    for tile in range(2):
+
+        @pl.when(lax.div(step, 2) == tile)
+        def _():
+            if tile == 1:
+                own[...] = jnp.zeros_like(own)
+                mirror[...] = jnp.zeros_like(mirror)
+                for channel, lane in EDGES:
+                    row = edge[2 * channel + layer]
+                    own[lane : lane + 1, :] = row * 0.5
+                    mirror[lane : lane + 1, :] = row * weight(channel)
+            for channel, lane in TILES[tile]:
                 line = 2 * channel + layer
-                weight = -0.5 if channel in (2, 4) else 0.5
-                tile, place = TILE_ROWS[channel]
-                base = (2 * layer + tile) * LANES + place
-                own[base : base + 32, :] = (kept[line] * 0.5).astype(bf16)
-                room[0:1, :] = jnp.where(first == 1, kept[line, 0:1, :], edge[line])
-                room[1:33, :] = got[line]
-                mirror[base : base + 32, :] = (
-                    jnp.where(upper == 1, room[1:33, :], room[0:32, :]) * weight
-                ).astype(bf16)
-            base = (2 * layer + 1) * LANES + 64
-            for target, weights in ((own, (0.5, 0.5)), (mirror, (0.5, -0.5))):
-                rows[...] = jnp.zeros_like(rows)
-                for channel, lane in EDGE_LANES.items():
-                    weight = weights[1] if channel in (2, 4) else weights[0]
-                    rows[lane - 64 : lane - 63, :] = edge[2 * channel + layer] * weight
-                target[base : base + 64, :] = rows[...].astype(bf16)
-
-    lane = lax.broadcasted_iota(jnp.int32, (LANES, n), 1)
-    wanted = RADIX * lax.broadcasted_iota(jnp.int32, (LANES, n), 0) + k
-    contract_last = (((1,), (1,)), ((), ()))
-    total = lax.dot_general(
-        (lane == wanted).astype(f32).astype(bf16), own[...], contract_last, preferred_element_type=f32
-    ) + lax.dot_general(
-        (lane == lax.rem(n - wanted, n)).astype(f32).astype(bf16),
-        mirror[...],
-        contract_last,
-        preferred_element_type=f32,
-    )
-    for layer in range(2):
-        pairs_a[layer] = total[:, 2 * layer * LANES : (2 * layer + 1) * LANES]
-        pairs_b[layer] = total[:, (2 * layer + 1) * LANES : (2 * layer + 2) * LANES]
-
-
-def pair_spec(flags, kept, got, edge):
-    count, half, n = kept.shape
-    whole = pl.BlockSpec((count, half, n), lambda k: (0, 0, 0))
-    out = pl.BlockSpec((2, LANES, LANES), lambda k: (0, k, 0))
+                kept = choose_rows(wanted, spec[line])
+                own[lane : lane + half, :] = kept * 0.5
+                room[0:1, :] = jnp.where(first == 1, kept[0:1, :], edge[line])
+                room[1 : 1 + half, :] = got_a[line] if tile == 0 else got_b[line - 8]
+                mirror[lane : lane + half, :] = (
+                    jnp.where(upper == 1, room[1 : 1 + half, :], room[0:half, :]) * weight(channel)
+                )
+
+    for block in range(n // LANES):
+        here = slice(block * LANES, (block + 1) * LANES)
+        own_t[here, :] = jnp.transpose(own[:, here])
+        mirror_t[here, :] = jnp.transpose(mirror[:, here])
+    row = lax.broadcasted_iota(jnp.int32, (LANES, LANES), 0)
+    for k in range(RADIX):
+        wanted_k = LANES - 1 - row if k > 0 else (LANES - row) & (LANES - 1)
+        other = mirror_t[pl.ds((RADIX - k) % RADIX, LANES, stride=RADIX), :]
+        pairs[0, k * LANES : (k + 1) * LANES, :] = own_t[
+            pl.ds(k, LANES, stride=RADIX), :
+        ] + choose_rows(wanted_k, other.astype(bf16))
+
+
+def pair_spec(flags, spec, got_a, got_b, edge):
+    count, width, n = spec.shape
+    single = pl.Buffered(1)
     return pl.pallas_call(
         pair_kernel,
-        grid=(RADIX,),
-        out_shape=[jax.ShapeDtypeStruct((2, n, LANES), f32)] * 2,
+        grid=(4,),
+        out_shape=pltpu.HBM((4, n, LANES), f32),
         in_specs=[
             pl.BlockSpec(memory_space=pltpu.SMEM),
-            whole,
-            whole,
-            pl.BlockSpec((count, 1, n), lambda k: (0, 0, 0)),
-        ],
-        out_specs=[out, out],
+            pl.BlockSpec((count, width, n), lambda s: (0, 0, 0), pipeline_mode=single),
+            pl.BlockSpec(got_a.shape, lambda s: (0, 0, 0), pipeline_mode=single),
+            pl.BlockSpec(got_b.shape, lambda s: (0, 0, 0), pipeline_mode=single),
+            pl.BlockSpec((count, 1, n), lambda s: (0, 0, 0)),
+        ],
+        out_specs=pl.BlockSpec((1, n, LANES), lambda s: (s, 0, 0)),
         scratch_shapes=[
-            pltpu.VMEM((4 * LANES, n), bf16),
-            pltpu.VMEM((4 * LANES, n), bf16),
+            pltpu.VMEM((LANES, n), f32),
+            pltpu.VMEM((LANES, n), f32),
             pltpu.VMEM((40, n), f32),
-            pltpu.VMEM((64, n), f32),
-        ],
-        compiler_params=pltpu.CompilerParams(vmem_limit_bytes=44 << 20),
+            pltpu.VMEM((n, LANES), f32),
+            pltpu.VMEM((n, LANES), f32),
+        ],
+        compiler_params=pltpu.CompilerParams(vmem_limit_bytes=24 << 20),
+        cost_estimate=pl.CostEstimate(flops=0, bytes_accessed=60_000_000, transcendentals=0),
         name="pair_spec",
-    )(flags, kept, got, edge)
+    )(flags, in_hbm(spec), in_hbm(got_a), in_hbm(got_b), edge)
 
 
 def misfit_rows_kernel(misfit, high, low, out_a, out_b, halves_high, halves_low):
@@ -499,7 +522,7 @@
     for index in range(4):
         out_a[index, :, :LANES] = parts[0][index]
         out_a[index, :, LANES:] = parts[1][index]
-    for index, value in enumerate(quad_transpose([real[4], real[5], imag[4], imag[5]])):
+    for index, value in enumerate(quad_transpose([real[4], imag[4], real[5], imag[5]])):
         out_b[index] = value
 
 
@@ -519,15 +542,33 @@
             pl.BlockSpec((4, rows, LANES), lambda s: (s, 0, 0)),
         ],
         scratch_shapes=[pltpu.VMEM((2, channels * rows, n // 2), bf16)] * 2,
-        compiler_params=pltpu.CompilerParams(vmem_limit_bytes=40 << 20),
+        compiler_params=pltpu.CompilerParams(vmem_limit_bytes=22 << 20),
         name="misfit_rows",
     )(misfit, *tables)
 
 
-def inverse_step(lhs, high, low, sums):
+AHEAD = 3
+
+
+def inverse_step(lhs, table, sums, held, arrived):
     s = pl.program_id(0)
     steps = pl.num_programs(0)
-    product = dot3(split(lhs), (high[0], low[0]))
+
+    def fetch(step):
+        return pltpu.make_async_copy(table.at[step], held.at[step], arrived.at[step])
+
+    @pl.when(s == 0)
+    def _():
+        for step in range(AHEAD):
+            fetch(step).start()
+
+    fetch(s).wait()
+
+    @pl.when(s + AHEAD < steps)
+    def _():
+        fetch(s + AHEAD).start()
+
+    product = dot3(split(lhs), (held[s, 0], held[s, 1]))
     side = s // (steps // 2)
     fresh = s % (steps // 2) == 0
 
@@ -540,214 +581,300 @@
         sums[side] += product
 
 
-def predicted_kernel_b(spectra, high, low, out, sums):
+def inverse_scratch(rows, n, steps):
+    return [
+        pltpu.VMEM((2, rows, n // 2), f32),
+        pltpu.VMEM((steps, 2, 2 * LANES, n // 2), bf16),
+        pltpu.SemaphoreType.DMA((steps,)),
+    ]
+
+
+def finish_channels(out, sums, channels):
     rows, n = out.shape[1:]
-    c4r, c5r, c4i, c5i = quad_transpose([spectra[index] for index in range(4)])
+
+    @pl.when(pl.program_id(0) == pl.num_programs(0) - 1)
+    def _():
+        for channel in range(channels):
+            here = slice(channel * rows, (channel + 1) * rows)
+            out[channel, :, : n // 2] = sums[0, here] + sums[1, here]
+            out[channel, :, n // 2 :] = sums[0, here] - sums[1, here]
+
+
+def predicted_kernel_b(spectra, table, out, sums, held, arrived):
+    c4r, c4i, c5r, c5i = quad_transpose([spectra[index] for index in range(4)])
     lhs = jnp.concatenate(
         [jnp.concatenate([c4r, c4i], axis=1), jnp.concatenate([c5r, c5i], axis=1)], axis=0
     )
-    inverse_step(lhs, high, low, sums)
-
-    @pl.when(pl.program_id(0) == pl.num_programs(0) - 1)
-    def _():
-        for channel in range(2):
-            even, odd = sums[0, channel * rows : (channel + 1) * rows], sums[1, channel * rows : (channel + 1) * rows]
-            out[channel, :, : n // 2] = even + odd
-            out[channel, :, n // 2 :] = even - odd
-
-
-def predicted_kernel_a(spectra, high, low, before, out, sums):
-    rows, n = out.shape[1:]
+    inverse_step(lhs, table, sums, held, arrived)
+    finish_channels(out, sums, 2)
+
+
+def predicted_kernel_a(spectra, table, before, out, sums, held, arrived):
     real = quad_transpose([spectra[index, :, :LANES] for index in range(4)])
     imag = quad_transpose([spectra[index, :, LANES:] for index in range(4)])
-    lhs = jnp.concatenate(
-        [jnp.concatenate(pair, axis=1) for pair in zip(real, imag)], axis=0
-    )
-    inverse_step(lhs, high, low, sums)
-
-    @pl.when(pl.program_id(0) == pl.num_programs(0) - 1)
-    def _():
-        for channel in range(4):
-            even, odd = sums[0, channel * rows : (channel + 1) * rows], sums[1, channel * rows : (channel + 1) * rows]
-            out[channel, :, : n // 2] = even + odd
-            out[channel, :, n // 2 :] = even - odd
-
-
-def predicted_rows(spectra, tables, before, n):
+    lhs = jnp.concatenate([jnp.concatenate(pair, axis=1) for pair in zip(real, imag)], axis=0)
+    inverse_step(lhs, table, sums, held, arrived)
+    finish_channels(out, sums, 4)
+
+
+def predicted_rows(spectra, table, before, n):
     devices, rows, lanes = spectra.shape
-    table = pl.BlockSpec((1, 2 * LANES, n // 2), lambda s: (s, 0, 0))
-    chunk = pl.BlockSpec((4, rows, lanes), lambda s: (s, 0, 0))
+    hbm = pl.BlockSpec(memory_space=pltpu.HBM)
     channels = 2 if before is None else 4
     return pl.pallas_call(
         predicted_kernel_b if before is None else predicted_kernel_a,
         grid=(devices // 4,),
         out_shape=jax.ShapeDtypeStruct((6, rows, n), f32),
-        in_specs=[chunk, table, table] + ([] if before is None else [pl.BlockSpec(memory_space=pl.ANY)]),
+        in_specs=[pl.BlockSpec((4, rows, lanes), lambda s: (s, 0, 0)), hbm] + ([] if before is None else [hbm]),
         out_specs=pl.BlockSpec((channels, rows, n), lambda s: (2 if before is None else 0, 0, 0)),
-        scratch_shapes=[pltpu.VMEM((2, channels * rows, n // 2), f32)],
-        input_output_aliases={} if before is None else {3: 0},
-        compiler_params=pltpu.CompilerParams(vmem_limit_bytes=32 << 20),
+        scratch_shapes=inverse_scratch(channels * rows, n, devices // 4),
+        input_output_aliases={} if before is None else {2: 0},
+        compiler_params=pltpu.CompilerParams(vmem_limit_bytes=26 << 20),
         name="predicted_rows_b" if before is None else "predicted_rows_a",
-    )(spectra, *tables, *([] if before is None else [before]))
-
-
-def write_sum(total, layer0, layer1):
-    return jnp.where(lane_of(total.shape) < 64, layer0, layer1)
-
-
-def adjoint_kernel_a(flags, spectra, pairs, high, low, sums, edges, work):
+    )(spectra, in_hbm(table), *([] if before is None else [before]))
+
+
+GROUPS = 4
+
+
+def started(*copies):
+    made = [pltpu.make_async_copy(*copy) for copy in copies]
+    for copy in made:
+        copy.start()
+    return made
+
+
+def group_rows(group):
+    size = RADIX // GROUPS * LANES
+    return pl.ds(group * size, size)
+
+
+def group_steps(group):
+    return pl.ds(group * (RADIX // GROUPS), RADIX // GROUPS)
+
+
+def in_group(group):
+    return range(group * (RADIX // GROUPS), (group + 1) * (RADIX // GROUPS))
+
+
+def pair_copies(pairs, tile, held, arrived, group):
+    here = group_rows(group)
+    return (pairs.at[pl.ds(2 * tile, 2), here], held.at[:, here], arrived.at[group])
+
+
+def table_copies(table, held, arrived, group):
+    here = group_steps(group)
+    return (table.at[here], held.at[here], arrived.at[group])
+
+
+def table_product(table, k, value):
+    return column_product((table[k, 0], table[k, 1]), value)
+
+
+TABLE = pltpu.VMEM((RADIX, 2, 2 * LANES, 2 * LANES), bf16)
+WORK = pltpu.VMEM((RADIX, 2 * LANES, LANES), f32)
+SIGNALS = pltpu.SemaphoreType.DMA((GROUPS,))
+
+
+def pairs_like(n):
+    return pltpu.VMEM((2, n, LANES), f32)
+
+
+def turn_phase(channel_lanes, real, imag, sign):
+    if sign < 0:
+        return jnp.where(channel_lanes, imag, real), jnp.where(channel_lanes, -real, imag)
+    return jnp.where(channel_lanes, -imag, real), jnp.where(channel_lanes, real, imag)
+
+
+def adjoint_kernel_a(
+    flags, spectra, pairs, table, sums, edges, work, here, held_pairs, held_table, got, got_pairs, got_table
+):
     first = flags[1] == 1
+    read = started((spectra, here, got.at[0]))
+    later = [
+        started(pair_copies(pairs, 0, held_pairs, got_pairs, g), table_copies(table, held_table, got_table, g))
+        for g in range(GROUPS)
+    ]
     lane8 = lane_of((8, LANES))
     packed = jnp.logical_and(lane8 % 32 == 0, first)
+    read[0].wait()
 
     def load(a, row):
-        real = spectra[pl.ds(a * LANES + row, 8), :LANES]
-        imag = spectra[pl.ds(a * LANES + row, 8), LANES:]
-        edges[pl.ds(a * LANES + row, 8), :] = jnp.where(
-            (lane8 == 65) | (lane8 == 97), turn(imag, 65), turn(imag, 2)
-        )
+        real = here[pl.ds(a * LANES + row, 8), :LANES]
+        imag = here[pl.ds(a * LANES + row, 8), LANES:]
+        edges[pl.ds(a * LANES + row, 8), :] = jnp.where(lane8 % 64 == 33, turn(imag, 33), turn(imag, 2))
         return (real, jnp.where(packed, 0.0, imag))
 
     forward_blocks(load, work)
     lane = lane_of((LANES, LANES))
     turned = lane // 32 == 2
-
-    @pl.loop(0, RADIX)
-    def _(k):
-        spectrum = column_product((high, low), k, work[k])
-        real, imag = spectrum[:LANES], spectrum[LANES:]
-        real, imag = jnp.where(turned, imag, real), jnp.where(turned, -real, imag)
-        row = pl.multiple_of(k * LANES, LANES)
-        for index, value in enumerate((real, imag)):
-            v0, v1 = value * pairs[0, pl.ds(row, LANES), :], value * pairs[1, pl.ds(row, LANES), :]
-            both = jnp.where(lane < 64, v0 + turn(v0, 64), v1 + turn(v1, 64))
-            sums[index, pl.ds(row, LANES), :] = both + turn(both, 96)
-
-
-def adjoint_columns_a(flags, spectra, pairs, tables):
+    for group in range(GROUPS):
+        for copy in later[group]:
+            copy.wait()
+        for k in in_group(group):
+            spectrum = table_product(held_table, k, work[k])
+            real, imag = turn_phase(turned, spectrum[:LANES], spectrum[LANES:], -1)
+            row = slice(k * LANES, (k + 1) * LANES)
+            for index, value in enumerate((real, imag)):
+                v0, v1 = value * held_pairs[0, row, :], value * held_pairs[1, row, :]
+                both = jnp.where(lane < 64, v0, turn(v1, 64)) + jnp.where(lane < 64, turn(v0, 64), v1)
+                sums[index, row, :] = both + turn(both, 96)
+
+
+def adjoint_columns_a(flags, spectra, pairs, table):
     n = spectra.shape[0]
+    hbm = pl.BlockSpec(memory_space=pltpu.HBM)
     return pl.pallas_call(
         adjoint_kernel_a,
         out_shape=[
             jax.ShapeDtypeStruct((2, n, LANES), f32),
             jax.ShapeDtypeStruct((n, LANES), f32),
         ],
-        in_specs=[pl.BlockSpec(memory_space=pltpu.SMEM)] + [pl.BlockSpec(memory_space=pltpu.VMEM)] * 4,
-        scratch_shapes=[pltpu.VMEM((RADIX, 2 * LANES, LANES), f32)],
-        compiler_params=pltpu.CompilerParams(vmem_limit_bytes=32 << 20),
+        in_specs=[pl.BlockSpec(memory_space=pltpu.SMEM), hbm, hbm, hbm],
+        scratch_shapes=[
+            WORK,
+            pltpu.VMEM((n, 2 * LANES), f32),
+            pairs_like(n),
+            TABLE,
+            pltpu.SemaphoreType.DMA((1,)),
+            SIGNALS,
+            SIGNALS,
+        ],
+        compiler_params=pltpu.CompilerParams(vmem_limit_bytes=24 << 20),
+        cost_estimate=pl.CostEstimate(flops=0, bytes_accessed=20_000_000, transcendentals=0),
         name="adjoint_columns_a",
-    )(flags, spectra, pairs, *tables)
-
-
-def adjoint_kernel_b(flags, spectra, edges, sums, pairs, high, low, high_i, low_i, out, work, fields):
+    )(flags, in_hbm(spectra), in_hbm(pairs), in_hbm(table))
+
+
+def adjoint_kernel_b(
+    flags, spectra, edges, sums, fold, pairs, table, table_i, out,
+    work, here, held_pairs, held_table, held_table_i, fields, chunks, got, got_pairs, got_table, got_table_i, left,
+):
     first = flags[1] == 1
+    read = started((spectra, here, got.at[0]))
+    later = [
+        started(
+            table_copies(table, held_table, got_table, g),
+            pair_copies(pairs, 1, held_pairs, got_pairs, g),
+        )
+        for g in range(GROUPS)
+    ]
+    last = [started(table_copies(table_i, held_table_i, got_table_i, g))[0] for g in range(GROUPS)]
     lane8 = lane_of((8, LANES))
-    packed = jnp.logical_and(lane8 % 32 == 0, first)
-    main = lane8 < 64
-    here = (lane8 == 64) | (lane8 == 96)
-    moved = (lane8 == 65) | (lane8 == 66) | (lane8 == 97) | (lane8 == 98)
+    main = lane8 % 64 < 32
+    packed = jnp.logical_and(lane8 % 64 == 0, first)
+    in_place = lane8 % 64 == 32
+    packed_edge = jnp.logical_and(in_place, first)
+    moved = (lane8 % 64 == 33) | (lane8 % 64 == 34)
+    read[0].wait()
 
     def load(a, row):
-        value = spectra[pl.ds(a * LANES + row, 8), :]
+        value = here[pl.ds(a * LANES + row, 8), :]
         edge = edges[pl.ds(a * LANES + row, 8), :]
-        real = jnp.where(main | here, value, jnp.where(moved, edge, 0.0))
-        imag = jnp.where(main, jnp.where(packed, 0.0, turn(value, 64)), 0.0)
+        real = jnp.where(main | in_place, value, jnp.where(moved, edge, 0.0))
+        imag = jnp.where(jnp.logical_and(main, jnp.logical_not(packed)), turn(value, 96), 0.0)
         return (real, imag)
 
     forward_blocks(load, work)
     lane = lane_of((LANES, LANES))
-    turned = (lane < 32) | (lane == 64) | (lane == 66)
-    low_main = lane < 32
-    high_main = (lane >= 64) & (lane < 96)
-
-    @pl.loop(0, RADIX)
-    def _(k):
-        spectrum = column_product((high, low), k, work[k])
-        real, imag = spectrum[:LANES], spectrum[LANES:]
-        real, imag = jnp.where(turned, imag, real), jnp.where(turned, -real, imag)
-        row = pl.multiple_of(k * LANES, LANES)
-        parts = []
-        for index, value in enumerate((real, imag)):
-            t0, t1 = (value * pairs[layer, pl.ds(row, LANES), :] for layer in range(2))
-            t0, t1 = t0 + turn(t0, 96), t1 + turn(t1, 96)
-            e0, e1 = (t + turn(t, 127) + turn(t, 126) for t in (t0, t1))
-            total = sums[index, pl.ds(row, LANES), :]
-            parts.append(
-                jnp.where(
-                    low_main,
-                    total + t0,
-                    jnp.where(
-                        high_main,
-                        total + turn(t1, 64),
-                        jnp.where(
-                            lane == 32, turn(e0, 96), jnp.where(lane == 96, turn(e1, 32), 0.0)
-                        ),
-                    ),
-                )
-            )
-        work[k] = column_product((high_i, low_i), k, jnp.concatenate(parts, axis=0))
+    turned = (lane <= 32) | (lane == 97)
+    on_main = lane % 64 < 32
+    for group in range(GROUPS):
+        for copy in later[group][:2]:
+            copy.wait()
+        for k in in_group(group):
+            spectrum = table_product(held_table, k, work[k])
+            row = slice(k * LANES, (k + 1) * LANES)
+            parts = []
+            for value in turn_phase(turned, spectrum[:LANES], spectrum[LANES:], -1):
+                terms = split(value * held_pairs[0, row, :]) + split(value * held_pairs[1, row, :])
+                parts.append(jnp.concatenate(terms, axis=1))
+            folded = dot(jnp.concatenate(parts, axis=0), fold[...])
+            for index in range(2):
+                half = slice(index * LANES, (index + 1) * LANES)
+                work[k, half] = folded[half] + jnp.where(on_main, sums[index, row, :], 0.0)
+    for group in range(GROUPS):
+        last[group].wait()
+        for k in in_group(group):
+            work[k] = table_product(held_table_i, k, work[k])
 
     def store(a, row, real, imag):
-        edge = turn(real, 96)
-        fields[0, pl.ds(a * LANES + row, 8), :] = real
-        fields[1, pl.ds(a * LANES + row, 8), :] = jnp.where(
-            jnp.logical_and(lane8 % 64 == 0, first), edge, imag
-        )
+        fields[pl.ds(a * LANES + row, 8), :] = jnp.where(main | packed_edge, real, turn(imag, 32))
 
     inverse_blocks(work, store)
     lane64 = lane_of((64, LANES))
+    leaving = []
     for band in range(RADIX):
-        pieces = [
-            fields[part, band * LANES + 64 * side : band * LANES + 64 * side + 64, :]
-            for part in range(2)
-            for side in range(2)
-        ]
-        for layer in range(2):
-            shifted = [turn(piece, 32 * q - 64 * layer) for q, piece in enumerate(pieces)]
-            out[2 * band + layer] = jnp.where(
-                lane64 < 32,
-                shifted[0],
-                jnp.where(lane64 < 64, shifted[1], jnp.where(lane64 < 96, shifted[2], shifted[3])),
-            )
-
-
-def adjoint_columns_b(flags, spectra, edges, sums, pairs, tables, inverse_tables):
+        upper, lower = (fields[band * LANES + side : band * LANES + side + 64, :] for side in (0, 64))
+        chunks[2 * band] = jnp.where(lane64 < 64, upper, turn(lower, 64))
+        chunks[2 * band + 1] = jnp.where(lane64 < 64, turn(upper, 64), lower)
+        if band % 4 == 3:
+            part = pl.ds(2 * (band - 3), 8)
+            leaving += started((chunks.at[part], out.at[part], left.at[band // 4]))
+    for copy in leaving:
+        copy.wait()
+
+
+def adjoint_columns_b(flags, spectra, edges, sums, pairs, table, table_i):
     n = spectra.shape[0]
+    hbm = pl.BlockSpec(memory_space=pltpu.HBM)
+    vmem = pl.BlockSpec(memory_space=pltpu.VMEM)
+    chunks = (2 * RADIX, 64, LANES)
     return pl.pallas_call(
         adjoint_kernel_b,
-        out_shape=jax.ShapeDtypeStruct((2 * RADIX, 64, LANES), f32),
-        in_specs=[pl.BlockSpec(memory_space=pltpu.SMEM)] + [pl.BlockSpec(memory_space=pltpu.VMEM)] * 8,
+        out_shape=pltpu.HBM(chunks, f32),
+        in_specs=[pl.BlockSpec(memory_space=pltpu.SMEM), hbm, vmem, vmem, vmem, hbm, hbm, hbm],
+        out_specs=hbm,
         scratch_shapes=[
-            pltpu.VMEM((RADIX, 2 * LANES, LANES), f32),
-            pltpu.VMEM((2, n, LANES), f32),
-        ],
-        compiler_params=pltpu.CompilerParams(vmem_limit_bytes=40 << 20),
+            WORK,
+            pltpu.VMEM((n, LANES), f32),
+            pairs_like(n),
+            TABLE,
+            TABLE,
+            pltpu.VMEM((n, LANES), f32),
+            pltpu.VMEM(chunks, f32),
+            pltpu.SemaphoreType.DMA((1,)),
+            SIGNALS,
+            SIGNALS,
+            SIGNALS,
+            SIGNALS,
+        ],
+        compiler_params=pltpu.CompilerParams(vmem_limit_bytes=30 << 20),
+        cost_estimate=pl.CostEstimate(flops=0, bytes_accessed=20_000_000, transcendentals=0),
         name="adjoint_columns_b",
-    )(flags, spectra, edges, sums, pairs, *tables, *inverse_tables)
-
-
-def forward_kernel_b(flags, moved, pairs, high, low, high_i, low_i, out, edges, model, work, fields):
+    )(flags, in_hbm(spectra), edges, sums, jnp.asarray(lane_tables()[0]), in_hbm(pairs), in_hbm(table), in_hbm(table_i))
+
+
+def forward_kernel_b(
+    flags, moved, spread, pairs, table, table_i, out, edges, model,
+    work, here, held_pairs, held_table, held_table_i, fields, chunk, held_model, held_edges,
+    got, got_pairs, got_table, got_table_i, left,
+):
     first = flags[1] == 1
+    read = started((moved, here, got.at[0]))
+    later = [
+        started(
+            table_copies(table, held_table, got_table, g),
+            pair_copies(pairs, 1, held_pairs, got_pairs, g),
+        )
+        for g in range(GROUPS)
+    ]
+    last = [started(table_copies(table_i, held_table_i, got_table_i, g))[0] for g in range(GROUPS)]
     lane64 = lane_of((64, LANES))
-    low_main = lane64 < 32
-    high_main = (lane64 >= 64) & (lane64 < 96)
-    edge_lane = (lane64 == 32) | (lane64 == 96)
+    main64 = lane64 % 64 < 32
+    packed64 = jnp.logical_and(lane64 % 64 == 0, first)
+    read[0].wait()
     for band in range(RADIX):
-        value0, value1 = moved[2 * band], moved[2 * band + 1]
-
-        def pick(q):
-            return jnp.where(
-                low_main,
-                turn(value0, -32 * q),
-                jnp.where(high_main, turn(value1, 64 - 32 * q), 0.0),
-            )
-
-        for side in range(2):
-            real, imag = pick(side), pick(2 + side)
+        value0, value1 = here[2 * band], here[2 * band + 1]
+        sides = (
+            jnp.where(lane64 < 64, value0, turn(value1, 64)),
+            jnp.where(lane64 < 64, turn(value0, 64), value1),
+        )
+        for side, value in enumerate(sides):
             row = band * LANES + 64 * side
-            fields[0, row : row + 64, :] = jnp.where(edge_lane, turn(imag, 32), real)
+            fields[0, row : row + 64, :] = value
             fields[1, row : row + 64, :] = jnp.where(
-                jnp.logical_and(lane64 % 64 == 0, first), 0.0, imag
+                jnp.logical_and(main64, jnp.logical_not(packed64)), turn(value, 96), 0.0
             )
 
     def load(a, row):
@@ -755,111 +882,168 @@
 
     forward_blocks(load, work)
     lane = lane_of((LANES, LANES))
-    turned = (lane < 32) | (lane == 64) | (lane == 66)
-
-    @pl.loop(0, RADIX)
-    def _(k):
-        spectrum = column_product((high, low), k, work[k])
-        row = pl.multiple_of(k * LANES, LANES)
-        totals = []
-        for part in range(2):
-            value = spectrum[part * LANES : (part + 1) * LANES]
-            spread = []
-            for layer in range(2):
-                main = jnp.where(lane < 32, turn(value, -64 * layer), 0.0)
-                main = main + turn(main, 32)
-                main = main + turn(main, 64)
-                model[layer, part, pl.ds(row, LANES), :] = main
-                at = 32 + 64 * layer
-                edge = jnp.broadcast_to(value[:, at : at + 1], value.shape)
-                spread.append(jnp.where(lane < 64, main, edge))
-            totals.append(
-                spread[0] * pairs[0, pl.ds(row, LANES), :] + spread[1] * pairs[1, pl.ds(row, LANES), :]
-            )
-        real, imag = totals
-        real, imag = jnp.where(turned, -imag, real), jnp.where(turned, real, imag)
-        work[k] = column_product((high_i, low_i), k, jnp.concatenate([real, imag], axis=0))
+    turned = (lane <= 32) | (lane == 97)
+    for group in range(GROUPS):
+        for copy in later[group]:
+            copy.wait()
+        for k in in_group(group):
+            spectrum = table_product(held_table, k, work[k])
+            held_model[k] = spectrum
+            row = slice(k * LANES, (k + 1) * LANES)
+            both = dot(jnp.concatenate(split(spectrum), axis=1), spread[...])
+            totals = [
+                both[part * LANES : (part + 1) * LANES, :LANES] * held_pairs[0, row, :]
+                + both[part * LANES : (part + 1) * LANES, LANES:] * held_pairs[1, row, :]
+                for part in range(2)
+            ]
+            work[k, :LANES], work[k, LANES:] = turn_phase(turned, *totals, 1)
+    leaving = started((held_model, model, left.at[1]))
+    for group in range(GROUPS):
+        last[group].wait()
+        for k in in_group(group):
+            work[k] = table_product(held_table_i, k, work[k])
 
     lane8 = lane_of((8, LANES))
+    main = lane8 % 64 < 32
+    packed = jnp.logical_and(lane8 % 64 == 32, first)
 
     def store(a, row, real, imag):
-        imag = jnp.where(jnp.logical_and(lane8 % 32 == 0, first), turn(real, 64), imag)
-        out[pl.ds(a * LANES + row, 8), :] = jnp.where(lane8 < 64, real, turn(imag, 64))
-        edges[pl.ds(a * LANES + row, 8), :] = real
+        chunk[pl.ds(a * LANES + row, 8), :] = jnp.where(
+            jnp.logical_or(main, packed), real, turn(imag, 32)
+        )
+        held_edges[pl.ds(a * LANES + row, 8), :] = real
 
     inverse_blocks(work, store)
-
-
-def forward_columns_b(flags, moved, pairs, tables, inverse_tables, n):
+    leaving += started((chunk, out, left.at[0]), (held_edges, edges, left.at[2]))
+    for copy in leaving:
+        copy.wait()
+
+
+def forward_columns_b(flags, moved, pairs, table, table_i, n):
+    hbm = pl.BlockSpec(memory_space=pltpu.HBM)
     return pl.pallas_call(
         forward_kernel_b,
         out_shape=[
-            jax.ShapeDtypeStruct((n, LANES), f32),
-            jax.ShapeDtypeStruct((n, LANES), f32),
-            jax.ShapeDtypeStruct((2, 2, n, LANES), f32),
-        ],
-        in_specs=[pl.BlockSpec(memory_space=pltpu.SMEM)] + [pl.BlockSpec(memory_space=pltpu.VMEM)] * 6,
+            pltpu.HBM((n, LANES), f32),
+            pltpu.HBM((n, LANES), f32),
+            pltpu.HBM((RADIX, 2 * LANES, LANES), f32),
+        ],
+        in_specs=[
+            pl.BlockSpec(memory_space=pltpu.SMEM),
+            hbm,
+            pl.BlockSpec(memory_space=pltpu.VMEM),
+            hbm,
+            hbm,
+            hbm,
+        ],
+        out_specs=[hbm, hbm, hbm],
         scratch_shapes=[
-            pltpu.VMEM((RADIX, 2 * LANES, LANES), f32),
-            pltpu.VMEM((2, n, LANES), f32),
-        ],
-        compiler_params=pltpu.CompilerParams(vmem_limit_bytes=40 << 20),
+            WORK,
+            pltpu.VMEM(moved.shape, f32),
+            pairs_like(n),
+            TABLE,
+            TABLE,
+            pairs_like(n),
+            pltpu.VMEM((n, LANES), f32),
+            WORK,
+            pltpu.VMEM((n, LANES), f32),
+            pltpu.SemaphoreType.DMA((1,)),
+            SIGNALS,
+            SIGNALS,
+            SIGNALS,
+            pltpu.SemaphoreType.DMA((3,)),
+        ],
+        compiler_params=pltpu.CompilerParams(vmem_limit_bytes=34 << 20),
+        cost_estimate=pl.CostEstimate(flops=0, bytes_accessed=20_000_000, transcendentals=0),
         name="forward_columns_b",
-    )(flags, moved, pairs, *tables, *inverse_tables)
-
-
-def forward_kernel_a(flags, model, edges, pairs, high_i, low_i, out, work):
+    )(flags, in_hbm(moved), jnp.asarray(lane_tables()[1]), in_hbm(pairs), in_hbm(table), in_hbm(table_i))
+
+
+def forward_kernel_a(
+    flags, model, edges, pairs, table_i, out,
+    work, held_model, held_edges, held_pairs, held_table_i, chunk, got, got_pairs, got_table_i, left,
+):
     first = flags[1] == 1
+    later = [
+        started(
+            (model.at[group_steps(g)], held_model.at[group_steps(g)], got.at[g]),
+            pair_copies(pairs, 0, held_pairs, got_pairs, g),
+            table_copies(table_i, held_table_i, got_table_i, g),
+        )
+        for g in range(GROUPS)
+    ]
+    edges_read = started((edges, held_edges, left.at[1]))
     lane = lane_of((LANES, LANES))
     turned = lane // 32 == 2
 
-    @pl.loop(0, RADIX)
-    def _(k):
-        row = pl.multiple_of(k * LANES, LANES)
-        real, imag = (
-            model[0, part, pl.ds(row, LANES), :] * pairs[0, pl.ds(row, LANES), :]
-            + model[1, part, pl.ds(row, LANES), :] * pairs[1, pl.ds(row, LANES), :]
-            for part in range(2)
-        )
-        real, imag = jnp.where(turned, -imag, real), jnp.where(turned, real, imag)
-        work[k] = column_product((high_i, low_i), k, jnp.concatenate([real, imag], axis=0))
+    def spread(value):
+        swapped = turn(value, 64)
+        both = (jnp.where(lane < 64, value, swapped), jnp.where(lane < 64, swapped, value))
+        return [jnp.where(lane % 64 < 32, layer, turn(layer, 32)) for layer in both]
+
+    for group in range(GROUPS):
+        for copy in later[group]:
+            copy.wait()
+        for k in in_group(group):
+            row = slice(k * LANES, (k + 1) * LANES)
+            totals = []
+            for part in range(2):
+                layers = spread(held_model[k, part * LANES : (part + 1) * LANES, :])
+                totals.append(layers[0] * held_pairs[0, row, :] + layers[1] * held_pairs[1, row, :])
+            real, imag = turn_phase(turned, *totals, 1)
+            work[k] = table_product(held_table_i, k, jnp.concatenate([real, imag], axis=0))
 
     lane8 = lane_of((8, LANES))
     packed = jnp.logical_and(lane8 % 32 == 0, first)
 
     def store(a, row, real, imag):
-        edge = edges[pl.ds(a * LANES + row, 8), :]
-        edge = jnp.where(lane8 < 64, turn(edge, 63), turn(edge, 126))
-        out[pl.ds(a * LANES + row, 8), :LANES] = real
-        out[pl.ds(a * LANES + row, 8), LANES:] = jnp.where(packed, edge, imag)
-
+        edge = held_edges[pl.ds(a * LANES + row, 8), :]
+        edge = jnp.where(lane8 % 64 < 32, turn(edge, 95), turn(edge, 126))
+        chunk[pl.ds(a * LANES + row, 8), :LANES] = real
+        chunk[pl.ds(a * LANES + row, 8), LANES:] = jnp.where(packed, edge, imag)
+
+    edges_read[0].wait()
     inverse_blocks(work, store)
-
-
-def forward_columns_a(flags, model, edges, pairs, inverse_tables):
+    for copy in started((chunk, out, left.at[0])):
+        copy.wait()
+
+
+def forward_columns_a(flags, model, edges, pairs, table_i):
     n = edges.shape[0]
+    hbm = pl.BlockSpec(memory_space=pltpu.HBM)
     return pl.pallas_call(
         forward_kernel_a,
-        out_shape=jax.ShapeDtypeStruct((n, 2 * LANES), f32),
-        in_specs=[pl.BlockSpec(memory_space=pltpu.SMEM)] + [pl.BlockSpec(memory_space=pltpu.VMEM)] * 5,
-        scratch_shapes=[pltpu.VMEM((RADIX, 2 * LANES, LANES), f32)],
-        compiler_params=pltpu.CompilerParams(vmem_limit_bytes=32 << 20),
+        out_shape=pltpu.HBM((n, 2 * LANES), f32),
+        in_specs=[pl.BlockSpec(memory_space=pltpu.SMEM), hbm, hbm, hbm, hbm],
+        out_specs=hbm,
+        scratch_shapes=[
+            WORK,
+            WORK,
+            pltpu.VMEM((n, LANES), f32),
+            pairs_like(n),
+            TABLE,
+            pltpu.VMEM((n, 2 * LANES), f32),
+            SIGNALS,
+            SIGNALS,
+            SIGNALS,
+            pltpu.SemaphoreType.DMA((2,)),
+        ],
+        compiler_params=pltpu.CompilerParams(vmem_limit_bytes=26 << 20),
+        cost_estimate=pl.CostEstimate(flops=0, bytes_accessed=16_000_000, transcendentals=0),
         name="forward_columns_a",
-    )(flags, model, edges, pairs, *inverse_tables)
-
-
-def block_row(block, rows):
-    return (block % RADIX) * rows + block // RADIX
-
-
-def gradient_kernel(counts, listing, spectra, high, low, gradient, outgoing, sums, blocks, compact):
+    )(flags, in_hbm(model), in_hbm(edges), in_hbm(pairs), in_hbm(table_i))
+
+
+def gradient_kernel(
+    counts, listing, spectra, table, gradient, outgoing, sums, held, arrived, blocks, compact
+):
     rows, n = gradient.shape
     parts = quad_transpose([spectra[index] for index in range(4)])
     lhs = jnp.concatenate(
-        [jnp.concatenate([parts[0], parts[1]], axis=0), jnp.concatenate([parts[2], parts[3]], axis=0)],
+        [jnp.concatenate([parts[0], parts[2]], axis=0), jnp.concatenate([parts[1], parts[3]], axis=0)],
         axis=1,
     )
-    inverse_step(lhs, high, low, sums)
+    inverse_step(lhs, table, sums, held, arrived)
 
     @pl.when(pl.program_id(0) == pl.num_programs(0) - 1)
     def _():
@@ -875,7 +1059,7 @@
         def _(step):
             for index in range(8):
                 at = step * 8 + index
-                compact[pl.ds(at, 1), :] = blocks[pl.ds(block_row(listing[at], rows), 1), :]
+                compact[pl.ds(at, 1), :] = blocks[pl.ds(listing[at], 1), :]
 
         offset = 0
         for o in range(owners):
@@ -883,11 +1067,10 @@
             offset = offset + counts[o]
 
 
-def gradient_rows(counts, listing, spectra, tables, rows, n, cap):
+def gradient_rows(counts, listing, spectra, table, rows, n, cap):
     devices = spectra.shape[0]
     owners = counts.shape[0]
     smem = pl.BlockSpec(memory_space=pltpu.SMEM)
-    table = pl.BlockSpec((1, 2 * LANES, n // 2), lambda s: (s, 0, 0))
     block_count = listing.shape[0]
     return pl.pallas_call(
         gradient_kernel,
@@ -900,56 +1083,78 @@
             smem,
             smem,
             pl.BlockSpec((4, rows // 2, LANES), lambda s: (s, 0, 0)),
-            table,
-            table,
+            pl.BlockSpec(memory_space=pltpu.HBM),
         ],
         out_specs=[
             pl.BlockSpec((rows, n), lambda s: (0, 0)),
             pl.BlockSpec((owners, cap, LANES), lambda s: (0, 0, 0)),
         ],
-        scratch_shapes=[
-            pltpu.VMEM((2, rows, n // 2), f32),
+        scratch_shapes=inverse_scratch(rows, n, devices // 4)
+        + [
             pltpu.VMEM((block_count, LANES), f32),
             pltpu.VMEM((block_count + cap, LANES), f32),
         ],
-        compiler_params=pltpu.CompilerParams(vmem_limit_bytes=32 << 20),
+        compiler_params=pltpu.CompilerParams(vmem_limit_bytes=26 << 20),
         name="gradient_rows",
-    )(counts, listing, spectra, *tables)
-
-
-def owner_kernel(counts, incoming, current, weights, model_new, updated, room, scales):
+    )(counts, listing, spectra, in_hbm(table))
+
+
+def owner_segments(counts, incoming, current, weights, room, scales, keep):
     sources, cap, _ = incoming.shape
     length = current.shape[0]
     room[:length, :] = current[...]
     room[length:, :] = jnp.zeros_like(room[length:, :])
     scales[:length, :] = weights[...].astype(f32) * step_size
     scales[length:, :] = jnp.zeros_like(scales[length:, :])
-    row = lax.broadcasted_iota(jnp.int32, (cap, LANES), 0)
     begin = 0
     for p in range(sources):
-        count = counts[p]
         before = room[pl.ds(begin, cap), :]
         after = jnp.clip(before - scales[pl.ds(begin, cap), :] * incoming[p], -1.0, 1.0)
+        keep(p, begin, before, after)
+        begin = begin + counts[p]
+
+
+def owner_send_kernel(counts, incoming, current, weights, updated, room, scales):
+    def keep(p, begin, before, after):
         updated[p] = after
-        room[pl.ds(begin, cap), :] = jnp.where(row < count, after, before)
-        begin = begin + count
-    model_new[...] = room[:length, :]
-
-
-def owner_update(counts, incoming, current, weights):
+
+    owner_segments(counts, incoming, current, weights, room, scales, keep)
+
+
+def owner_keep_kernel(counts, incoming, current, weights, model_new, room, scales):
+    row = lax.broadcasted_iota(jnp.int32, incoming.shape[1:], 0)
+
+    def keep(p, begin, before, after):
+        room[pl.ds(begin, before.shape[0]), :] = jnp.where(row < counts[p], after, before)
+
+    owner_segments(counts, incoming, current, weights, room, scales, keep)
+    model_new[...] = room[: current.shape[0], :]
+
+
+def owner_call(kernel, name, shape, counts, incoming, current, weights):
     sources, cap, _ = incoming.shape
     length = current.shape[0]
     return pl.pallas_call(
-        owner_kernel,
-        out_shape=[
-            jax.ShapeDtypeStruct((length, LANES), f32),
-            jax.ShapeDtypeStruct((sources, cap, LANES), f32),
-        ],
+        kernel,
+        out_shape=jax.ShapeDtypeStruct(shape, f32),
         in_specs=[pl.BlockSpec(memory_space=pltpu.SMEM)] + [pl.BlockSpec(memory_space=pltpu.VMEM)] * 3,
         scratch_shapes=[pltpu.VMEM((length + cap, LANES), f32)] * 2,
-        compiler_params=pltpu.CompilerParams(vmem_limit_bytes=24 << 20),
-        name="owner_update",
+        compiler_params=pltpu.CompilerParams(vmem_limit_bytes=16 << 20),
+        name=name,
     )(counts, incoming, current, weights)
+
+
+def copy_kernel(source, target):
+    target[...] = source[...]
+
+
+def copied(value):
+    return pl.pallas_call(
+        copy_kernel,
+        out_shape=jax.ShapeDtypeStruct(value.shape, value.dtype),
+        compiler_params=pltpu.CompilerParams(vmem_limit_bytes=8 << 20),
+        name="copied",
+    )(value)
 
 
 def model_rows_kernel(counts, listing, returned, high, low, out, compact, grid, halves_high, halves_low):
@@ -970,11 +1175,11 @@
         def _(step):
             for index in range(8):
                 at = step * 8 + index
-                grid[pl.ds(block_row(listing[at], rows), 1), :] = compact[pl.ds(at, 1), :]
+                grid[pl.ds(listing[at], 1), :] = compact[pl.ds(at, 1), :]
 
         @pl.loop(lax.div(total, 8) * 8, total)
         def _(at):
-            grid[pl.ds(block_row(listing[at], rows), 1), :] = compact[pl.ds(at, 1), :]
+            grid[pl.ds(listing[at], 1), :] = compact[pl.ds(at, 1), :]
 
         half = RADIX // 2
         for q in range(half):
@@ -989,7 +1194,7 @@
     result = dot3((halves_high[side], halves_low[side]), (high[0], low[0]))
     half = rows // 2
     parts = quad_transpose(
-        [result[:half, :LANES], result[half:, :LANES], result[:half, LANES:], result[half:, LANES:]]
+        [result[:half, :LANES], result[:half, LANES:], result[half:, :LANES], result[half:, LANES:]]
     )
     for index in range(4):
         out[index] = parts[index]
@@ -1018,9 +1223,13 @@
             pltpu.VMEM((2, rows, n // 2), bf16),
             pltpu.VMEM((2, rows, n // 2), bf16),
         ],
-        compiler_params=pltpu.CompilerParams(vmem_limit_bytes=32 << 20),
+        compiler_params=pltpu.CompilerParams(vmem_limit_bytes=16 << 20),
         name="model_rows",
     )(counts, listing, returned, *tables)
+
+
+def in_hbm(value):
+    return pltpu.with_memory_space_constraint(value, pltpu.HBM)
 
 
 def swap_all(value, axes):
@@ -1034,48 +1243,63 @@
     channels, rows, n = misfit.shape
     band = n // pen_count
     forward_np, inverse_np = row_tables(n, devices)
-    row_forward, row_inverse = tuple(map(jnp.asarray, forward_np)), tuple(map(jnp.asarray, inverse_np))
+    row_forward = tuple(map(jnp.asarray, forward_np))
+    row_inverse = jnp.asarray(np.stack(inverse_np, axis=1))
     forward_np, inverse_np = column_tables()
-    col_forward, col_inverse = tuple(map(jnp.asarray, forward_np)), tuple(map(jnp.asarray, inverse_np))
+    col_forward = jnp.asarray(np.stack(forward_np, axis=1))
+    col_inverse = jnp.asarray(np.stack(inverse_np, axis=1))
     me = lax.axis_index(both)
     half = devices // 2
     flags = jnp.stack([(me >= half).astype(jnp.int32), (me == 0).astype(jnp.int32)])
     counts = send_counts.reshape(pen_count)
     listing = active_list.reshape(-1)
+    places = (listing & (RADIX - 1)) * band + (listing >> 4)
     owner_length = model_vec.shape[2]
     cap = owner_length // pen_count
 
     spec = kernel_spec.reshape((-1,) + kernel_spec.shape[2:])
-    sent, kept = part_spec(flags, spec)
-    got = lax.ppermute(sent, both, [(d, devices - 1 - d) for d in range(devices)])
+    partner = [(d, devices - 1 - d) for d in range(devices)]
+    got_b = lax.ppermute(part_spec(flags, spec, 8, 12), both, partner)
+    sent_a = part_spec(flags, spec, 0, 8)
+    got_a = lax.ppermute(sent_a, both, partner)
     edge = lax.ppermute(
         spec[:, 0:1, :].astype(f32), both, [(d, (devices - d) % half) for d in range(half, devices)]
     )
     source_counts = swap_all(counts, "pen")
 
+    misfit, _ = lax.optimization_barrier((misfit, sent_a))
     chunk_a, chunk_b = misfit_rows(misfit, row_forward, devices)
+    chunk_a, got_b, edge, source_counts = lax.optimization_barrier((chunk_a, got_b, edge, source_counts))
+    chunk_b, got_a, got_b, edge = lax.optimization_barrier((chunk_b, got_a, got_b, edge))
     columns_a = swap_all(chunk_a, both).reshape(n, 2 * LANES)
     columns_b = swap_all(chunk_b, both).reshape(n, LANES)
-    pairs_a, pairs_b = pair_spec(flags, kept, got, edge)
-    sums, edges = adjoint_columns_a(flags, columns_a, pairs_a, col_forward)
-    fields = adjoint_columns_b(flags, columns_b, edges, sums, pairs_b, col_forward, col_inverse)
+    pairs = pair_spec(flags, spec, got_a, got_b, edge)
+    sums, edges = adjoint_columns_a(flags, columns_a, pairs, col_forward)
+    fields = adjoint_columns_b(flags, columns_b, edges, sums, pairs, col_forward, col_inverse)
     gradient, outgoing = gradient_rows(
-        counts, listing, swap_all(fields, both), row_inverse, band, n, cap
+        counts, places, swap_all(fields, both), row_inverse, band, n, cap
     )
     incoming = swap_all(outgoing, "pen")
-    model_new, updated = owner_update(
+    owned = (
         source_counts,
         incoming,
         model_vec.reshape(owner_length, LANES),
         weight_vec.reshape(owner_length, LANES),
     )
+    updated = owner_call(owner_send_kernel, "owner_send", incoming.shape, *owned)
+    updated, incoming = lax.optimization_barrier((updated, incoming))
     returned = swap_all(updated, "pen")
-    model_chunks = model_rows(counts, listing, returned, row_forward, band, n, devices)
+    model_new = owner_call(
+        owner_keep_kernel, "owner_keep", (owner_length, LANES), owned[0], incoming, *owned[2:]
+    )
+    model_chunks = model_rows(counts, places, returned, row_forward, band, n, devices)
+    model_chunks, gradient = lax.optimization_barrier((model_chunks, gradient))
+    gradient = copied(gradient)
     out_b, edges, model = forward_columns_b(
-        flags, swap_all(model_chunks, both), pairs_b, col_forward, col_inverse, n
+        flags, swap_all(model_chunks, both), pairs, col_forward, col_inverse, n
     )
     back_b = swap_all(out_b.reshape(devices, rows, LANES), both)
-    out_a = forward_columns_a(flags, model, edges, pairs_a, col_inverse)
+    out_a = forward_columns_a(flags, model, edges, pairs, col_inverse)
     back_a = swap_all(out_a.reshape(devices, rows, 2 * LANES), both)
     predicted = predicted_rows(back_b, row_inverse, None, n)
     predicted = predicted_rows(back_a, row_inverse, predicted, n)

time: 629 us -> 520 us (0.83)
  waiting for transfers between devices: 297 us -> 195 us
  starting transfers between devices: 37.1 us -> 82.4 us
  local copies, waits for them, and re-layouts: 50.5 us -> 8.95 us
  Pallas kernels: 149 us -> 114 us
  blocking collectives: 89.8 us -> 115 us
    all_to_all x7 -> x6, waiting for transfers between devices: 209 us -> 115 us  [swap_all(): return lax.all_to_all(value, axes, split_axis=0, concat_axis=0, tiled=True)]
    ppermute x1, waiting for transfers between devices: 88.4 us -> 0.01 us  [local_paired(): lax.ppermute(spec[:, 0:1, :].astype(f32), both, [(d, (devices - d) % half...]
    ppermute x1 -> x2, waiting for transfers between devices: 0.01 us -> 79.8 us  [the longest x1 79.8 us: local_paired(): got_a = lax.ppermute(sent_a, both, partner)]
    unnamed x90 -> x36, local copies, waits for them, and re-layouts: 49.8 us -> 8.27 us
    all_to_all x7 -> x6, starting transfers between devices: 30.6 us -> 69.5 us  [swap_all(): return lax.all_to_all(value, axes, split_axis=0, concat_axis=0, tiled=True)]
    pallas_call x6 -> x9, Pallas kernels: 90.3 us -> 60.8 us  [the longest x1 15.1 us: adjoint_columns_b(): pl.pallas_call(adjoint_kernel_b, out_shape=pltpu.HBM(chunks, f32), in_spe...]
    all_to_all x2 -> x3, blocking collectives: 89.8 us -> 115 us  [swap_all(): return lax.all_to_all(value, axes, split_axis=0, concat_axis=0, tiled=True)]
    pallas_call x2, Pallas kernels: 13.5 us -> 20.7 us  [predicted_rows(): pl.pallas_call(predicted_kernel_b if before is None else predicted_kernel...]
  transfers between devices with their start and end apart: 9 -> 9, of which waited for: 6 -> 7; matrix products, arithmetic and copies ran while one was open for 0% -> 0% of each run, Pallas kernels for 12% -> 10%
where the time goes in v2:
time: 520 us; the launch traced here: 518 us
  waiting for transfers between devices  195 us (38%)
  blocking collectives  115 us (22%)
  Pallas kernels  114 us (22%)
  starting transfers between devices  82.4 us (16%)
  local copies, waits for them, and re-layouts  8.95 us (2%)
    all_to_all x6, waiting for transfers between devices, swap_all(): return lax.all_to_all(value, axes, split_axis=0, concat_axis=0, tiled=True)  115 us
    all_to_all x3, blocking collectives, swap_all(): return lax.all_to_all(value, axes, split_axis=0, concat_axis=0, tiled=True)  115 us
    ppermute x1, waiting for transfers between devices, local_paired(): got_a = lax.ppermute(sent_a, both, partner)  79.8 us
    all_to_all x6, starting transfers between devices, swap_all(): return lax.all_to_all(value, axes, split_axis=0, concat_axis=0, tiled=True)  69.5 us
    pallas_call x2, Pallas kernels, predicted_rows(): pl.pallas_call(predicted_kernel_b if before is None else predicted_kernel...  20.7 us
    pallas_call x1, Pallas kernels, adjoint_columns_b(): pl.pallas_call(adjoint_kernel_b, out_shape=pltpu.HBM(chunks, f32), in_spe...  15.1 us
    pallas_call x1, Pallas kernels, forward_columns_b(): pl.pallas_call(forward_kernel_b, out_shape=[pltpu.HBM((n, LANES), f32), p...  15.1 us
    pallas_call x1, Pallas kernels, pair_spec(): pl.pallas_call(pair_kernel, grid=(4,), out_shape=pltpu.HBM((4, n, LANES),...  10.5 us
  transfers between devices with their start and end apart: 9, of which 7 were waited for; matrix products, arithmetic and copies ran while one was open for 0% of the time, Pallas kernels for 10%

profile of v2, /device:TPU:0, one launch (start us, length us, event | category | flops | bytes accessed | tf_op | source)
XLA Modules:
  0.0 518.4 jit_solution(16189603304229383236)
XLA Ops:
  0.6 0.7 add_convert_fusion.flags
  1.3 2.3 part_spec.3
  3.6 6.4 %collective-permute-start = (f32[4,32,2048]{2,1,0:T(8,128)}, f32[4,32,2048]{2,1,0:T(8,128)}, u32[]{:S(2)}, u32[]{:S(2)}) collective-permute-start(f32[4,32,2048]{2,1,0:T(8,128)} %part_spec.3), channel_id=1, source_target_pairs={{0,31},{1,30},{2,29},{3,28},{4,27},{5,26},{6,25},{7,24},{8,23},{9,... | collective-permute-start | bytes 3145736 | tf_op jit(solution)/shard_map/ppermute | solution.py:1262
  10.0 1.0 slice_convert_fusion
  11.0 1.3 collective-permute-start.1
  12.3 0.7 copy.18
  13.0 6.7 %all-to-all-start = ((s32[16,1,1]{2,1,0:T(1,128)}), s32[16,1,1]{2,1,0:T(1,128)S(1)}, u32[]{:S(2)}, u32[]{:S(2)}) async-start(s32[16,1,1]{2,1,0:T(1,128)} %copy.18), calls=%async_computation | async-start | bytes 16384 | tf_op jit(solution)/shard_map/all_to_all | solution.py:1236
  19.8 4.3 part_spec.2
  24.1 2.2 copy-done
  26.3 2.2 copy-done.2
  28.5 9.0 %misfit_rows.1 = (f32[32,64,256]{2,1,0:T(8,128)S(1)}, f32[32,64,128]{2,1,0:T(8,128)}) custom-call(f32[6,64,2048]{2,1,0:T(8,128)S(1)} %copy-done.5, bf16[8,1024,256]{2,1,0:T(8,128)(2,1)S(1)} %copy-done.2, bf16[8,1024,256]{2,1,0:T(8,128)(2,1)S(1)} %copy-done), custom_call_target="tpu_custom_call" | custom-call | tf_op jit(solution)/shard_map/misfit_rows/pallas_call | solution.py:532
  37.4 1.3 copy-done.8
  38.8 21.7 %all-to-all-done = s32[16,1,1]{2,1,0:T(1,128)S(1)} async-done(((s32[16,1,1]{2,1,0:T(1,128)}), s32[16,1,1]{2,1,0:T(1,128)S(1)}, u32[]{:S(2)}, u32[]{:S(2)}) %all-to-all-start) | async-done | bytes 96 | tf_op jit(solution)/shard_map/all_to_all | solution.py:1236
  60.5 0.4 reduce.counts
  60.9 2.7 all-to-all-start.2
  63.6 5.3 %collective-permute-start.2 = (f32[8,32,2048]{2,1,0:T(8,128)}, f32[8,32,2048]{2,1,0:T(8,128)S(1)}, u32[]{:S(2)}, u32[]{:S(2)}) collective-permute-start(f32[8,32,2048]{2,1,0:T(8,128)} %part_spec.2), channel_id=1, source_target_pairs={{0,31},{1,30},{2,29},{3,28},{4,27},{5,26},{6,25},{7,24},{8,23},{9,... | collective-permute-start | bytes 6291464 | tf_op jit(solution)/shard_map/ppermute | solution.py:1264
  68.9 79.8 %collective-permute-done.2.got_a = f32[8,32,2048]{2,1,0:T(8,128)S(1)} collective-permute-done((f32[8,32,2048]{2,1,0:T(8,128)}, f32[8,32,2048]{2,1,0:T(8,128)S(1)}, u32[]{:S(2)}, u32[]{:S(2)}) %collective-permute-start.2) | collective-permute-done | bytes 2097184 | tf_op jit(solution)/shard_map/ppermute | solution.py:1264
  148.7 1.4 copy-done.16
  150.1 7.7 %all-to-all-done.2 = f32[32,64,256]{2,1,0:T(8,128)S(1)} async-done(((f32[32,64,256]{2,1,0:T(8,128)}), f32[32,64,256]{2,1,0:T(8,128)S(1)}, u32[]{:S(2)}, u32[]{:S(2)}) %all-to-all-start.2) | async-done | bytes 2097184 | tf_op jit(solution)/shard_map/all_to_all | solution.py:1236
  157.7 48.9 %all-to-all-start.1 = ((f32[32,64,128]{2,1,0:T(8,128)}), f32[32,64,128]{2,1,0:T(8,128)}, u32[]{:S(2)}, u32[]{:S(2)}) async-start(f32[32,64,128]{2,1,0:T(8,128)} %get-tuple-element.31), calls=%async_computation.1 | async-start | bytes 2097152 | tf_op jit(solution)/shard_map/all_to_all | solution.py:1236
  206.7 10.5 %pair_spec.1.pairs = f32[4,2048,128]{2,1,0:T(8,128)} custom-call(s32[2]{0:T(128)S(1)} %copy-done.13, bf16[12,64,2048]{2,1,0:T(8,128)(2,1)} %bitcast.26, f32[8,32,2048]{2,1,0:T(8,128)} %copy-done.16, f32[4,32,2048]{2,1,0:T(8,128)} %collective-permute-done.got_b, f32[12,1,2048]{2,1,0:T(1,128)S(1)} %collective-permute-done.1.edge), custom_call_target="tpu_custom_call" | custom-call | bytes 60000000 | tf_op jit(solution)/shard_map/pair_spec/pallas_call | solution.py:481
  217.1 8.1 %adjoint_columns_a.1 = (f32[2,2048,128]{2,1,0:T(8,128)S(1)}, f32[2048,128]{1,0:T(8,128)S(1)}) custom-call(s32[2]{0:T(128)S(1)} %copy-done.13, f32[2048,256]{1,0:T(8,128)} %bitcast.27, f32[4,2048,128]{2,1,0:T(8,128)} %pair_spec.1.pairs, bf16[16,2,256,256]{3,2,1,0:T(8,128)(2,1)} %constant.37.clone.table), custom_call_target="tpu_custom_call" | custom-call | bytes 20000000 | tf_op jit(solution)/shard_map/adjoint_columns_a/pallas_call | solution.py:727
  225.3 7.4 %all-to-all-done.1 = f32[32,64,128]{2,1,0:T(8,128)} async-done(((f32[32,64,128]{2,1,0:T(8,128)}), f32[32,64,128]{2,1,0:T(8,128)}, u32[]{:S(2)}, u32[]{:S(2)}) %all-to-all-start.1) | async-done | bytes 1048608 | tf_op jit(solution)/shard_map/all_to_all | solution.py:1236
  232.7 15.1 %adjoint_columns_b.1 = f32[32,64,128]{2,1,0:T(8,128)} custom-call(s32[2]{0:T(128)S(1)} %copy-done.13, f32[2048,128]{1,0:T(8,128)} %bitcast.6.spectra, f32[2048,128]{1,0:T(8,128)S(1)} %get-tuple-element.36.edges, f32[2,2048,128]{2,1,0:T(8,128)S(1)} %get-tuple-element.37.sums, bf16[512,128]{1,0:T(8,128)(2,1)S(1)} %copy-done.12, ...), custom_call_target="tpu_custom_call" | custom-call | bytes 20000000 | tf_op jit(solution)/shard_map/adjoint_columns_b/pallas_call | solution.py:823
  247.9 0.0 copy-start.17
  247.9 3.6 all-to-all-start.3
  251.5 26.2 %all-to-all-done.3.spectra = f32[32,64,128]{2,1,0:T(8,128)S(1)} async-done(((f32[32,64,128]{2,1,0:T(8,128)}), f32[32,64,128]{2,1,0:T(8,128)S(1)}, u32[]{:S(2)}, u32[]{:S(2)}) %all-to-all-start.3) | async-done | bytes 1048608 | tf_op jit(solution)/shard_map/all_to_all | solution.py:1236
  277.7 8.7 %gradient_rows.1 = (f32[128,2048]{1,0:T(8,128)S(1)}, f32[16,192,128]{2,1,0:T(8,128)S(1)}) custom-call(s32[16]{0:T(128)S(1)} %bitcast.21, s32[2048]{0:T(1024)S(1)} %bitcast.18, f32[32,64,128]{2,1,0:T(8,128)S(1)} %all-to-all-done.3.spectra, bf16[8,2,256,1024]{3,2,1,0:T(8,128)(2,1)} %constant.36.clone.table), custom_call_target="tpu_custom_call" | custom-call | tf_op jit(solution)/shard_map/gradient_rows/pallas_call | solution.py:1075
  286.4 0.0 copy-start.9
  286.4 39.9 %all_to_all.52.incoming = f32[16,192,128]{2,1,0:T(8,128)S(1)} all-to-all(f32[16,192,128]{2,1,0:T(8,128)S(1)} %get-tuple-element.38), channel_id=1, replica_groups=mesh['grp'=1,'pen'=16,'dep'=2,'chan'=1] {'pen'}, dimensions={0} | all-to-all | bytes 3145728 | tf_op jit(solution)/shard_map/all_to_all | solution.py:1236
  326.3 0.0 copy-start.1
  326.3 0.0 copy-start.3
  326.4 1.0 owner_send.1
  327.4 41.2 %all_to_all.53.returned = f32[16,192,128]{2,1,0:T(8,128)S(1)} all-to-all(f32[16,192,128]{2,1,0:T(8,128)S(1)} %owner_send.1), channel_id=1, replica_groups=mesh['grp'=1,'pen'=16,'dep'=2,'chan'=1] {'pen'}, dimensions={0} | all-to-all | bytes 3145728 | tf_op jit(solution)/shard_map/all_to_all | solution.py:1236
  368.6 7.0 %model_rows.1 = f32[32,64,128]{2,1,0:T(8,128)S(1)} custom-call(s32[16]{0:T(128)S(1)} %bitcast.22, s32[2048]{0:T(1024)S(1)} %bitcast.19, f32[16,192,128]{2,1,0:T(8,128)S(1)} %all_to_all.53.returned, bf16[8,1024,256]{2,1,0:T(8,128)(2,1)S(1)} %copy-done.3, bf16[8,1024,256]{2,1,0:T(8,128)(2,1)S(1)} %copy-done.1), custom_call_target="tpu_custom_call" | custom-call | tf_op jit(solution)/shard_map/model_rows/pallas_call | solution.py:1208
  375.6 0.0 copy-start.11
  375.6 33.6 %all_to_all.54.moved = f32[32,64,128]{2,1,0:T(8,128)} all-to-all(f32[32,64,128]{2,1,0:T(8,128)S(1)} %model_rows.1), channel_id=1, replica_groups=mesh['grp'=1,'pen'=16,'dep'=2,'chan'=1] {'pen','dep'}, dimensions={0} | all-to-all | bytes 2097152 | tf_op jit(solution)/shard_map/all_to_all | solution.py:1236
  409.2 15.1 %forward_columns_b.1 = (f32[2048,128]{1,0:T(8,128)}, f32[2048,128]{1,0:T(8,128)}, f32[16,256,128]{2,1,0:T(8,128)}) custom-call(s32[2]{0:T(128)S(1)} %copy-done.13, f32[32,64,128]{2,1,0:T(8,128)} %all_to_all.54.moved, bf16[256,256]{1,0:T(8,128)(2,1)S(1)} %copy-done.11, f32[4,2048,128]{2,1,0:T(8,128)} %pair_spec.1.pairs, ...), custom_call_target="tpu_custom_call" | custom-call | bytes 20000000 | tf_op jit(solution)/shard_map/forward_columns_b/pallas_call | solution.py:924
  424.3 3.8 all-to-all-start.8
  428.0 8.9 %forward_columns_a.1 = f32[2048,256]{1,0:T(8,128)} custom-call(s32[2]{0:T(128)S(1)} %copy-done.13, f32[16,256,128]{2,1,0:T(8,128)} %get-tuple-element.44.model, f32[2048,128]{1,0:T(8,128)} %get-tuple-element.45.edges, f32[4,2048,128]{2,1,0:T(8,128)} %pair_spec.1.pairs, bf16[16,2,256,256]{3,2,1,0:T(8,128)(2,1)} %constant.38.clone.table_i), custom_call_target="tpu_custom_call" | custom-call | bytes 16000000 | tf_op jit(solution)/shard_map/forward_columns_a/pallas_call | solution.py:1014
  436.9 17.4 %all-to-all-done.8.spectra = f32[32,64,128]{2,1,0:T(8,128)} async-done(((f32[32,64,128]{2,1,0:T(8,128)}), f32[32,64,128]{2,1,0:T(8,128)}, u32[]{:S(2)}, u32[]{:S(2)}) %all-to-all-start.8) | async-done | bytes 1048608 | tf_op jit(solution)/shard_map/all_to_all | solution.py:1236
  454.3 3.7 all-to-all-start.7
  458.0 1.1 copy-done.7
  459.2 2.5 owner_keep.1
  461.7 1.0 copied.1
  462.7 9.3 %predicted_rows_b.1.before = f32[6,64,2048]{2,1,0:T(8,128)} custom-call(f32[32,64,128]{2,1,0:T(8,128)} %all-to-all-done.8.spectra, bf16[8,2,256,1024]{3,2,1,0:T(8,128)(2,1)} %constant.36.clone.table), custom_call_target="tpu_custom_call" | custom-call | tf_op jit(solution)/shard_map/predicted_rows_b/pallas_call | solution.py:624
  472.0 34.7 %all-to-all-done.7.spectra = f32[32,64,256]{2,1,0:T(8,128)} async-done(((f32[32,64,256]{2,1,0:T(8,128)}), f32[32,64,256]{2,1,0:T(8,128)}, u32[]{:S(2)}, u32[]{:S(2)}) %all-to-all-start.7) | async-done | bytes 2097184 | tf_op jit(solution)/shard_map/all_to_all | solution.py:1236
  506.7 11.5 %predicted_rows_a.1 = f32[6,64,2048]{2,1,0:T(8,128)} custom-call(f32[32,64,256]{2,1,0:T(8,128)} %all-to-all-done.7.spectra, bf16[8,2,256,1024]{3,2,1,0:T(8,128)(2,1)} %constant.36.clone.table, f32[6,64,2048]{2,1,0:T(8,128)} %predicted_rows_b.1.before), custom_call_target="tpu_custom_call", output_to_operand_aliasing={{}: (2, {})} | custom-call | tf_op jit(solution)/shard_map/predicted_rows_a/pallas_call | solution.py:624
  (29 shorter events, 0.1 us)
Async XLA Ops:
  1.3 11.0 %copy-start.14 = (s32[1,1,16]{2,1,0:T(1,128)S(1)}, s32[1,1,16]{2,1,0:T(1,128)}, u32[]{:S(2)}) copy-start(s32[1,1,16]{2,1,0:T(1,128)} %param.18) | copy-start | bytes 196
  3.6 57.2 %collective-permute-start = (f32[4,32,2048]{2,1,0:T(8,128)}, f32[4,32,2048]{2,1,0:T(8,128)}, u32[]{:S(2)}, u32[]{:S(2)}) collective-permute-start(f32[4,32,2048]{2,1,0:T(8,128)} %part_spec.3), channel_id=1, source_target_pairs={{0,31},{1,30},{2,29},{3,28},{4,27},{5,26},{6,25},{7,24},{8,23},{9,... | collective-permute-start | bytes 3145736 | tf_op jit(solution)/shard_map/ppermute | solution.py:1262
  11.0 49.8 %collective-permute-start.1 = (f32[12,1,2048]{2,1,0:T(1,128)S(1)}, f32[12,1,2048]{2,1,0:T(1,128)S(1)}, u32[]{:S(2)}, u32[]{:S(2)}) collective-permute-start(f32[12,1,2048]{2,1,0:T(1,128)S(1)} %slice_convert_fusion), channel_id=1, source_target_pairs={{16,0},{17,15},{18,14},{19,13},{20,12},{21,11},{22,10},{23,9},{24,... | collective-permute-start | bytes 294920 | tf_op jit(solution)/shard_map/ppermute | solution.py:1265
  13.0 47.5 %all-to-all-start = ((s32[16,1,1]{2,1,0:T(1,128)}), s32[16,1,1]{2,1,0:T(1,128)S(1)}, u32[]{:S(2)}, u32[]{:S(2)}) async-start(s32[16,1,1]{2,1,0:T(1,128)} %copy.18), calls=%async_computation | async-start | bytes 16384 | tf_op jit(solution)/shard_map/all_to_all | solution.py:1236
  19.8 4.3 copy-start.5
  24.1 2.2 copy-start
  26.3 2.2 copy-start.2
  37.4 1.3 copy-start.8
  60.9 96.9 %all-to-all-start.2 = ((f32[32,64,256]{2,1,0:T(8,128)}), f32[32,64,256]{2,1,0:T(8,128)S(1)}, u32[]{:S(2)}, u32[]{:S(2)}) async-start(f32[32,64,256]{2,1,0:T(8,128)} %copy-done.8), calls=%async_computation.2 | async-start | bytes 4194304 | tf_op jit(solution)/shard_map/all_to_all | solution.py:1236
  63.6 143.0 %copy-start.13 = (s32[2]{0:T(128)S(1)}, s32[2]{0:T(128)}, u32[]{:S(2)}) copy-start(s32[2]{0:T(128)} %add_convert_fusion.flags) | copy-start | bytes 28
  63.6 85.0 %collective-permute-start.2 = (f32[8,32,2048]{2,1,0:T(8,128)}, f32[8,32,2048]{2,1,0:T(8,128)S(1)}, u32[]{:S(2)}, u32[]{:S(2)}) collective-permute-start(f32[8,32,2048]{2,1,0:T(8,128)} %part_spec.2), channel_id=1, source_target_pairs={{0,31},{1,30},{2,29},{3,28},{4,27},{5,26},{6,25},{7,24},{8,23},{9,... | collective-permute-start | bytes 6291464 | tf_op jit(solution)/shard_map/ppermute | solution.py:1264
  148.7 1.4 copy-start.16
  157.7 59.4 %copy-start.15 = (f32[32,64,256]{2,1,0:T(8,128)}, f32[32,64,256]{2,1,0:T(8,128)S(1)}, u32[]{:S(2)}) copy-start(f32[32,64,256]{2,1,0:T(8,128)S(1)} %all-to-all-done.2) | copy-start | bytes 6291460
  157.7 75.0 %all-to-all-start.1 = ((f32[32,64,128]{2,1,0:T(8,128)}), f32[32,64,128]{2,1,0:T(8,128)}, u32[]{:S(2)}, u32[]{:S(2)}) async-start(f32[32,64,128]{2,1,0:T(8,128)} %get-tuple-element.31), calls=%async_computation.1 | async-start | bytes 2097152 | tf_op jit(solution)/shard_map/all_to_all | solution.py:1236
  217.1 15.6 %copy-start.12 = (bf16[512,128]{1,0:T(8,128)(2,1)S(1)}, bf16[512,128]{1,0:T(8,128)(2,1)}, u32[]{:S(2)}) copy-start(bf16[512,128]{1,0:T(8,128)(2,1)} %constant.39.clone.fold) | copy-start | bytes 393220
  247.9 3.6 copy-start.17
  247.9 29.8 %all-to-all-start.3 = ((f32[32,64,128]{2,1,0:T(8,128)}), f32[32,64,128]{2,1,0:T(8,128)S(1)}, u32[]{:S(2)}, u32[]{:S(2)}) async-start(f32[32,64,128]{2,1,0:T(8,128)} %adjoint_columns_b.1), calls=%async_computation.3 | async-start | bytes 2097152 | tf_op jit(solution)/shard_map/all_to_all | solution.py:1236
  286.4 39.9 %copy-start.9 = (f32[128,2048]{1,0:T(8,128)}, f32[128,2048]{1,0:T(8,128)S(1)}, u32[]{:S(2)}) copy-start(f32[128,2048]{1,0:T(8,128)S(1)} %get-tuple-element.41.source) | copy-start | bytes 3145732
  286.4 39.9 %copy-start.4 = (f32[1,1,3072,128]{3,2,1,0:T(8,128)S(1)}, f32[1,1,3072,128]{3,2,1,0:T(8,128)}, u32[]{:S(2)}) copy-start(f32[1,1,3072,128]{3,2,1,0:T(8,128)} %param.15) | copy-start | bytes 4718596
  286.4 39.9 %copy-start.6 = (bf16[1,1,3072,128]{3,2,1,0:T(8,128)(2,1)S(1)}, bf16[1,1,3072,128]{3,2,1,0:T(8,128)(2,1)}, u32[]{:S(2)}) copy-start(bf16[1,1,3072,128]{3,2,1,0:T(8,128)(2,1)} %param.16) | copy-start | bytes 2359300
  326.3 42.3 %copy-start.1 = (bf16[8,1024,256]{2,1,0:T(8,128)(2,1)S(1)}, bf16[8,1024,256]{2,1,0:T(8,128)(2,1)}, u32[]{:S(2)}) copy-start(bf16[8,1024,256]{2,1,0:T(8,128)(2,1)} %constant.35.clone.low) | copy-start | bytes 12582916
  326.3 42.3 %copy-start.3 = (bf16[8,1024,256]{2,1,0:T(8,128)(2,1)S(1)}, bf16[8,1024,256]{2,1,0:T(8,128)(2,1)}, u32[]{:S(2)}) copy-start(bf16[8,1024,256]{2,1,0:T(8,128)(2,1)} %constant.34.clone.high) | copy-start | bytes 12582916
  375.6 33.6 %copy-start.11 = (bf16[256,256]{1,0:T(8,128)(2,1)S(1)}, bf16[256,256]{1,0:T(8,128)(2,1)}, u32[]{:S(2)}) copy-start(bf16[256,256]{1,0:T(8,128)(2,1)} %constant.40.clone.spread) | copy-start | bytes 393220
  424.3 30.0 %all-to-all-start.8 = ((f32[32,64,128]{2,1,0:T(8,128)}), f32[32,64,128]{2,1,0:T(8,128)}, u32[]{:S(2)}, u32[]{:S(2)}) async-start(f32[32,64,128]{2,1,0:T(8,128)} %bitcast.31), calls=%async_computation.8 | async-start | bytes 2097152 | tf_op jit(solution)/shard_map/all_to_all | solution.py:1236
  454.3 52.5 %all-to-all-start.7 = ((f32[32,64,256]{2,1,0:T(8,128)}), f32[32,64,256]{2,1,0:T(8,128)}, u32[]{:S(2)}, u32[]{:S(2)}) async-start(f32[32,64,256]{2,1,0:T(8,128)} %bitcast.28), calls=%async_computation.7 | async-start | bytes 4194304 | tf_op jit(solution)/shard_map/all_to_all | solution.py:1236
  458.0 1.1 copy-start.7
  459.2 2.5 copy-start.10

commit v3 on v2

--- a/solution.py
+++ b/solution.py
@@ -232,6 +232,7 @@
 
 
 RADIX = 16
+UNROLL = 4
 LANES = 128
 TILES = (((0, 0), (1, 32), (2, 64), (3, 96)), ((4, 0), (5, 64)))
 EDGES = ((4, 32), (0, 33), (1, 34), (5, 96), (2, 97), (3, 98))
@@ -263,7 +264,7 @@
     inverse = 2.0 * forward
     inverse[0, :, 0] *= 0.5
     inverse[0, :, LANES] *= 0.5
-    inverse = inverse.swapaxes(1, 2) / float(n) ** 2
+    inverse = inverse.swapaxes(1, 2).reshape(2, n // 2, 4, n // 8).transpose(2, 0, 1, 3) / float(n) ** 2
     return (two_terms(forward), two_terms(inverse))
 
 
@@ -375,7 +376,7 @@
 
 
 def forward_blocks(load, work):
-    @pl.loop(0, LANES // 8)
+    @pl.loop(0, LANES // 8, unroll=UNROLL)
     def _(step):
         first = pl.multiple_of(step * 8, 8)
         outputs = radix16([load(a, first) for a in range(RADIX)], -1)
@@ -385,7 +386,7 @@
 
 
 def inverse_blocks(work, store):
-    @pl.loop(0, LANES // 8)
+    @pl.loop(0, LANES // 8, unroll=UNROLL)
     def _(step):
         first = pl.multiple_of(step * 8, 8)
         inputs = [
@@ -547,89 +548,90 @@
     )(misfit, *tables)
 
 
-AHEAD = 3
-
-
-def inverse_step(lhs, table, sums, held, arrived):
+TILES_Y = 4
+
+
+def gather_columns(pieces, lhs_high, lhs_low):
+    quads = 2 * lhs_high.shape[2] // (2 * LANES)
+    for quad in range(quads):
+        side, place = divmod(quad, quads // 2)
+        here = slice(place * 2 * LANES, (place + 1) * 2 * LANES)
+        lhs_high[side, :, here], lhs_low[side, :, here] = split(pieces(quad))
+
+
+def half_rows(lhs_high, lhs_low, table):
+    even, odd = (dot3((lhs_high[side], lhs_low[side]), (table[0, side, 0], table[0, side, 1])) for side in range(2))
+    return even + odd, even - odd
+
+
+def lhs_scratch(rows, n):
+    return [pltpu.VMEM((2, rows, n // 2), bf16)] * 2
+
+
+def table_spec(n):
+    return pl.BlockSpec((1, 2, 2, n // 2, n // 8), lambda s: (s, 0, 0, 0, 0))
+
+
+def predicted_kernel(begin, count, spectra, table, *refs):
+    out, lhs_high, lhs_low, held, left = refs[-5:]
     s = pl.program_id(0)
-    steps = pl.num_programs(0)
-
-    def fetch(step):
-        return pltpu.make_async_copy(table.at[step], held.at[step], arrived.at[step])
+    rows, n = out.shape[1:]
+    width = n // 2 // TILES_Y
+
+    def pieces(quad):
+        if count == 2:
+            c4r, c4i, c5r, c5i = quad_transpose([spectra[4 * quad + index] for index in range(4)])
+            real, imag = (c4r, c5r), (c4i, c5i)
+        else:
+            real = quad_transpose([spectra[4 * quad + index, :, :LANES] for index in range(4)])
+            imag = quad_transpose([spectra[4 * quad + index, :, LANES:] for index in range(4)])
+        return jnp.concatenate([jnp.concatenate(pair, axis=1) for pair in zip(real, imag)], axis=0)
+
+    def leave(step, side):
+        here = (pl.ds(begin, count), slice(None), pl.ds(side * (n // 2) + step * width, width))
+        return pltpu.make_async_copy(held.at[2 * step + side], out.at[here], left.at[2 * step + side])
 
     @pl.when(s == 0)
     def _():
-        for step in range(AHEAD):
-            fetch(step).start()
-
-    fetch(s).wait()
-
-    @pl.when(s + AHEAD < steps)
+        gather_columns(pieces, lhs_high, lhs_low)
+
+    halves = half_rows(lhs_high, lhs_low, table)
+    for step in range(TILES_Y):
+
+        @pl.when(s == step)
+        def _():
+            for side in range(2):
+                held[2 * step + side] = halves[side].reshape(count, rows, width)
+                leave(step, side).start()
+
+    @pl.when(s == TILES_Y - 1)
     def _():
-        fetch(s + AHEAD).start()
-
-    product = dot3(split(lhs), (held[s, 0], held[s, 1]))
-    side = s // (steps // 2)
-    fresh = s % (steps // 2) == 0
-
-    @pl.when(fresh)
-    def _():
-        sums[side] = product
-
-    @pl.when(jnp.logical_not(fresh))
-    def _():
-        sums[side] += product
-
-
-def inverse_scratch(rows, n, steps):
-    return [
-        pltpu.VMEM((2, rows, n // 2), f32),
-        pltpu.VMEM((steps, 2, 2 * LANES, n // 2), bf16),
-        pltpu.SemaphoreType.DMA((steps,)),
-    ]
-
-
-def finish_channels(out, sums, channels):
-    rows, n = out.shape[1:]
-
-    @pl.when(pl.program_id(0) == pl.num_programs(0) - 1)
-    def _():
-        for channel in range(channels):
-            here = slice(channel * rows, (channel + 1) * rows)
-            out[channel, :, : n // 2] = sums[0, here] + sums[1, here]
-            out[channel, :, n // 2 :] = sums[0, here] - sums[1, here]
-
-
-def predicted_kernel_b(spectra, table, out, sums, held, arrived):
-    c4r, c4i, c5r, c5i = quad_transpose([spectra[index] for index in range(4)])
-    lhs = jnp.concatenate(
-        [jnp.concatenate([c4r, c4i], axis=1), jnp.concatenate([c5r, c5i], axis=1)], axis=0
-    )
-    inverse_step(lhs, table, sums, held, arrived)
-    finish_channels(out, sums, 2)
-
-
-def predicted_kernel_a(spectra, table, before, out, sums, held, arrived):
-    real = quad_transpose([spectra[index, :, :LANES] for index in range(4)])
-    imag = quad_transpose([spectra[index, :, LANES:] for index in range(4)])
-    lhs = jnp.concatenate([jnp.concatenate(pair, axis=1) for pair in zip(real, imag)], axis=0)
-    inverse_step(lhs, table, sums, held, arrived)
-    finish_channels(out, sums, 4)
+        for step in range(TILES_Y):
+            for side in range(2):
+                leave(step, side).wait()
 
 
 def predicted_rows(spectra, table, before, n):
     devices, rows, lanes = spectra.shape
     hbm = pl.BlockSpec(memory_space=pltpu.HBM)
-    channels = 2 if before is None else 4
+    begin, count = (4, 2) if before is None else (0, 4)
     return pl.pallas_call(
-        predicted_kernel_b if before is None else predicted_kernel_a,
-        grid=(devices // 4,),
-        out_shape=jax.ShapeDtypeStruct((6, rows, n), f32),
-        in_specs=[pl.BlockSpec((4, rows, lanes), lambda s: (s, 0, 0)), hbm] + ([] if before is None else [hbm]),
-        out_specs=pl.BlockSpec((channels, rows, n), lambda s: (2 if before is None else 0, 0, 0)),
-        scratch_shapes=inverse_scratch(channels * rows, n, devices // 4),
+        functools.partial(predicted_kernel, begin, count),
+        grid=(TILES_Y,),
+        out_shape=pltpu.HBM((6, rows, n), f32),
+        in_specs=[
+            pl.BlockSpec(spectra.shape, lambda s: (0, 0, 0), pipeline_mode=pl.Buffered(1)),
+            table_spec(n),
+        ]
+        + ([] if before is None else [hbm]),
+        out_specs=hbm,
+        scratch_shapes=lhs_scratch(count * rows, n)
+        + [
+            pltpu.VMEM((2 * TILES_Y, count, rows, n // 2 // TILES_Y), f32),
+            pltpu.SemaphoreType.DMA((2 * TILES_Y,)),
+        ],
         input_output_aliases={} if before is None else {2: 0},
-        compiler_params=pltpu.CompilerParams(vmem_limit_bytes=26 << 20),
+        compiler_params=pltpu.CompilerParams(vmem_limit_bytes=24 << 20),
         name="predicted_rows_b" if before is None else "predicted_rows_a",
     )(spectra, in_hbm(table), *([] if before is None else [before]))
 
@@ -752,6 +754,13 @@
 ):
     first = flags[1] == 1
     read = started((spectra, here, got.at[0]))
+    lane8 = lane_of((8, LANES))
+    main = lane8 % 64 < 32
+    packed = jnp.logical_and(lane8 % 64 == 0, first)
+    in_place = lane8 % 64 == 32
+    packed_edge = jnp.logical_and(in_place, first)
+    moved = (lane8 % 64 == 33) | (lane8 % 64 == 34)
+    read[0].wait()
     later = [
         started(
             table_copies(table, held_table, got_table, g),
@@ -760,13 +769,6 @@
         for g in range(GROUPS)
     ]
     last = [started(table_copies(table_i, held_table_i, got_table_i, g))[0] for g in range(GROUPS)]
-    lane8 = lane_of((8, LANES))
-    main = lane8 % 64 < 32
-    packed = jnp.logical_and(lane8 % 64 == 0, first)
-    in_place = lane8 % 64 == 32
-    packed_edge = jnp.logical_and(in_place, first)
-    moved = (lane8 % 64 == 33) | (lane8 % 64 == 34)
-    read[0].wait()
 
     def load(a, row):
         value = here[pl.ds(a * LANES + row, 8), :]
@@ -852,6 +854,10 @@
 ):
     first = flags[1] == 1
     read = started((moved, here, got.at[0]))
+    lane64 = lane_of((64, LANES))
+    main64 = lane64 % 64 < 32
+    packed64 = jnp.logical_and(lane64 % 64 == 0, first)
+    read[0].wait()
     later = [
         started(
             table_copies(table, held_table, got_table, g),
@@ -860,10 +866,6 @@
         for g in range(GROUPS)
     ]
     last = [started(table_copies(table_i, held_table_i, got_table_i, g))[0] for g in range(GROUPS)]
-    lane64 = lane_of((64, LANES))
-    main64 = lane64 % 64 < 32
-    packed64 = jnp.logical_and(lane64 % 64 == 0, first)
-    read[0].wait()
     for band in range(RADIX):
         value0, value1 = here[2 * band], here[2 * band + 1]
         sides = (
@@ -1035,66 +1037,91 @@
 
 
 def gradient_kernel(
-    counts, listing, spectra, table, gradient, outgoing, sums, held, arrived, blocks, compact
+    counts, listing, spectra, table, gradient, outgoing,
+    lhs_high, lhs_low, held, blocks, compact, segments, left, sent,
 ):
+    s = pl.program_id(0)
     rows, n = gradient.shape
-    parts = quad_transpose([spectra[index] for index in range(4)])
-    lhs = jnp.concatenate(
-        [jnp.concatenate([parts[0], parts[2]], axis=0), jnp.concatenate([parts[1], parts[3]], axis=0)],
-        axis=1,
-    )
-    inverse_step(lhs, table, sums, held, arrived)
-
-    @pl.when(pl.program_id(0) == pl.num_programs(0) - 1)
+    owners, cap, _ = outgoing.shape
+    width = n // 2 // TILES_Y
+
+    def pieces(quad):
+        parts = quad_transpose([spectra[4 * quad + index] for index in range(4)])
+        return jnp.concatenate(
+            [jnp.concatenate([parts[0], parts[2]], axis=0), jnp.concatenate([parts[1], parts[3]], axis=0)],
+            axis=1,
+        )
+
+    def leave(step, side):
+        here = (slice(None), pl.ds(side * (n // 2) + step * width, width))
+        return pltpu.make_async_copy(held.at[2 * step + side], gradient.at[here], left.at[2 * step + side])
+
+    @pl.when(s == 0)
     def _():
-        gradient[:, : n // 2] = sums[0] + sums[1]
-        gradient[:, n // 2 :] = sums[0] - sums[1]
-        for q in range(RADIX):
-            blocks[q * rows : (q + 1) * rows, :] = gradient[:, q * LANES : (q + 1) * LANES]
-        owners = outgoing.shape[0]
-        cap = outgoing.shape[1]
+        gather_columns(pieces, lhs_high, lhs_low)
+
+    halves = half_rows(lhs_high, lhs_low, table)
+    for step in range(TILES_Y):
+
+        @pl.when(s == step)
+        def _():
+            for side in range(2):
+                held[2 * step + side] = halves[side]
+                leave(step, side).start()
+                for q in range(width // LANES):
+                    place = side * (RADIX // 2) + step * (width // LANES) + q
+                    blocks[place * rows : (place + 1) * rows, :] = halves[side][:, q * LANES : (q + 1) * LANES]
+
+    @pl.when(s == TILES_Y - 1)
+    def _():
         total = lax.fori_loop(0, owners, lambda o, t: t + counts[o], jnp.int32(0))
 
-        @pl.loop(0, lax.div(total + 7, 8))
+        @pl.loop(0, lax.div(total + 15, 16))
         def _(step):
-            for index in range(8):
-                at = step * 8 + index
+            for index in range(16):
+                at = step * 16 + index
                 compact[pl.ds(at, 1), :] = blocks[pl.ds(listing[at], 1), :]
 
+        copies = []
         offset = 0
         for o in range(owners):
-            outgoing[o] = compact[pl.ds(offset, cap), :]
+            segments[o] = compact[pl.ds(offset, cap), :]
+            copies.append(pltpu.make_async_copy(segments.at[o], outgoing.at[o], sent.at[o]))
+            copies[-1].start()
             offset = offset + counts[o]
+        for copy in copies:
+            copy.wait()
+        for step in range(TILES_Y):
+            for side in range(2):
+                leave(step, side).wait()
 
 
 def gradient_rows(counts, listing, spectra, table, rows, n, cap):
-    devices = spectra.shape[0]
     owners = counts.shape[0]
     smem = pl.BlockSpec(memory_space=pltpu.SMEM)
+    hbm = pl.BlockSpec(memory_space=pltpu.HBM)
     block_count = listing.shape[0]
     return pl.pallas_call(
         gradient_kernel,
-        grid=(devices // 4,),
-        out_shape=[
-            jax.ShapeDtypeStruct((rows, n), f32),
-            jax.ShapeDtypeStruct((owners, cap, LANES), f32),
-        ],
+        grid=(TILES_Y,),
+        out_shape=[pltpu.HBM((rows, n), f32), pltpu.HBM((owners, cap, LANES), f32)],
         in_specs=[
             smem,
             smem,
-            pl.BlockSpec((4, rows // 2, LANES), lambda s: (s, 0, 0)),
-            pl.BlockSpec(memory_space=pltpu.HBM),
-        ],
-        out_specs=[
-            pl.BlockSpec((rows, n), lambda s: (0, 0)),
-            pl.BlockSpec((owners, cap, LANES), lambda s: (0, 0, 0)),
-        ],
-        scratch_shapes=inverse_scratch(rows, n, devices // 4)
+            pl.BlockSpec(spectra.shape, lambda s: (0, 0, 0), pipeline_mode=pl.Buffered(1)),
+            table_spec(n),
+        ],
+        out_specs=[hbm, hbm],
+        scratch_shapes=lhs_scratch(rows, n)
         + [
+            pltpu.VMEM((2 * TILES_Y, rows, n // 2 // TILES_Y), f32),
             pltpu.VMEM((block_count, LANES), f32),
             pltpu.VMEM((block_count + cap, LANES), f32),
-        ],
-        compiler_params=pltpu.CompilerParams(vmem_limit_bytes=26 << 20),
+            pltpu.VMEM((owners, cap, LANES), f32),
+            pltpu.SemaphoreType.DMA((2 * TILES_Y,)),
+            pltpu.SemaphoreType.DMA((owners,)),
+        ],
+        compiler_params=pltpu.CompilerParams(vmem_limit_bytes=20 << 20),
         name="gradient_rows",
     )(counts, listing, spectra, in_hbm(table))
 
@@ -1149,12 +1176,17 @@
 
 
 def copied(value):
+    rows, n = value.shape
+    block = pl.BlockSpec((rows // 4, n), lambda s: (s, 0))
     return pl.pallas_call(
         copy_kernel,
-        out_shape=jax.ShapeDtypeStruct(value.shape, value.dtype),
-        compiler_params=pltpu.CompilerParams(vmem_limit_bytes=8 << 20),
+        grid=(4,),
+        out_shape=pltpu.HBM(value.shape, value.dtype),
+        in_specs=[block],
+        out_specs=block,
+        cost_estimate=pl.CostEstimate(flops=0, bytes_accessed=4_000_000, transcendentals=0),
         name="copied",
-    )(value)
+    )(in_hbm(value))
 
 
 def model_rows_kernel(counts, listing, returned, high, low, out, compact, grid, halves_high, halves_low):
@@ -1244,7 +1276,7 @@
     band = n // pen_count
     forward_np, inverse_np = row_tables(n, devices)
     row_forward = tuple(map(jnp.asarray, forward_np))
-    row_inverse = jnp.asarray(np.stack(inverse_np, axis=1))
+    row_inverse = jnp.asarray(np.stack(inverse_np, axis=2))
     forward_np, inverse_np = column_tables()
     col_forward = jnp.asarray(np.stack(forward_np, axis=1))
     col_inverse = jnp.asarray(np.stack(inverse_np, axis=1))
@@ -1279,7 +1311,9 @@
     gradient, outgoing = gradient_rows(
         counts, places, swap_all(fields, both), row_inverse, band, n, cap
     )
+    outgoing, gradient = lax.optimization_barrier((outgoing, gradient))
     incoming = swap_all(outgoing, "pen")
+    gradient, source_counts = lax.optimization_barrier((copied(gradient), source_counts))
     owned = (
         source_counts,
         incoming,
@@ -1289,14 +1323,15 @@
     updated = owner_call(owner_send_kernel, "owner_send", incoming.shape, *owned)
     updated, incoming = lax.optimization_barrier((updated, incoming))
     returned = swap_all(updated, "pen")
+    model_chunks = model_rows(counts, places, returned, row_forward, band, n, devices)
+    model_chunks, incoming = lax.optimization_barrier((model_chunks, incoming))
+    moved = swap_all(model_chunks, both)
     model_new = owner_call(
         owner_keep_kernel, "owner_keep", (owner_length, LANES), owned[0], incoming, *owned[2:]
     )
-    model_chunks = model_rows(counts, places, returned, row_forward, band, n, devices)
-    model_chunks, gradient = lax.optimization_barrier((model_chunks, gradient))
-    gradient = copied(gradient)
+    model_new, flags = lax.optimization_barrier((model_new, flags))
     out_b, edges, model = forward_columns_b(
-        flags, swap_all(model_chunks, both), pairs, col_forward, col_inverse, n
+        flags, moved, pairs, col_forward, col_inverse, n
     )
     back_b = swap_all(out_b.reshape(devices, rows, LANES), both)
     out_a = forward_columns_a(flags, model, edges, pairs, col_inverse)

time: 520 us -> 513 us (0.987)
  blocking collectives: 115 us -> 45.2 us
  waiting for transfers between devices: 195 us -> 254 us
  starting transfers between devices: 82.4 us -> 93.9 us
  Pallas kernels: 114 us -> 105 us
    all_to_all x3 -> x1, blocking collectives: 115 us -> 45.2 us  [swap_all(): return lax.all_to_all(value, axes, split_axis=0, concat_axis=0, tiled=True)]
    all_to_all x6 -> x8, waiting for transfers between devices: 115 us -> 174 us  [swap_all(): return lax.all_to_all(value, axes, split_axis=0, concat_axis=0, tiled=True)]
    all_to_all x6 -> x8, starting transfers between devices: 69.5 us -> 81 us  [swap_all(): return lax.all_to_all(value, axes, split_axis=0, concat_axis=0, tiled=True)]
  transfers between devices with their start and end apart: 9 -> 11, of which waited for: 7 -> 9; matrix products, arithmetic and copies ran while one was open for 0% -> 0% of each run, Pallas kernels for 10% -> 10%
where the time goes in v3:
time: 513 us; the launch traced here: 512 us
  waiting for transfers between devices  254 us (50%)
  Pallas kernels  105 us (20%)
  starting transfers between devices  93.9 us (18%)
  blocking collectives  45.2 us (9%)
  local copies, waits for them, and re-layouts  11 us (2%)
    all_to_all x8, waiting for transfers between devices, swap_all(): return lax.all_to_all(value, axes, split_axis=0, concat_axis=0, tiled=True)  174 us
    all_to_all x8, starting transfers between devices, swap_all(): return lax.all_to_all(value, axes, split_axis=0, concat_axis=0, tiled=True)  81 us
    ppermute x1, waiting for transfers between devices, local_paired(): got_a = lax.ppermute(sent_a, both, partner)  79.8 us
    all_to_all x1, blocking collectives, swap_all(): return lax.all_to_all(value, axes, split_axis=0, concat_axis=0, tiled=True)  45.2 us
    pallas_call x2, Pallas kernels, predicted_rows(): pl.pallas_call(functools.partial(predicted_kernel, begin, count), grid=(T...  16.5 us
    pallas_call x1, Pallas kernels, forward_columns_b(): pl.pallas_call(forward_kernel_b, out_shape=[pltpu.HBM((n, LANES), f32), p...  12.1 us
    pallas_call x1, Pallas kernels, adjoint_columns_b(): pl.pallas_call(adjoint_kernel_b, out_shape=pltpu.HBM(chunks, f32), in_spe...  11.6 us
    pallas_call x1, Pallas kernels, pair_spec(): pl.pallas_call(pair_kernel, grid=(4,), out_shape=pltpu.HBM((4, n, LANES),...  10.5 us
  transfers between devices with their start and end apart: 11, of which 9 were waited for; matrix products, arithmetic and copies ran while one was open for 0% of the time, Pallas kernels for 10%

profile of v3, /device:TPU:0, one launch (start us, length us, event | category | flops | bytes accessed | tf_op | source)
XLA Modules:
  0.0 511.8 jit_solution(819711928668305827)
XLA Ops:
  0.6 0.7 add_convert_fusion.flags
  1.3 2.3 part_spec.3
  3.6 6.4 %collective-permute-start.1 = (f32[4,32,2048]{2,1,0:T(8,128)}, f32[4,32,2048]{2,1,0:T(8,128)}, u32[]{:S(2)}, u32[]{:S(2)}) collective-permute-start(f32[4,32,2048]{2,1,0:T(8,128)} %part_spec.3), channel_id=1, source_target_pairs={{0,31},{1,30},{2,29},{3,28},{4,27},{5,26},{6,25},{7,24},{8,23},{9,... | collective-permute-start | bytes 3145736 | tf_op jit(solution)/shard_map/ppermute | solution.py:1294
  10.0 1.0 slice_convert_fusion
  11.0 1.3 collective-permute-start.2
  12.3 0.7 copy.18
  13.0 6.7 %all-to-all-start = ((s32[16,1,1]{2,1,0:T(1,128)}), s32[16,1,1]{2,1,0:T(1,128)S(1)}, u32[]{:S(2)}, u32[]{:S(2)}) async-start(s32[16,1,1]{2,1,0:T(1,128)} %copy.18), calls=%async_computation | async-start | bytes 16384 | tf_op jit(solution)/shard_map/all_to_all | solution.py:1268
  19.8 4.3 part_spec.2
  24.1 2.2 copy-done
  26.3 2.2 copy-done.2
  28.5 9.0 %misfit_rows.1 = (f32[32,64,256]{2,1,0:T(8,128)S(1)}, f32[32,64,128]{2,1,0:T(8,128)}) custom-call(f32[6,64,2048]{2,1,0:T(8,128)S(1)} %copy-done.6, bf16[8,1024,256]{2,1,0:T(8,128)(2,1)S(1)} %copy-done.2, bf16[8,1024,256]{2,1,0:T(8,128)(2,1)S(1)} %copy-done), custom_call_target="tpu_custom_call" | custom-call | tf_op jit(solution)/shard_map/misfit_rows/pallas_call | solution.py:533
  37.5 1.3 copy-done.9
  38.8 21.7 %all-to-all-done = s32[16,1,1]{2,1,0:T(1,128)S(1)} async-done(((s32[16,1,1]{2,1,0:T(1,128)}), s32[16,1,1]{2,1,0:T(1,128)S(1)}, u32[]{:S(2)}, u32[]{:S(2)}) %all-to-all-start) | async-done | bytes 96 | tf_op jit(solution)/shard_map/all_to_all | solution.py:1268
  60.5 0.4 reduce.counts
  60.9 2.7 all-to-all-start.2
  63.6 5.3 %collective-permute-start = (f32[8,32,2048]{2,1,0:T(8,128)}, f32[8,32,2048]{2,1,0:T(8,128)S(1)}, u32[]{:S(2)}, u32[]{:S(2)}) collective-permute-start(f32[8,32,2048]{2,1,0:T(8,128)} %part_spec.2), channel_id=1, source_target_pairs={{0,31},{1,30},{2,29},{3,28},{4,27},{5,26},{6,25},{7,24},{8,23},{9,... | collective-permute-start | bytes 6291464 | tf_op jit(solution)/shard_map/ppermute | solution.py:1296
  68.9 79.8 %collective-permute-done.got_a = f32[8,32,2048]{2,1,0:T(8,128)S(1)} collective-permute-done((f32[8,32,2048]{2,1,0:T(8,128)}, f32[8,32,2048]{2,1,0:T(8,128)S(1)}, u32[]{:S(2)}, u32[]{:S(2)}) %collective-permute-start) | collective-permute-done | bytes 2097184 | tf_op jit(solution)/shard_map/ppermute | solution.py:1296
  148.7 1.4 copy-done.15
  150.1 7.7 %all-to-all-done.2 = f32[32,64,256]{2,1,0:T(8,128)S(1)} async-done(((f32[32,64,256]{2,1,0:T(8,128)}), f32[32,64,256]{2,1,0:T(8,128)S(1)}, u32[]{:S(2)}, u32[]{:S(2)}) %all-to-all-start.2) | async-done | bytes 2097184 | tf_op jit(solution)/shard_map/all_to_all | solution.py:1268
  157.7 48.9 %all-to-all-start.1 = ((f32[32,64,128]{2,1,0:T(8,128)}), f32[32,64,128]{2,1,0:T(8,128)}, u32[]{:S(2)}, u32[]{:S(2)}) async-start(f32[32,64,128]{2,1,0:T(8,128)} %get-tuple-element.36), calls=%async_computation.1 | async-start | bytes 2097152 | tf_op jit(solution)/shard_map/all_to_all | solution.py:1268
  206.7 10.5 %pair_spec.1.pairs = f32[4,2048,128]{2,1,0:T(8,128)} custom-call(s32[2]{0:T(128)S(1)} %copy-done.12, bf16[12,64,2048]{2,1,0:T(8,128)(2,1)} %bitcast.26, f32[8,32,2048]{2,1,0:T(8,128)} %copy-done.15, f32[4,32,2048]{2,1,0:T(8,128)} %collective-permute-done.1.got_b, f32[12,1,2048]{2,1,0:T(1,128)S(1)} %collective-permute-done.2.edge), custom_call_target="tpu_custom_call" | custom-call | bytes 60000000 | tf_op jit(solution)/shard_map/pair_spec/pallas_call | solution.py:482
  217.1 7.5 %adjoint_columns_a.1 = (f32[2,2048,128]{2,1,0:T(8,128)S(1)}, f32[2048,128]{1,0:T(8,128)S(1)}) custom-call(s32[2]{0:T(128)S(1)} %copy-done.12, f32[2048,256]{1,0:T(8,128)} %bitcast.27, f32[4,2048,128]{2,1,0:T(8,128)} %pair_spec.1.pairs, bf16[16,2,256,256]{3,2,1,0:T(8,128)(2,1)} %constant.37.clone.table), custom_call_target="tpu_custom_call" | custom-call | bytes 20000000 | tf_op jit(solution)/shard_map/adjoint_columns_a/pallas_call | solution.py:729
  224.6 8.1 %all-to-all-done.1 = f32[32,64,128]{2,1,0:T(8,128)} async-done(((f32[32,64,128]{2,1,0:T(8,128)}), f32[32,64,128]{2,1,0:T(8,128)}, u32[]{:S(2)}, u32[]{:S(2)}) %all-to-all-start.1) | async-done | bytes 1048608 | tf_op jit(solution)/shard_map/all_to_all | solution.py:1268
  232.7 11.6 %adjoint_columns_b.1 = f32[32,64,128]{2,1,0:T(8,128)} custom-call(s32[2]{0:T(128)S(1)} %copy-done.12, f32[2048,128]{1,0:T(8,128)} %bitcast.6.spectra, f32[2048,128]{1,0:T(8,128)S(1)} %get-tuple-element.41.edges, f32[2,2048,128]{2,1,0:T(8,128)S(1)} %get-tuple-element.42.sums, bf16[512,128]{1,0:T(8,128)(2,1)S(1)} %copy-done.11, ...), custom_call_target="tpu_custom_call" | custom-call | bytes 20000000 | tf_op jit(solution)/shard_map/adjoint_columns_b/pallas_call | solution.py:825
  244.3 3.8 all-to-all-start.3
  248.1 26.0 %all-to-all-done.3.spectra = f32[32,64,128]{2,1,0:T(8,128)S(1)} async-done(((f32[32,64,128]{2,1,0:T(8,128)}), f32[32,64,128]{2,1,0:T(8,128)S(1)}, u32[]{:S(2)}, u32[]{:S(2)}) %all-to-all-start.3) | async-done | bytes 1048608 | tf_op jit(solution)/shard_map/all_to_all | solution.py:1268
  274.1 8.9 %gradient_rows.1 = (f32[128,2048]{1,0:T(8,128)}, f32[16,192,128]{2,1,0:T(8,128)}) custom-call(s32[16]{0:T(128)S(1)} %bitcast.21, s32[2048]{0:T(1024)S(1)} %bitcast.18, f32[32,64,128]{2,1,0:T(8,128)S(1)} %all-to-all-done.3.spectra, bf16[4,2,2,1024,256]{4,3,2,1,0:T(8,128)(2,1)} %constant.36.clone.table), custom_call_target="tpu_custom_call" | custom-call | tf_op jit(solution)/shard_map/gradient_rows/pallas_call | solution.py:1104
  283.0 0.0 copy-start.4
  283.0 3.9 all-to-all-start.4
  287.0 3.4 copied.1
  290.4 28.6 %all-to-all-done.4.incoming = f32[16,192,128]{2,1,0:T(8,128)S(1)} async-done(((f32[16,192,128]{2,1,0:T(8,128)}), f32[16,192,128]{2,1,0:T(8,128)S(1)}, u32[]{:S(2)}, u32[]{:S(2)}) %all-to-all-start.4) | async-done | bytes 1572896 | tf_op jit(solution)/shard_map/all_to_all | solution.py:1268
  319.0 1.1 copy-done.7
  320.1 1.1 owner_send.1
  321.2 45.2 %all_to_all.52.returned = f32[16,192,128]{2,1,0:T(8,128)S(1)} all-to-all(f32[16,192,128]{2,1,0:T(8,128)S(1)} %owner_send.1), channel_id=1, replica_groups=mesh['grp'=1,'pen'=16,'dep'=2,'chan'=1] {'pen'}, dimensions={0} | all-to-all | bytes 3145728 | tf_op jit(solution)/shard_map/all_to_all | solution.py:1268
  366.4 6.9 %model_rows.1 = f32[32,64,128]{2,1,0:T(8,128)S(1)} custom-call(s32[16]{0:T(128)S(1)} %bitcast.22, s32[2048]{0:T(1024)S(1)} %bitcast.19, f32[16,192,128]{2,1,0:T(8,128)S(1)} %all_to_all.52.returned, bf16[8,1024,256]{2,1,0:T(8,128)(2,1)S(1)} %copy-done.3, bf16[8,1024,256]{2,1,0:T(8,128)(2,1)S(1)} %copy-done.1), custom_call_target="tpu_custom_call" | custom-call | tf_op jit(solution)/shard_map/model_rows/pallas_call | solution.py:1240
  373.4 1.0 copy-done.5
  374.3 7.3 %all-to-all-start.6 = ((f32[32,64,128]{2,1,0:T(8,128)}), f32[32,64,128]{2,1,0:T(8,128)}, u32[]{:S(2)}, u32[]{:S(2)}) async-start(f32[32,64,128]{2,1,0:T(8,128)} %copy-done.5), calls=%async_computation.6 | async-start | bytes 2097152 | tf_op jit(solution)/shard_map/all_to_all | solution.py:1268
  381.7 1.1 copy-done.8
  382.8 2.6 owner_keep.1
  385.4 22.5 %all-to-all-done.6.moved = f32[32,64,128]{2,1,0:T(8,128)} async-done(((f32[32,64,128]{2,1,0:T(8,128)}), f32[32,64,128]{2,1,0:T(8,128)}, u32[]{:S(2)}, u32[]{:S(2)}) %all-to-all-start.6) | async-done | bytes 1048608 | tf_op jit(solution)/shard_map/all_to_all | solution.py:1268
  407.9 12.1 %forward_columns_b.1 = (f32[2048,128]{1,0:T(8,128)}, f32[2048,128]{1,0:T(8,128)}, f32[16,256,128]{2,1,0:T(8,128)}) custom-call(s32[2]{0:T(128)S(1)} %copy-done.12, f32[32,64,128]{2,1,0:T(8,128)} %all-to-all-done.6.moved, bf16[256,256]{1,0:T(8,128)(2,1)S(1)} %copy-done.10, f32[4,2048,128]{2,1,0:T(8,128)} %pair_spec.1.pairs, ...), custom_call_target="tpu_custom_call" | custom-call | bytes 20000000 | tf_op jit(solution)/shard_map/forward_columns_b/pallas_call | solution.py:926
  420.0 3.9 all-to-all-start.8
  423.9 8.0 %forward_columns_a.1 = f32[2048,256]{1,0:T(8,128)} custom-call(s32[2]{0:T(128)S(1)} %copy-done.12, f32[16,256,128]{2,1,0:T(8,128)} %get-tuple-element.56.model, f32[2048,128]{1,0:T(8,128)} %get-tuple-element.57.edges, f32[4,2048,128]{2,1,0:T(8,128)} %pair_spec.1.pairs, bf16[16,2,256,256]{3,2,1,0:T(8,128)(2,1)} %constant.38.clone.table_i), custom_call_target="tpu_custom_call" | custom-call | bytes 16000000 | tf_op jit(solution)/shard_map/forward_columns_a/pallas_call | solution.py:1016
  431.9 17.9 %all-to-all-done.8.spectra = f32[32,64,128]{2,1,0:T(8,128)S(1)} async-done(((f32[32,64,128]{2,1,0:T(8,128)}), f32[32,64,128]{2,1,0:T(8,128)S(1)}, u32[]{:S(2)}, u32[]{:S(2)}) %all-to-all-start.8) | async-done | bytes 1048608 | tf_op jit(solution)/shard_map/all_to_all | solution.py:1268
  449.9 3.6 all-to-all-start.7
  453.5 7.1 %predicted_rows_b.1.refs_0_ = f32[6,64,2048]{2,1,0:T(8,128)} custom-call(f32[32,64,128]{2,1,0:T(8,128)S(1)} %all-to-all-done.8.spectra, bf16[4,2,2,1024,256]{4,3,2,1,0:T(8,128)(2,1)} %constant.36.clone.table), custom_call_target="tpu_custom_call" | custom-call | tf_op jit(solution)/shard_map/predicted_rows_b/pallas_call | solution.py:618
  460.6 41.6 %all-to-all-done.7.spectra = f32[32,64,256]{2,1,0:T(8,128)S(1)} async-done(((f32[32,64,256]{2,1,0:T(8,128)}), f32[32,64,256]{2,1,0:T(8,128)S(1)}, u32[]{:S(2)}, u32[]{:S(2)}) %all-to-all-start.7) | async-done | bytes 2097184 | tf_op jit(solution)/shard_map/all_to_all | solution.py:1268
  502.2 9.4 %predicted_rows_a.1 = f32[6,64,2048]{2,1,0:T(8,128)} custom-call(f32[32,64,256]{2,1,0:T(8,128)S(1)} %all-to-all-done.7.spectra, bf16[4,2,2,1024,256]{4,3,2,1,0:T(8,128)(2,1)} %constant.36.clone.table, f32[6,64,2048]{2,1,0:T(8,128)} %predicted_rows_b.1.refs_0_), custom_call_target="tpu_custom_call", output_to_operand_aliasing={{}: (2, {})} | custom-call | tf_op jit(solution)/shard_map/predicted_rows_a/pallas_call | solution.py:618
  (29 shorter events, 0.1 us)
Async XLA Ops:
  1.3 11.0 %copy-start.13 = (s32[1,1,16]{2,1,0:T(1,128)S(1)}, s32[1,1,16]{2,1,0:T(1,128)}, u32[]{:S(2)}) copy-start(s32[1,1,16]{2,1,0:T(1,128)} %param.18) | copy-start | bytes 196
  3.6 57.2 %collective-permute-start.1 = (f32[4,32,2048]{2,1,0:T(8,128)}, f32[4,32,2048]{2,1,0:T(8,128)}, u32[]{:S(2)}, u32[]{:S(2)}) collective-permute-start(f32[4,32,2048]{2,1,0:T(8,128)} %part_spec.3), channel_id=1, source_target_pairs={{0,31},{1,30},{2,29},{3,28},{4,27},{5,26},{6,25},{7,24},{8,23},{9,... | collective-permute-start | bytes 3145736 | tf_op jit(solution)/shard_map/ppermute | solution.py:1294
  11.0 49.8 %collective-permute-start.2 = (f32[12,1,2048]{2,1,0:T(1,128)S(1)}, f32[12,1,2048]{2,1,0:T(1,128)S(1)}, u32[]{:S(2)}, u32[]{:S(2)}) collective-permute-start(f32[12,1,2048]{2,1,0:T(1,128)S(1)} %slice_convert_fusion), channel_id=1, source_target_pairs={{16,0},{17,15},{18,14},{19,13},{20,12},{21,11},{22,10},{23,9},{24,... | collective-permute-start | bytes 294920 | tf_op jit(solution)/shard_map/ppermute | solution.py:1297
  13.0 47.4 %all-to-all-start = ((s32[16,1,1]{2,1,0:T(1,128)}), s32[16,1,1]{2,1,0:T(1,128)S(1)}, u32[]{:S(2)}, u32[]{:S(2)}) async-start(s32[16,1,1]{2,1,0:T(1,128)} %copy.18), calls=%async_computation | async-start | bytes 16384 | tf_op jit(solution)/shard_map/all_to_all | solution.py:1268
  19.8 4.3 copy-start.6
  24.1 2.2 copy-start
  26.3 2.2 copy-start.2
  37.5 1.3 copy-start.9
  60.9 96.9 %all-to-all-start.2 = ((f32[32,64,256]{2,1,0:T(8,128)}), f32[32,64,256]{2,1,0:T(8,128)S(1)}, u32[]{:S(2)}, u32[]{:S(2)}) async-start(f32[32,64,256]{2,1,0:T(8,128)} %copy-done.9), calls=%async_computation.2 | async-start | bytes 4194304 | tf_op jit(solution)/shard_map/all_to_all | solution.py:1268
  63.6 143.0 %copy-start.12 = (s32[2]{0:T(128)S(1)}, s32[2]{0:T(128)}, u32[]{:S(2)}) copy-start(s32[2]{0:T(128)} %add_convert_fusion.flags) | copy-start | bytes 28
  63.6 85.0 %collective-permute-start = (f32[8,32,2048]{2,1,0:T(8,128)}, f32[8,32,2048]{2,1,0:T(8,128)S(1)}, u32[]{:S(2)}, u32[]{:S(2)}) collective-permute-start(f32[8,32,2048]{2,1,0:T(8,128)} %part_spec.2), channel_id=1, source_target_pairs={{0,31},{1,30},{2,29},{3,28},{4,27},{5,26},{6,25},{7,24},{8,23},{9,... | collective-permute-start | bytes 6291464 | tf_op jit(solution)/shard_map/ppermute | solution.py:1296
  148.7 1.4 copy-start.15
  157.7 59.4 %copy-start.14 = (f32[32,64,256]{2,1,0:T(8,128)}, f32[32,64,256]{2,1,0:T(8,128)S(1)}, u32[]{:S(2)}) copy-start(f32[32,64,256]{2,1,0:T(8,128)S(1)} %all-to-all-done.2) | copy-start | bytes 6291460
  157.7 74.9 %all-to-all-start.1 = ((f32[32,64,128]{2,1,0:T(8,128)}), f32[32,64,128]{2,1,0:T(8,128)}, u32[]{:S(2)}, u32[]{:S(2)}) async-start(f32[32,64,128]{2,1,0:T(8,128)} %get-tuple-element.36), calls=%async_computation.1 | async-start | bytes 2097152 | tf_op jit(solution)/shard_map/all_to_all | solution.py:1268
  217.1 15.6 %copy-start.11 = (bf16[512,128]{1,0:T(8,128)(2,1)S(1)}, bf16[512,128]{1,0:T(8,128)(2,1)}, u32[]{:S(2)}) copy-start(bf16[512,128]{1,0:T(8,128)(2,1)} %constant.39.clone.fold) | copy-start | bytes 393220
  244.3 3.9 copy-start.16
  244.3 29.9 %all-to-all-start.3 = ((f32[32,64,128]{2,1,0:T(8,128)}), f32[32,64,128]{2,1,0:T(8,128)S(1)}, u32[]{:S(2)}, u32[]{:S(2)}) async-start(f32[32,64,128]{2,1,0:T(8,128)} %adjoint_columns_b.1), calls=%async_computation.3 | async-start | bytes 2097152 | tf_op jit(solution)/shard_map/all_to_all | solution.py:1268
  283.0 35.9 %copy-start.4 = (f32[1,1,3072,128]{3,2,1,0:T(8,128)S(1)}, f32[1,1,3072,128]{3,2,1,0:T(8,128)}, u32[]{:S(2)}) copy-start(f32[1,1,3072,128]{3,2,1,0:T(8,128)} %param.15) | copy-start | bytes 4718596
  283.0 35.9 %all-to-all-start.4 = ((f32[16,192,128]{2,1,0:T(8,128)}), f32[16,192,128]{2,1,0:T(8,128)S(1)}, u32[]{:S(2)}, u32[]{:S(2)}) async-start(f32[16,192,128]{2,1,0:T(8,128)} %get-tuple-element.49), calls=%async_computation.4 | async-start | bytes 3145728 | tf_op jit(solution)/shard_map/all_to_all | solution.py:1268
  319.0 1.1 copy-start.7
  320.1 46.3 %copy-start.1 = (bf16[8,1024,256]{2,1,0:T(8,128)(2,1)S(1)}, bf16[8,1024,256]{2,1,0:T(8,128)(2,1)}, u32[]{:S(2)}) copy-start(bf16[8,1024,256]{2,1,0:T(8,128)(2,1)} %constant.35.clone.low) | copy-start | bytes 12582916
  320.1 46.3 %copy-start.3 = (bf16[8,1024,256]{2,1,0:T(8,128)(2,1)S(1)}, bf16[8,1024,256]{2,1,0:T(8,128)(2,1)}, u32[]{:S(2)}) copy-start(bf16[8,1024,256]{2,1,0:T(8,128)(2,1)} %constant.34.clone.high) | copy-start | bytes 12582916
  373.4 1.0 copy-start.5
  374.3 33.6 %all-to-all-start.6 = ((f32[32,64,128]{2,1,0:T(8,128)}), f32[32,64,128]{2,1,0:T(8,128)}, u32[]{:S(2)}, u32[]{:S(2)}) async-start(f32[32,64,128]{2,1,0:T(8,128)} %copy-done.5), calls=%async_computation.6 | async-start | bytes 2097152 | tf_op jit(solution)/shard_map/all_to_all | solution.py:1268
  381.7 1.1 copy-start.8
  382.8 25.1 %copy-start.10 = (bf16[256,256]{1,0:T(8,128)(2,1)S(1)}, bf16[256,256]{1,0:T(8,128)(2,1)}, u32[]{:S(2)}) copy-start(bf16[256,256]{1,0:T(8,128)(2,1)} %constant.40.clone.spread) | copy-start | bytes 393220
  420.0 29.9 %all-to-all-start.8 = ((f32[32,64,128]{2,1,0:T(8,128)}), f32[32,64,128]{2,1,0:T(8,128)S(1)}, u32[]{:S(2)}, u32[]{:S(2)}) async-start(f32[32,64,128]{2,1,0:T(8,128)} %bitcast.31), calls=%async_computation.8 | async-start | bytes 2097152 | tf_op jit(solution)/shard_map/all_to_all | solution.py:1268
  449.9 52.4 %all-to-all-start.7 = ((f32[32,64,256]{2,1,0:T(8,128)}), f32[32,64,256]{2,1,0:T(8,128)S(1)}, u32[]{:S(2)}, u32[]{:S(2)}) async-start(f32[32,64,256]{2,1,0:T(8,128)} %bitcast.28), calls=%async_computation.7 | async-start | bytes 4194304 | tf_op jit(solution)/shard_map/all_to_all | solution.py:1268

commit v4 on v3

--- a/solution.py
+++ b/solution.py
@@ -375,14 +375,14 @@
     return outputs
 
 
-def forward_blocks(load, work):
-    @pl.loop(0, LANES // 8, unroll=UNROLL)
+def forward_blocks(load, work, begin=0, rows=LANES):
+    @pl.loop(0, rows // 8, unroll=UNROLL)
     def _(step):
-        first = pl.multiple_of(step * 8, 8)
-        outputs = radix16([load(a, first) for a in range(RADIX)], -1)
+        row = pl.multiple_of(step * 8, 8)
+        outputs = radix16([load(a, row) for a in range(RADIX)], -1)
         for k, (re, im) in enumerate(outputs):
-            work[k, pl.ds(first, 8), :] = re
-            work[k, pl.ds(first + LANES, 8), :] = im
+            work[k, pl.ds(begin + row, 8), :] = re
+            work[k, pl.ds(begin + row + LANES, 8), :] = im
 
 
 def inverse_blocks(work, store):
@@ -551,51 +551,70 @@
 TILES_Y = 4
 
 
-def gather_columns(pieces, lhs_high, lhs_low):
-    quads = 2 * lhs_high.shape[2] // (2 * LANES)
+def gather_columns(pieces, fetched, lhs_high, lhs_low):
+    spectra, here, arrived, table, held, ready = fetched
+    quads = spectra.shape[0] // 4
+    copies = [
+        pltpu.make_async_copy(
+            spectra.at[pl.ds(4 * quad, 4)], here.at[pl.ds(4 * quad, 4)], arrived.at[quad]
+        )
+        for quad in range(quads)
+    ]
+    for copy in copies:
+        copy.start()
+    for step in range(TILES_Y):
+        pltpu.make_async_copy(table.at[step], held.at[step], ready.at[step]).start()
     for quad in range(quads):
+        copies[quad].wait()
         side, place = divmod(quad, quads // 2)
-        here = slice(place * 2 * LANES, (place + 1) * 2 * LANES)
-        lhs_high[side, :, here], lhs_low[side, :, here] = split(pieces(quad))
-
-
-def half_rows(lhs_high, lhs_low, table):
-    even, odd = (dot3((lhs_high[side], lhs_low[side]), (table[0, side, 0], table[0, side, 1])) for side in range(2))
+        at = slice(place * 2 * LANES, (place + 1) * 2 * LANES)
+        lhs_high[side, :, at], lhs_low[side, :, at] = split(pieces(quad))
+
+
+def half_rows(lhs_high, lhs_low, fetched):
+    s = pl.program_id(0)
+    _, _, _, table, held, ready = fetched
+    pltpu.make_async_copy(table.at[s], held.at[s], ready.at[s]).wait()
+    even, odd = (dot3((lhs_high[side], lhs_low[side]), (held[s, side, 0], held[s, side, 1])) for side in range(2))
     return even + odd, even - odd
 
 
-def lhs_scratch(rows, n):
-    return [pltpu.VMEM((2, rows, n // 2), bf16)] * 2
-
-
-def table_spec(n):
-    return pl.BlockSpec((1, 2, 2, n // 2, n // 8), lambda s: (s, 0, 0, 0, 0))
+def row_scratch(spectra, rows, n):
+    return [
+        pltpu.VMEM(spectra.shape, f32),
+        pltpu.SemaphoreType.DMA((spectra.shape[0] // 4,)),
+        pltpu.VMEM((TILES_Y, 2, 2, n // 2, n // 2 // TILES_Y), bf16),
+        pltpu.SemaphoreType.DMA((TILES_Y,)),
+        pltpu.VMEM((2, rows, n // 2), bf16),
+        pltpu.VMEM((2, rows, n // 2), bf16),
+    ]
 
 
 def predicted_kernel(begin, count, spectra, table, *refs):
-    out, lhs_high, lhs_low, held, left = refs[-5:]
+    out, here, arrived, held_table, ready, lhs_high, lhs_low, held, left = refs[-9:]
+    fetched = (spectra, here, arrived, table, held_table, ready)
     s = pl.program_id(0)
     rows, n = out.shape[1:]
     width = n // 2 // TILES_Y
 
     def pieces(quad):
         if count == 2:
-            c4r, c4i, c5r, c5i = quad_transpose([spectra[4 * quad + index] for index in range(4)])
+            c4r, c4i, c5r, c5i = quad_transpose([here[4 * quad + index] for index in range(4)])
             real, imag = (c4r, c5r), (c4i, c5i)
         else:
-            real = quad_transpose([spectra[4 * quad + index, :, :LANES] for index in range(4)])
-            imag = quad_transpose([spectra[4 * quad + index, :, LANES:] for index in range(4)])
+            real = quad_transpose([here[4 * quad + index, :, :LANES] for index in range(4)])
+            imag = quad_transpose([here[4 * quad + index, :, LANES:] for index in range(4)])
         return jnp.concatenate([jnp.concatenate(pair, axis=1) for pair in zip(real, imag)], axis=0)
 
     def leave(step, side):
-        here = (pl.ds(begin, count), slice(None), pl.ds(side * (n // 2) + step * width, width))
-        return pltpu.make_async_copy(held.at[2 * step + side], out.at[here], left.at[2 * step + side])
+        place = (pl.ds(begin, count), slice(None), pl.ds(side * (n // 2) + step * width, width))
+        return pltpu.make_async_copy(held.at[2 * step + side], out.at[place], left.at[2 * step + side])
 
     @pl.when(s == 0)
     def _():
-        gather_columns(pieces, lhs_high, lhs_low)
-
-    halves = half_rows(lhs_high, lhs_low, table)
+        gather_columns(pieces, fetched, lhs_high, lhs_low)
+
+    halves = half_rows(lhs_high, lhs_low, fetched)
     for step in range(TILES_Y):
 
         @pl.when(s == step)
@@ -619,19 +638,15 @@
         functools.partial(predicted_kernel, begin, count),
         grid=(TILES_Y,),
         out_shape=pltpu.HBM((6, rows, n), f32),
-        in_specs=[
-            pl.BlockSpec(spectra.shape, lambda s: (0, 0, 0), pipeline_mode=pl.Buffered(1)),
-            table_spec(n),
-        ]
-        + ([] if before is None else [hbm]),
+        in_specs=[pl.BlockSpec(memory_space=pl.ANY)] + [hbm] * (1 if before is None else 2),
         out_specs=hbm,
-        scratch_shapes=lhs_scratch(count * rows, n)
+        scratch_shapes=row_scratch(spectra, count * rows, n)
         + [
             pltpu.VMEM((2 * TILES_Y, count, rows, n // 2 // TILES_Y), f32),
             pltpu.SemaphoreType.DMA((2 * TILES_Y,)),
         ],
         input_output_aliases={} if before is None else {2: 0},
-        compiler_params=pltpu.CompilerParams(vmem_limit_bytes=24 << 20),
+        compiler_params=pltpu.CompilerParams(vmem_limit_bytes=28 << 20),
         name="predicted_rows_b" if before is None else "predicted_rows_a",
     )(spectra, in_hbm(table), *([] if before is None else [before]))
 
@@ -667,6 +682,14 @@
 def table_copies(table, held, arrived, group):
     here = group_steps(group)
     return (table.at[here], held.at[here], arrived.at[group])
+
+
+def stacked_product(table, k, value):
+    high, low = split(value)
+    terms = jnp.concatenate([table[k, 0], table[k, 1]], axis=0)
+    wide = dot(terms, jnp.concatenate([high, low], axis=1))
+    size = high.shape[0]
+    return wide[:size, :LANES] + wide[:size, LANES:] + wide[size:, :LANES]
 
 
 def table_product(table, k, value):
@@ -785,7 +808,7 @@
         for copy in later[group][:2]:
             copy.wait()
         for k in in_group(group):
-            spectrum = table_product(held_table, k, work[k])
+            spectrum = stacked_product(held_table, k, work[k])
             row = slice(k * LANES, (k + 1) * LANES)
             parts = []
             for value in turn_phase(turned, spectrum[:LANES], spectrum[LANES:], -1):
@@ -798,7 +821,7 @@
     for group in range(GROUPS):
         last[group].wait()
         for k in in_group(group):
-            work[k] = table_product(held_table_i, k, work[k])
+            work[k] = stacked_product(held_table_i, k, work[k])
 
     def store(a, row, real, imag):
         fields[pl.ds(a * LANES + row, 8), :] = jnp.where(main | packed_edge, real, turn(imag, 32))
@@ -849,14 +872,11 @@
 
 def forward_kernel_b(
     flags, moved, spread, pairs, table, table_i, out, edges, model,
-    work, here, held_pairs, held_table, held_table_i, fields, chunk, held_model, held_edges,
+    work, here, held_pairs, held_table, held_table_i, chunk, held_model, held_edges,
     got, got_pairs, got_table, got_table_i, left,
 ):
     first = flags[1] == 1
     read = started((moved, here, got.at[0]))
-    lane64 = lane_of((64, LANES))
-    main64 = lane64 % 64 < 32
-    packed64 = jnp.logical_and(lane64 % 64 == 0, first)
     read[0].wait()
     later = [
         started(
@@ -866,23 +886,21 @@
         for g in range(GROUPS)
     ]
     last = [started(table_copies(table_i, held_table_i, got_table_i, g))[0] for g in range(GROUPS)]
-    for band in range(RADIX):
-        value0, value1 = here[2 * band], here[2 * band + 1]
-        sides = (
-            jnp.where(lane64 < 64, value0, turn(value1, 64)),
-            jnp.where(lane64 < 64, turn(value0, 64), value1),
-        )
-        for side, value in enumerate(sides):
-            row = band * LANES + 64 * side
-            fields[0, row : row + 64, :] = value
-            fields[1, row : row + 64, :] = jnp.where(
-                jnp.logical_and(main64, jnp.logical_not(packed64)), turn(value, 96), 0.0
-            )
-
-    def load(a, row):
-        return tuple(fields[part, pl.ds(a * LANES + row, 8), :] for part in range(2))
-
-    forward_blocks(load, work)
+    lane8 = lane_of((8, LANES))
+    main = lane8 % 64 < 32
+    real_only = jnp.logical_or(jnp.logical_not(main), jnp.logical_and(lane8 % 64 == 0, first))
+
+    for side in range(2):
+
+        def load(band, row):
+            value0, value1 = here[2 * band, pl.ds(row, 8), :], here[2 * band + 1, pl.ds(row, 8), :]
+            if side == 0:
+                value = jnp.where(lane8 < 64, value0, turn(value1, 64))
+            else:
+                value = jnp.where(lane8 < 64, turn(value0, 64), value1)
+            return (value, jnp.where(real_only, 0.0, turn(value, 96)))
+
+        forward_blocks(load, work, 64 * side, 64)
     lane = lane_of((LANES, LANES))
     turned = (lane <= 32) | (lane == 97)
     for group in range(GROUPS):
@@ -905,8 +923,6 @@
         for k in in_group(group):
             work[k] = table_product(held_table_i, k, work[k])
 
-    lane8 = lane_of((8, LANES))
-    main = lane8 % 64 < 32
     packed = jnp.logical_and(lane8 % 64 == 32, first)
 
     def store(a, row, real, imag):
@@ -945,7 +961,6 @@
             pairs_like(n),
             TABLE,
             TABLE,
-            pairs_like(n),
             pltpu.VMEM((n, LANES), f32),
             WORK,
             pltpu.VMEM((n, LANES), f32),
@@ -1038,29 +1053,30 @@
 
 def gradient_kernel(
     counts, listing, spectra, table, gradient, outgoing,
-    lhs_high, lhs_low, held, blocks, compact, segments, left, sent,
+    here, arrived, held_table, ready, lhs_high, lhs_low, held, blocks, compact, segments, left, sent,
 ):
     s = pl.program_id(0)
     rows, n = gradient.shape
+    fetched = (spectra, here, arrived, table, held_table, ready)
     owners, cap, _ = outgoing.shape
     width = n // 2 // TILES_Y
 
     def pieces(quad):
-        parts = quad_transpose([spectra[4 * quad + index] for index in range(4)])
+        parts = quad_transpose([here[4 * quad + index] for index in range(4)])
         return jnp.concatenate(
             [jnp.concatenate([parts[0], parts[2]], axis=0), jnp.concatenate([parts[1], parts[3]], axis=0)],
             axis=1,
         )
 
     def leave(step, side):
-        here = (slice(None), pl.ds(side * (n // 2) + step * width, width))
-        return pltpu.make_async_copy(held.at[2 * step + side], gradient.at[here], left.at[2 * step + side])
+        place = (slice(None), pl.ds(side * (n // 2) + step * width, width))
+        return pltpu.make_async_copy(held.at[2 * step + side], gradient.at[place], left.at[2 * step + side])
 
     @pl.when(s == 0)
     def _():
-        gather_columns(pieces, lhs_high, lhs_low)
-
-    halves = half_rows(lhs_high, lhs_low, table)
+        gather_columns(pieces, fetched, lhs_high, lhs_low)
+
+    halves = half_rows(lhs_high, lhs_low, fetched)
     for step in range(TILES_Y):
 
         @pl.when(s == step)
@@ -1076,7 +1092,14 @@
     def _():
         total = lax.fori_loop(0, owners, lambda o, t: t + counts[o], jnp.int32(0))
 
-        @pl.loop(0, lax.div(total + 15, 16))
+        full = total == blocks.shape[0]
+
+        @pl.when(full)
+        def _():
+            for q in range(RADIX):
+                compact[pl.ds(q, rows, stride=RADIX), :] = blocks[q * rows : (q + 1) * rows, :]
+
+        @pl.loop(0, jnp.where(full, 0, lax.div(total + 15, 16)))
         def _(step):
             for index in range(16):
                 at = step * 16 + index
@@ -1108,11 +1131,11 @@
         in_specs=[
             smem,
             smem,
-            pl.BlockSpec(spectra.shape, lambda s: (0, 0, 0), pipeline_mode=pl.Buffered(1)),
-            table_spec(n),
+            pl.BlockSpec(memory_space=pl.ANY),
+            hbm,
         ],
         out_specs=[hbm, hbm],
-        scratch_shapes=lhs_scratch(rows, n)
+        scratch_shapes=row_scratch(spectra, rows, n)
         + [
             pltpu.VMEM((2 * TILES_Y, rows, n // 2 // TILES_Y), f32),
             pltpu.VMEM((block_count, LANES), f32),
@@ -1121,7 +1144,7 @@
             pltpu.SemaphoreType.DMA((2 * TILES_Y,)),
             pltpu.SemaphoreType.DMA((owners,)),
         ],
-        compiler_params=pltpu.CompilerParams(vmem_limit_bytes=20 << 20),
+        compiler_params=pltpu.CompilerParams(vmem_limit_bytes=26 << 20),
         name="gradient_rows",
     )(counts, listing, spectra, in_hbm(table))
 
@@ -1196,12 +1219,21 @@
 
     @pl.when(s == 0)
     def _():
-        grid[...] = jnp.zeros_like(grid)
         offset = 0
         for o in range(owners):
             compact[pl.ds(offset, cap), :] = returned[o]
             offset = offset + counts[o]
-        total = offset
+        full = offset == grid.shape[0]
+        total = jnp.where(full, 0, offset)
+
+        @pl.when(full)
+        def _():
+            for q in range(RADIX):
+                grid[q * rows : (q + 1) * rows, :] = compact[pl.ds(q, rows, stride=RADIX), :]
+
+        @pl.when(jnp.logical_not(full))
+        def _():
+            grid[...] = jnp.zeros_like(grid)
 
         @pl.loop(0, lax.div(total, 8))
         def _(step):
@@ -1240,7 +1272,7 @@
     return pl.pallas_call(
         model_rows_kernel,
         grid=(devices // 4,),
-        out_shape=jax.ShapeDtypeStruct((devices, rows // 2, LANES), f32),
+        out_shape=pltpu.HBM((devices, rows // 2, LANES), f32),
         in_specs=[
             smem,
             smem,

time: 513 us -> 507 us (0.988)
    unnamed x34 -> x32, local copies, waits for them, and re-layouts: 10.3 us -> 9.38 us
where the time goes in v4:
time: 507 us; the launch traced here: 505 us
  waiting for transfers between devices  255 us (50%)
  Pallas kernels  102 us (20%)
  starting transfers between devices  90.7 us (18%)
  blocking collectives  45.3 us (9%)
  local copies, waits for them, and re-layouts  10.1 us (2%)
    all_to_all x8, waiting for transfers between devices, swap_all(): return lax.all_to_all(value, axes, split_axis=0, concat_axis=0, tiled=True)  175 us
    ppermute x1, waiting for transfers between devices, local_paired(): got_a = lax.ppermute(sent_a, both, partner)  79.8 us
    all_to_all x8, starting transfers between devices, swap_all(): return lax.all_to_all(value, axes, split_axis=0, concat_axis=0, tiled=True)  77.8 us
    all_to_all x1, blocking collectives, swap_all(): return lax.all_to_all(value, axes, split_axis=0, concat_axis=0, tiled=True)  45.3 us
    pallas_call x2, Pallas kernels, predicted_rows(): pl.pallas_call(functools.partial(predicted_kernel, begin, count), grid=(T...  14.1 us
    pallas_call x1, Pallas kernels, forward_columns_b(): pl.pallas_call(forward_kernel_b, out_shape=[pltpu.HBM((n, LANES), f32), p...  11.2 us
    pallas_call x1, Pallas kernels, adjoint_columns_b(): pl.pallas_call(adjoint_kernel_b, out_shape=pltpu.HBM(chunks, f32), in_spe...  10.9 us
    pallas_call x1, Pallas kernels, pair_spec(): pl.pallas_call(pair_kernel, grid=(4,), out_shape=pltpu.HBM((4, n, LANES),...  10.5 us
  transfers between devices with their start and end apart: 11, of which 9 were waited for; matrix products, arithmetic and copies ran while one was open for 0% of the time, Pallas kernels for 10%

profile of v4, /device:TPU:0, one launch (start us, length us, event | category | flops | bytes accessed | tf_op | source)
XLA Modules:
  0.0 505.3 jit_solution(3250908638199377372)
XLA Ops:
  0.6 0.7 add_convert_fusion.flags
  1.3 2.3 part_spec.3
  3.6 6.4 %collective-permute-start.1 = (f32[4,32,2048]{2,1,0:T(8,128)}, f32[4,32,2048]{2,1,0:T(8,128)}, u32[]{:S(2)}, u32[]{:S(2)}) collective-permute-start(f32[4,32,2048]{2,1,0:T(8,128)} %part_spec.3), channel_id=1, source_target_pairs={{0,31},{1,30},{2,29},{3,28},{4,27},{5,26},{6,25},{7,24},{8,23},{9,... | collective-permute-start | bytes 3145736 | tf_op jit(solution)/shard_map/ppermute | solution.py:1326
  10.0 1.0 slice_convert_fusion
  11.0 1.3 collective-permute-start.2
  12.3 0.7 copy.18
  13.0 6.7 %all-to-all-start = ((s32[16,1,1]{2,1,0:T(1,128)}), s32[16,1,1]{2,1,0:T(1,128)S(1)}, u32[]{:S(2)}, u32[]{:S(2)}) async-start(s32[16,1,1]{2,1,0:T(1,128)} %copy.18), calls=%async_computation | async-start | bytes 16384 | tf_op jit(solution)/shard_map/all_to_all | solution.py:1300
  19.7 0.0 copy-start.5
  19.7 4.3 part_spec.2
  24.1 2.2 copy-done
  26.3 2.2 copy-done.2
  28.4 9.0 %misfit_rows.1 = (f32[32,64,256]{2,1,0:T(8,128)S(1)}, f32[32,64,128]{2,1,0:T(8,128)}) custom-call(f32[6,64,2048]{2,1,0:T(8,128)S(1)} %copy-done.5, bf16[8,1024,256]{2,1,0:T(8,128)(2,1)S(1)} %copy-done.2, bf16[8,1024,256]{2,1,0:T(8,128)(2,1)S(1)} %copy-done), custom_call_target="tpu_custom_call" | custom-call | tf_op jit(solution)/shard_map/misfit_rows/pallas_call | solution.py:533
  37.4 1.3 copy-done.8
  38.8 21.7 %all-to-all-done = s32[16,1,1]{2,1,0:T(1,128)S(1)} async-done(((s32[16,1,1]{2,1,0:T(1,128)}), s32[16,1,1]{2,1,0:T(1,128)S(1)}, u32[]{:S(2)}, u32[]{:S(2)}) %all-to-all-start) | async-done | bytes 96 | tf_op jit(solution)/shard_map/all_to_all | solution.py:1300
  60.5 0.4 reduce.counts
  60.9 2.7 all-to-all-start.2
  63.6 5.3 %collective-permute-start = (f32[8,32,2048]{2,1,0:T(8,128)}, f32[8,32,2048]{2,1,0:T(8,128)S(1)}, u32[]{:S(2)}, u32[]{:S(2)}) collective-permute-start(f32[8,32,2048]{2,1,0:T(8,128)} %part_spec.2), channel_id=1, source_target_pairs={{0,31},{1,30},{2,29},{3,28},{4,27},{5,26},{6,25},{7,24},{8,23},{9,... | collective-permute-start | bytes 6291464 | tf_op jit(solution)/shard_map/ppermute | solution.py:1328
  68.9 79.8 %collective-permute-done.got_a = f32[8,32,2048]{2,1,0:T(8,128)S(1)} collective-permute-done((f32[8,32,2048]{2,1,0:T(8,128)}, f32[8,32,2048]{2,1,0:T(8,128)S(1)}, u32[]{:S(2)}, u32[]{:S(2)}) %collective-permute-start) | collective-permute-done | bytes 2097184 | tf_op jit(solution)/shard_map/ppermute | solution.py:1328
  148.7 1.4 copy-done.14
  150.1 7.7 %all-to-all-done.2 = f32[32,64,256]{2,1,0:T(8,128)S(1)} async-done(((f32[32,64,256]{2,1,0:T(8,128)}), f32[32,64,256]{2,1,0:T(8,128)S(1)}, u32[]{:S(2)}, u32[]{:S(2)}) %all-to-all-start.2) | async-done | bytes 2097184 | tf_op jit(solution)/shard_map/all_to_all | solution.py:1300
  157.7 48.9 %all-to-all-start.1 = ((f32[32,64,128]{2,1,0:T(8,128)}), f32[32,64,128]{2,1,0:T(8,128)}, u32[]{:S(2)}, u32[]{:S(2)}) async-start(f32[32,64,128]{2,1,0:T(8,128)} %get-tuple-element.36), calls=%async_computation.1 | async-start | bytes 2097152 | tf_op jit(solution)/shard_map/all_to_all | solution.py:1300
  206.6 10.5 %pair_spec.1.pairs = f32[4,2048,128]{2,1,0:T(8,128)} custom-call(s32[2]{0:T(128)S(1)} %copy-done.11, bf16[12,64,2048]{2,1,0:T(8,128)(2,1)} %bitcast.26, f32[8,32,2048]{2,1,0:T(8,128)} %copy-done.14, f32[4,32,2048]{2,1,0:T(8,128)} %collective-permute-done.1.got_b, f32[12,1,2048]{2,1,0:T(1,128)S(1)} %collective-permute-done.2.edge), custom_call_target="tpu_custom_call" | custom-call | bytes 60000000 | tf_op jit(solution)/shard_map/pair_spec/pallas_call | solution.py:482
  217.1 7.5 %adjoint_columns_a.1 = (f32[2,2048,128]{2,1,0:T(8,128)S(1)}, f32[2048,128]{1,0:T(8,128)S(1)}) custom-call(s32[2]{0:T(128)S(1)} %copy-done.11, f32[2048,256]{1,0:T(8,128)} %bitcast.27, f32[4,2048,128]{2,1,0:T(8,128)} %pair_spec.1.pairs, bf16[16,2,256,256]{3,2,1,0:T(8,128)(2,1)} %constant.37.clone.table), custom_call_target="tpu_custom_call" | custom-call | bytes 20000000 | tf_op jit(solution)/shard_map/adjoint_columns_a/pallas_call | solution.py:752
  224.6 8.1 %all-to-all-done.1 = f32[32,64,128]{2,1,0:T(8,128)} async-done(((f32[32,64,128]{2,1,0:T(8,128)}), f32[32,64,128]{2,1,0:T(8,128)}, u32[]{:S(2)}, u32[]{:S(2)}) %all-to-all-start.1) | async-done | bytes 1048608 | tf_op jit(solution)/shard_map/all_to_all | solution.py:1300
  232.7 10.9 %adjoint_columns_b.1 = f32[32,64,128]{2,1,0:T(8,128)} custom-call(s32[2]{0:T(128)S(1)} %copy-done.11, f32[2048,128]{1,0:T(8,128)} %bitcast.6.spectra, f32[2048,128]{1,0:T(8,128)S(1)} %get-tuple-element.41.edges, f32[2,2048,128]{2,1,0:T(8,128)S(1)} %get-tuple-element.42.sums, bf16[512,128]{1,0:T(8,128)(2,1)S(1)} %copy-done.10, ...), custom_call_target="tpu_custom_call" | custom-call | bytes 20000000 | tf_op jit(solution)/shard_map/adjoint_columns_b/pallas_call | solution.py:848
  243.6 3.8 all-to-all-start.3
  247.5 26.0 %all-to-all-done.3.spectra = f32[32,64,128]{2,1,0:T(8,128)S(1)} async-done(((f32[32,64,128]{2,1,0:T(8,128)}), f32[32,64,128]{2,1,0:T(8,128)S(1)}, u32[]{:S(2)}, u32[]{:S(2)}) %all-to-all-start.3) | async-done | bytes 1048608 | tf_op jit(solution)/shard_map/all_to_all | solution.py:1300
  273.4 8.9 %gradient_rows.1 = (f32[128,2048]{1,0:T(8,128)}, f32[16,192,128]{2,1,0:T(8,128)}) custom-call(s32[16]{0:T(128)S(1)} %bitcast.21, s32[2048]{0:T(1024)S(1)} %bitcast.18, f32[32,64,128]{2,1,0:T(8,128)S(1)} %all-to-all-done.3.spectra, bf16[4,2,2,1024,256]{4,3,2,1,0:T(8,128)(2,1)} %constant.36.clone.table), custom_call_target="tpu_custom_call" | custom-call | tf_op jit(solution)/shard_map/gradient_rows/pallas_call | solution.py:1127
  282.4 3.9 all-to-all-start.4
  286.3 3.4 copied.1
  289.7 28.6 %all-to-all-done.4.incoming = f32[16,192,128]{2,1,0:T(8,128)S(1)} async-done(((f32[16,192,128]{2,1,0:T(8,128)}), f32[16,192,128]{2,1,0:T(8,128)S(1)}, u32[]{:S(2)}, u32[]{:S(2)}) %all-to-all-start.4) | async-done | bytes 1572896 | tf_op jit(solution)/shard_map/all_to_all | solution.py:1300
  318.3 1.1 copy-done.6
  319.4 1.1 owner_send.1
  320.5 45.3 %all_to_all.52.returned = f32[16,192,128]{2,1,0:T(8,128)S(1)} all-to-all(f32[16,192,128]{2,1,0:T(8,128)S(1)} %owner_send.1), channel_id=1, replica_groups=mesh['grp'=1,'pen'=16,'dep'=2,'chan'=1] {'pen'}, dimensions={0} | all-to-all | bytes 3145728 | tf_op jit(solution)/shard_map/all_to_all | solution.py:1300
  365.7 7.9 %model_rows.1 = f32[32,64,128]{2,1,0:T(8,128)} custom-call(s32[16]{0:T(128)S(1)} %bitcast.22, s32[2048]{0:T(1024)S(1)} %bitcast.19, f32[16,192,128]{2,1,0:T(8,128)S(1)} %all_to_all.52.returned, bf16[8,1024,256]{2,1,0:T(8,128)(2,1)S(1)} %copy-done.3, bf16[8,1024,256]{2,1,0:T(8,128)(2,1)S(1)} %copy-done.1), custom_call_target="tpu_custom_call" | custom-call | tf_op jit(solution)/shard_map/model_rows/pallas_call | solution.py:1272
  373.6 4.2 all-to-all-start.6
  377.8 0.0 copy-start.7
  377.8 1.1 copy-done.7
  378.9 2.6 owner_keep.1
  381.5 22.5 %all-to-all-done.6.moved = f32[32,64,128]{2,1,0:T(8,128)} async-done(((f32[32,64,128]{2,1,0:T(8,128)}), f32[32,64,128]{2,1,0:T(8,128)}, u32[]{:S(2)}, u32[]{:S(2)}) %all-to-all-start.6) | async-done | bytes 1048608 | tf_op jit(solution)/shard_map/all_to_all | solution.py:1300
  404.0 11.2 %forward_columns_b.1 = (f32[2048,128]{1,0:T(8,128)}, f32[2048,128]{1,0:T(8,128)}, f32[16,256,128]{2,1,0:T(8,128)}) custom-call(s32[2]{0:T(128)S(1)} %copy-done.11, f32[32,64,128]{2,1,0:T(8,128)} %all-to-all-done.6.moved, bf16[256,256]{1,0:T(8,128)(2,1)S(1)} %copy-done.9, f32[4,2048,128]{2,1,0:T(8,128)} %pair_spec.1.pairs, ...), custom_call_target="tpu_custom_call" | custom-call | bytes 20000000 | tf_op jit(solution)/shard_map/forward_columns_b/pallas_call | solution.py:942
  415.2 3.9 all-to-all-start.8
  419.1 8.0 %forward_columns_a.1 = f32[2048,256]{1,0:T(8,128)} custom-call(s32[2]{0:T(128)S(1)} %copy-done.11, f32[16,256,128]{2,1,0:T(8,128)} %get-tuple-element.56.model, f32[2048,128]{1,0:T(8,128)} %get-tuple-element.57.edges, f32[4,2048,128]{2,1,0:T(8,128)} %pair_spec.1.pairs, bf16[16,2,256,256]{3,2,1,0:T(8,128)(2,1)} %constant.38.clone.table_i), custom_call_target="tpu_custom_call" | custom-call | bytes 16000000 | tf_op jit(solution)/shard_map/forward_columns_a/pallas_call | solution.py:1031
  427.1 17.9 %all-to-all-done.8.spectra = f32[32,64,128]{2,1,0:T(8,128)S(1)} async-done(((f32[32,64,128]{2,1,0:T(8,128)}), f32[32,64,128]{2,1,0:T(8,128)S(1)}, u32[]{:S(2)}, u32[]{:S(2)}) %all-to-all-start.8) | async-done | bytes 1048608 | tf_op jit(solution)/shard_map/all_to_all | solution.py:1300
  445.1 3.6 all-to-all-start.7
  448.7 6.4 %predicted_rows_b.1.refs_0_ = f32[6,64,2048]{2,1,0:T(8,128)} custom-call(f32[32,64,128]{2,1,0:T(8,128)S(1)} %all-to-all-done.8.spectra, bf16[4,2,2,1024,256]{4,3,2,1,0:T(8,128)(2,1)} %constant.36.clone.table), custom_call_target="tpu_custom_call" | custom-call | tf_op jit(solution)/shard_map/predicted_rows_b/pallas_call | solution.py:637
  455.1 42.3 %all-to-all-done.7.spectra = f32[32,64,256]{2,1,0:T(8,128)S(1)} async-done(((f32[32,64,256]{2,1,0:T(8,128)}), f32[32,64,256]{2,1,0:T(8,128)S(1)}, u32[]{:S(2)}, u32[]{:S(2)}) %all-to-all-start.7) | async-done | bytes 2097184 | tf_op jit(solution)/shard_map/all_to_all | solution.py:1300
  497.4 7.7 %predicted_rows_a.1 = f32[6,64,2048]{2,1,0:T(8,128)} custom-call(f32[32,64,256]{2,1,0:T(8,128)S(1)} %all-to-all-done.7.spectra, bf16[4,2,2,1024,256]{4,3,2,1,0:T(8,128)(2,1)} %constant.36.clone.table, f32[6,64,2048]{2,1,0:T(8,128)} %predicted_rows_b.1.refs_0_), custom_call_target="tpu_custom_call", output_to_operand_aliasing={{}: (2, {})} | custom-call | tf_op jit(solution)/shard_map/predicted_rows_a/pallas_call | solution.py:637
  (27 shorter events, 0.1 us)
Async XLA Ops:
  1.3 11.0 %copy-start.12 = (s32[1,1,16]{2,1,0:T(1,128)S(1)}, s32[1,1,16]{2,1,0:T(1,128)}, u32[]{:S(2)}) copy-start(s32[1,1,16]{2,1,0:T(1,128)} %param.18) | copy-start | bytes 196
  3.6 57.2 %collective-permute-start.1 = (f32[4,32,2048]{2,1,0:T(8,128)}, f32[4,32,2048]{2,1,0:T(8,128)}, u32[]{:S(2)}, u32[]{:S(2)}) collective-permute-start(f32[4,32,2048]{2,1,0:T(8,128)} %part_spec.3), channel_id=1, source_target_pairs={{0,31},{1,30},{2,29},{3,28},{4,27},{5,26},{6,25},{7,24},{8,23},{9,... | collective-permute-start | bytes 3145736 | tf_op jit(solution)/shard_map/ppermute | solution.py:1326
  11.0 49.8 %collective-permute-start.2 = (f32[12,1,2048]{2,1,0:T(1,128)S(1)}, f32[12,1,2048]{2,1,0:T(1,128)S(1)}, u32[]{:S(2)}, u32[]{:S(2)}) collective-permute-start(f32[12,1,2048]{2,1,0:T(1,128)S(1)} %slice_convert_fusion), channel_id=1, source_target_pairs={{16,0},{17,15},{18,14},{19,13},{20,12},{21,11},{22,10},{23,9},{24,... | collective-permute-start | bytes 294920 | tf_op jit(solution)/shard_map/ppermute | solution.py:1329
  13.0 47.5 %all-to-all-start = ((s32[16,1,1]{2,1,0:T(1,128)}), s32[16,1,1]{2,1,0:T(1,128)S(1)}, u32[]{:S(2)}, u32[]{:S(2)}) async-start(s32[16,1,1]{2,1,0:T(1,128)} %copy.18), calls=%async_computation | async-start | bytes 16384 | tf_op jit(solution)/shard_map/all_to_all | solution.py:1300
  19.7 4.3 copy-start.5
  24.1 2.2 copy-start
  26.3 2.2 copy-start.2
  37.4 1.3 copy-start.8
  60.9 96.9 %all-to-all-start.2 = ((f32[32,64,256]{2,1,0:T(8,128)}), f32[32,64,256]{2,1,0:T(8,128)S(1)}, u32[]{:S(2)}, u32[]{:S(2)}) async-start(f32[32,64,256]{2,1,0:T(8,128)} %copy-done.8), calls=%async_computation.2 | async-start | bytes 4194304 | tf_op jit(solution)/shard_map/all_to_all | solution.py:1300
  63.6 143.0 %copy-start.11 = (s32[2]{0:T(128)S(1)}, s32[2]{0:T(128)}, u32[]{:S(2)}) copy-start(s32[2]{0:T(128)} %add_convert_fusion.flags) | copy-start | bytes 28
  63.6 85.0 %collective-permute-start = (f32[8,32,2048]{2,1,0:T(8,128)}, f32[8,32,2048]{2,1,0:T(8,128)S(1)}, u32[]{:S(2)}, u32[]{:S(2)}) collective-permute-start(f32[8,32,2048]{2,1,0:T(8,128)} %part_spec.2), channel_id=1, source_target_pairs={{0,31},{1,30},{2,29},{3,28},{4,27},{5,26},{6,25},{7,24},{8,23},{9,... | collective-permute-start | bytes 6291464 | tf_op jit(solution)/shard_map/ppermute | solution.py:1328
  148.7 1.4 copy-start.14
  157.7 59.4 %copy-start.13 = (f32[32,64,256]{2,1,0:T(8,128)}, f32[32,64,256]{2,1,0:T(8,128)S(1)}, u32[]{:S(2)}) copy-start(f32[32,64,256]{2,1,0:T(8,128)S(1)} %all-to-all-done.2) | copy-start | bytes 6291460
  157.7 74.9 %all-to-all-start.1 = ((f32[32,64,128]{2,1,0:T(8,128)}), f32[32,64,128]{2,1,0:T(8,128)}, u32[]{:S(2)}, u32[]{:S(2)}) async-start(f32[32,64,128]{2,1,0:T(8,128)} %get-tuple-element.36), calls=%async_computation.1 | async-start | bytes 2097152 | tf_op jit(solution)/shard_map/all_to_all | solution.py:1300
  217.1 15.6 %copy-start.10 = (bf16[512,128]{1,0:T(8,128)(2,1)S(1)}, bf16[512,128]{1,0:T(8,128)(2,1)}, u32[]{:S(2)}) copy-start(bf16[512,128]{1,0:T(8,128)(2,1)} %constant.39.clone.fold) | copy-start | bytes 393220
  243.6 3.9 copy-start.15
  243.6 29.9 %all-to-all-start.3 = ((f32[32,64,128]{2,1,0:T(8,128)}), f32[32,64,128]{2,1,0:T(8,128)S(1)}, u32[]{:S(2)}, u32[]{:S(2)}) async-start(f32[32,64,128]{2,1,0:T(8,128)} %adjoint_columns_b.1), calls=%async_computation.3 | async-start | bytes 2097152 | tf_op jit(solution)/shard_map/all_to_all | solution.py:1300
  282.4 35.9 %copy-start.4 = (f32[1,1,3072,128]{3,2,1,0:T(8,128)S(1)}, f32[1,1,3072,128]{3,2,1,0:T(8,128)}, u32[]{:S(2)}) copy-start(f32[1,1,3072,128]{3,2,1,0:T(8,128)} %param.15) | copy-start | bytes 4718596
  282.4 35.9 %all-to-all-start.4 = ((f32[16,192,128]{2,1,0:T(8,128)}), f32[16,192,128]{2,1,0:T(8,128)S(1)}, u32[]{:S(2)}, u32[]{:S(2)}) async-start(f32[16,192,128]{2,1,0:T(8,128)} %get-tuple-element.49), calls=%async_computation.4 | async-start | bytes 3145728 | tf_op jit(solution)/shard_map/all_to_all | solution.py:1300
  318.3 1.1 copy-start.6
  319.4 46.3 %copy-start.1 = (bf16[8,1024,256]{2,1,0:T(8,128)(2,1)S(1)}, bf16[8,1024,256]{2,1,0:T(8,128)(2,1)}, u32[]{:S(2)}) copy-start(bf16[8,1024,256]{2,1,0:T(8,128)(2,1)} %constant.35.clone.low) | copy-start | bytes 12582916
  319.4 46.3 %copy-start.3 = (bf16[8,1024,256]{2,1,0:T(8,128)(2,1)S(1)}, bf16[8,1024,256]{2,1,0:T(8,128)(2,1)}, u32[]{:S(2)}) copy-start(bf16[8,1024,256]{2,1,0:T(8,128)(2,1)} %constant.34.clone.high) | copy-start | bytes 12582916
  373.6 30.4 %all-to-all-start.6 = ((f32[32,64,128]{2,1,0:T(8,128)}), f32[32,64,128]{2,1,0:T(8,128)}, u32[]{:S(2)}, u32[]{:S(2)}) async-start(f32[32,64,128]{2,1,0:T(8,128)} %model_rows.1), calls=%async_computation.6 | async-start | bytes 2097152 | tf_op jit(solution)/shard_map/all_to_all | solution.py:1300
  377.8 1.1 copy-start.7
  378.9 25.1 %copy-start.9 = (bf16[256,256]{1,0:T(8,128)(2,1)S(1)}, bf16[256,256]{1,0:T(8,128)(2,1)}, u32[]{:S(2)}) copy-start(bf16[256,256]{1,0:T(8,128)(2,1)} %constant.40.clone.spread) | copy-start | bytes 393220
  415.2 29.9 %all-to-all-start.8 = ((f32[32,64,128]{2,1,0:T(8,128)}), f32[32,64,128]{2,1,0:T(8,128)S(1)}, u32[]{:S(2)}, u32[]{:S(2)}) async-start(f32[32,64,128]{2,1,0:T(8,128)} %bitcast.31), calls=%async_computation.8 | async-start | bytes 2097152 | tf_op jit(solution)/shard_map/all_to_all | solution.py:1300
  445.1 52.4 %all-to-all-start.7 = ((f32[32,64,256]{2,1,0:T(8,128)}), f32[32,64,256]{2,1,0:T(8,128)S(1)}, u32[]{:S(2)}, u32[]{:S(2)}) async-start(f32[32,64,256]{2,1,0:T(8,128)} %bitcast.28), calls=%async_computation.7 | async-start | bytes 4194304 | tf_op jit(solution)/shard_map/all_to_all | solution.py:1300

commit v5 on v4

--- a/solution.py
+++ b/solution.py
@@ -808,7 +808,9 @@
         for copy in later[group][:2]:
             copy.wait()
         for k in in_group(group):
-            spectrum = stacked_product(held_table, k, work[k])
+            work[k] = stacked_product(held_table, k, work[k])
+        for k in in_group(group):
+            spectrum = work[k]
             row = slice(k * LANES, (k + 1) * LANES)
             parts = []
             for value in turn_phase(turned, spectrum[:LANES], spectrum[LANES:], -1):
@@ -907,8 +909,9 @@
         for copy in later[group]:
             copy.wait()
         for k in in_group(group):
-            spectrum = table_product(held_table, k, work[k])
-            held_model[k] = spectrum
+            held_model[k] = table_product(held_table, k, work[k])
+        for k in in_group(group):
+            spectrum = held_model[k]
             row = slice(k * LANES, (k + 1) * LANES)
             both = dot(jnp.concatenate(split(spectrum), axis=1), spread[...])
             totals = [

time: 507 us -> 505 us (level)
  no operation moved by 1% of the time
where the time goes in v5:
time: 505 us; the launch traced here: 503 us
  waiting for transfers between devices  255 us (50%)
  Pallas kernels  99.5 us (20%)
  starting transfers between devices  90.7 us (18%)
  blocking collectives  45.3 us (9%)
  local copies, waits for them, and re-layouts  10.1 us (2%)
    all_to_all x8, waiting for transfers between devices, swap_all(): return lax.all_to_all(value, axes, split_axis=0, concat_axis=0, tiled=True)  175 us
    ppermute x1, waiting for transfers between devices, local_paired(): got_a = lax.ppermute(sent_a, both, partner)  79.8 us
    all_to_all x8, starting transfers between devices, swap_all(): return lax.all_to_all(value, axes, split_axis=0, concat_axis=0, tiled=True)  77.7 us
    all_to_all x1, blocking collectives, swap_all(): return lax.all_to_all(value, axes, split_axis=0, concat_axis=0, tiled=True)  45.3 us
    pallas_call x2, Pallas kernels, predicted_rows(): pl.pallas_call(functools.partial(predicted_kernel, begin, count), grid=(T...  14.1 us
    pallas_call x1, Pallas kernels, pair_spec(): pl.pallas_call(pair_kernel, grid=(4,), out_shape=pltpu.HBM((4, n, LANES),...  10.5 us
  transfers between devices with their start and end apart: 11, of which 9 were waited for; matrix products, arithmetic and copies ran while one was open for 0% of the time, Pallas kernels for 10%

profile of v5, /device:TPU:0, one launch (start us, length us, event | category | flops | bytes accessed | tf_op | source)
XLA Modules:
  0.0 503.3 jit_solution(16280892150106405485)
XLA Ops:
  0.6 0.7 add_convert_fusion.flags
  1.3 2.3 part_spec.3
  3.6 6.4 %collective-permute-start.1 = (f32[4,32,2048]{2,1,0:T(8,128)}, f32[4,32,2048]{2,1,0:T(8,128)}, u32[]{:S(2)}, u32[]{:S(2)}) collective-permute-start(f32[4,32,2048]{2,1,0:T(8,128)} %part_spec.3), channel_id=1, source_target_pairs={{0,31},{1,30},{2,29},{3,28},{4,27},{5,26},{6,25},{7,24},{8,23},{9,... | collective-permute-start | bytes 3145736 | tf_op jit(solution)/shard_map/ppermute | solution.py:1329
  10.0 1.0 slice_convert_fusion
  11.0 1.3 collective-permute-start.2
  12.3 0.7 copy.18
  13.0 6.7 %all-to-all-start = ((s32[16,1,1]{2,1,0:T(1,128)}), s32[16,1,1]{2,1,0:T(1,128)S(1)}, u32[]{:S(2)}, u32[]{:S(2)}) async-start(s32[16,1,1]{2,1,0:T(1,128)} %copy.18), calls=%async_computation | async-start | bytes 16384 | tf_op jit(solution)/shard_map/all_to_all | solution.py:1303
  19.7 0.0 copy-start.5
  19.7 4.3 part_spec.2
  24.1 2.2 copy-done
  26.3 2.2 copy-done.2
  28.4 9.0 %misfit_rows.1 = (f32[32,64,256]{2,1,0:T(8,128)S(1)}, f32[32,64,128]{2,1,0:T(8,128)}) custom-call(f32[6,64,2048]{2,1,0:T(8,128)S(1)} %copy-done.5, bf16[8,1024,256]{2,1,0:T(8,128)(2,1)S(1)} %copy-done.2, bf16[8,1024,256]{2,1,0:T(8,128)(2,1)S(1)} %copy-done), custom_call_target="tpu_custom_call" | custom-call | tf_op jit(solution)/shard_map/misfit_rows/pallas_call | solution.py:533
  37.4 1.3 copy-done.8
  38.8 21.7 %all-to-all-done = s32[16,1,1]{2,1,0:T(1,128)S(1)} async-done(((s32[16,1,1]{2,1,0:T(1,128)}), s32[16,1,1]{2,1,0:T(1,128)S(1)}, u32[]{:S(2)}, u32[]{:S(2)}) %all-to-all-start) | async-done | bytes 96 | tf_op jit(solution)/shard_map/all_to_all | solution.py:1303
  60.5 0.4 reduce.counts
  60.9 2.7 all-to-all-start.2
  63.6 5.3 %collective-permute-start = (f32[8,32,2048]{2,1,0:T(8,128)}, f32[8,32,2048]{2,1,0:T(8,128)S(1)}, u32[]{:S(2)}, u32[]{:S(2)}) collective-permute-start(f32[8,32,2048]{2,1,0:T(8,128)} %part_spec.2), channel_id=1, source_target_pairs={{0,31},{1,30},{2,29},{3,28},{4,27},{5,26},{6,25},{7,24},{8,23},{9,... | collective-permute-start | bytes 6291464 | tf_op jit(solution)/shard_map/ppermute | solution.py:1331
  68.9 79.8 %collective-permute-done.got_a = f32[8,32,2048]{2,1,0:T(8,128)S(1)} collective-permute-done((f32[8,32,2048]{2,1,0:T(8,128)}, f32[8,32,2048]{2,1,0:T(8,128)S(1)}, u32[]{:S(2)}, u32[]{:S(2)}) %collective-permute-start) | collective-permute-done | bytes 2097184 | tf_op jit(solution)/shard_map/ppermute | solution.py:1331
  148.7 1.4 copy-done.14
  150.1 7.7 %all-to-all-done.2 = f32[32,64,256]{2,1,0:T(8,128)S(1)} async-done(((f32[32,64,256]{2,1,0:T(8,128)}), f32[32,64,256]{2,1,0:T(8,128)S(1)}, u32[]{:S(2)}, u32[]{:S(2)}) %all-to-all-start.2) | async-done | bytes 2097184 | tf_op jit(solution)/shard_map/all_to_all | solution.py:1303
  157.7 48.9 %all-to-all-start.1 = ((f32[32,64,128]{2,1,0:T(8,128)}), f32[32,64,128]{2,1,0:T(8,128)}, u32[]{:S(2)}, u32[]{:S(2)}) async-start(f32[32,64,128]{2,1,0:T(8,128)} %get-tuple-element.36), calls=%async_computation.1 | async-start | bytes 2097152 | tf_op jit(solution)/shard_map/all_to_all | solution.py:1303
  206.6 10.5 %pair_spec.1.pairs = f32[4,2048,128]{2,1,0:T(8,128)} custom-call(s32[2]{0:T(128)S(1)} %copy-done.11, bf16[12,64,2048]{2,1,0:T(8,128)(2,1)} %bitcast.26, f32[8,32,2048]{2,1,0:T(8,128)} %copy-done.14, f32[4,32,2048]{2,1,0:T(8,128)} %collective-permute-done.1.got_b, f32[12,1,2048]{2,1,0:T(1,128)S(1)} %collective-permute-done.2.edge), custom_call_target="tpu_custom_call" | custom-call | bytes 60000000 | tf_op jit(solution)/shard_map/pair_spec/pallas_call | solution.py:482
  217.1 7.5 %adjoint_columns_a.1 = (f32[2,2048,128]{2,1,0:T(8,128)S(1)}, f32[2048,128]{1,0:T(8,128)S(1)}) custom-call(s32[2]{0:T(128)S(1)} %copy-done.11, f32[2048,256]{1,0:T(8,128)} %bitcast.27, f32[4,2048,128]{2,1,0:T(8,128)} %pair_spec.1.pairs, bf16[16,2,256,256]{3,2,1,0:T(8,128)(2,1)} %constant.37.clone.table), custom_call_target="tpu_custom_call" | custom-call | bytes 20000000 | tf_op jit(solution)/shard_map/adjoint_columns_a/pallas_call | solution.py:752
  224.6 8.1 %all-to-all-done.1 = f32[32,64,128]{2,1,0:T(8,128)} async-done(((f32[32,64,128]{2,1,0:T(8,128)}), f32[32,64,128]{2,1,0:T(8,128)}, u32[]{:S(2)}, u32[]{:S(2)}) %all-to-all-start.1) | async-done | bytes 1048608 | tf_op jit(solution)/shard_map/all_to_all | solution.py:1303
  232.7 9.9 %adjoint_columns_b.1 = f32[32,64,128]{2,1,0:T(8,128)} custom-call(s32[2]{0:T(128)S(1)} %copy-done.11, f32[2048,128]{1,0:T(8,128)} %bitcast.6.spectra, f32[2048,128]{1,0:T(8,128)S(1)} %get-tuple-element.41.edges, f32[2,2048,128]{2,1,0:T(8,128)S(1)} %get-tuple-element.42.sums, bf16[512,128]{1,0:T(8,128)(2,1)S(1)} %copy-done.10, ...), custom_call_target="tpu_custom_call" | custom-call | bytes 20000000 | tf_op jit(solution)/shard_map/adjoint_columns_b/pallas_call | solution.py:850
  242.6 0.0 copy-start.15
  242.6 3.6 all-to-all-start.3
  246.3 26.2 %all-to-all-done.3.spectra = f32[32,64,128]{2,1,0:T(8,128)S(1)} async-done(((f32[32,64,128]{2,1,0:T(8,128)}), f32[32,64,128]{2,1,0:T(8,128)S(1)}, u32[]{:S(2)}, u32[]{:S(2)}) %all-to-all-start.3) | async-done | bytes 1048608 | tf_op jit(solution)/shard_map/all_to_all | solution.py:1303
  272.5 8.9 %gradient_rows.1 = (f32[128,2048]{1,0:T(8,128)}, f32[16,192,128]{2,1,0:T(8,128)}) custom-call(s32[16]{0:T(128)S(1)} %bitcast.21, s32[2048]{0:T(1024)S(1)} %bitcast.18, f32[32,64,128]{2,1,0:T(8,128)S(1)} %all-to-all-done.3.spectra, bf16[4,2,2,1024,256]{4,3,2,1,0:T(8,128)(2,1)} %constant.36.clone.table), custom_call_target="tpu_custom_call" | custom-call | tf_op jit(solution)/shard_map/gradient_rows/pallas_call | solution.py:1130
  281.4 4.1 all-to-all-start.4
  285.5 3.4 copied.1
  288.9 28.4 %all-to-all-done.4.incoming = f32[16,192,128]{2,1,0:T(8,128)S(1)} async-done(((f32[16,192,128]{2,1,0:T(8,128)}), f32[16,192,128]{2,1,0:T(8,128)S(1)}, u32[]{:S(2)}, u32[]{:S(2)}) %all-to-all-start.4) | async-done | bytes 1572896 | tf_op jit(solution)/shard_map/all_to_all | solution.py:1303
  317.3 1.1 copy-done.6
  318.5 1.1 owner_send.1
  319.5 45.3 %all_to_all.52.returned = f32[16,192,128]{2,1,0:T(8,128)S(1)} all-to-all(f32[16,192,128]{2,1,0:T(8,128)S(1)} %owner_send.1), channel_id=1, replica_groups=mesh['grp'=1,'pen'=16,'dep'=2,'chan'=1] {'pen'}, dimensions={0} | all-to-all | bytes 3145728 | tf_op jit(solution)/shard_map/all_to_all | solution.py:1303
  364.8 7.9 %model_rows.1 = f32[32,64,128]{2,1,0:T(8,128)} custom-call(s32[16]{0:T(128)S(1)} %bitcast.22, s32[2048]{0:T(1024)S(1)} %bitcast.19, f32[16,192,128]{2,1,0:T(8,128)S(1)} %all_to_all.52.returned, bf16[8,1024,256]{2,1,0:T(8,128)(2,1)S(1)} %copy-done.3, bf16[8,1024,256]{2,1,0:T(8,128)(2,1)S(1)} %copy-done.1), custom_call_target="tpu_custom_call" | custom-call | tf_op jit(solution)/shard_map/model_rows/pallas_call | solution.py:1275
  372.7 4.1 all-to-all-start.6
  376.8 1.1 copy-done.7
  378.0 2.5 owner_keep.1
  380.5 22.5 %all-to-all-done.6.moved = f32[32,64,128]{2,1,0:T(8,128)} async-done(((f32[32,64,128]{2,1,0:T(8,128)}), f32[32,64,128]{2,1,0:T(8,128)}, u32[]{:S(2)}, u32[]{:S(2)}) %all-to-all-start.6) | async-done | bytes 1048608 | tf_op jit(solution)/shard_map/all_to_all | solution.py:1303
  403.1 10.1 %forward_columns_b.1 = (f32[2048,128]{1,0:T(8,128)}, f32[2048,128]{1,0:T(8,128)}, f32[16,256,128]{2,1,0:T(8,128)}) custom-call(s32[2]{0:T(128)S(1)} %copy-done.11, f32[32,64,128]{2,1,0:T(8,128)} %all-to-all-done.6.moved, bf16[256,256]{1,0:T(8,128)(2,1)S(1)} %copy-done.9, f32[4,2048,128]{2,1,0:T(8,128)} %pair_spec.1.pairs, ...), custom_call_target="tpu_custom_call" | custom-call | bytes 20000000 | tf_op jit(solution)/shard_map/forward_columns_b/pallas_call | solution.py:945
  413.1 3.6 all-to-all-start.8
  416.8 8.0 %forward_columns_a.1 = f32[2048,256]{1,0:T(8,128)} custom-call(s32[2]{0:T(128)S(1)} %copy-done.11, f32[16,256,128]{2,1,0:T(8,128)} %get-tuple-element.56.model, f32[2048,128]{1,0:T(8,128)} %get-tuple-element.57.edges, f32[4,2048,128]{2,1,0:T(8,128)} %pair_spec.1.pairs, bf16[16,2,256,256]{3,2,1,0:T(8,128)(2,1)} %constant.38.clone.table_i), custom_call_target="tpu_custom_call" | custom-call | bytes 16000000 | tf_op jit(solution)/shard_map/forward_columns_a/pallas_call | solution.py:1034
  424.8 18.2 %all-to-all-done.8.spectra = f32[32,64,128]{2,1,0:T(8,128)S(1)} async-done(((f32[32,64,128]{2,1,0:T(8,128)}), f32[32,64,128]{2,1,0:T(8,128)S(1)}, u32[]{:S(2)}, u32[]{:S(2)}) %all-to-all-start.8) | async-done | bytes 1048608 | tf_op jit(solution)/shard_map/all_to_all | solution.py:1303
  443.0 3.9 all-to-all-start.7
  446.9 6.4 %predicted_rows_b.1.refs_0_ = f32[6,64,2048]{2,1,0:T(8,128)} custom-call(f32[32,64,128]{2,1,0:T(8,128)S(1)} %all-to-all-done.8.spectra, bf16[4,2,2,1024,256]{4,3,2,1,0:T(8,128)(2,1)} %constant.36.clone.table), custom_call_target="tpu_custom_call" | custom-call | tf_op jit(solution)/shard_map/predicted_rows_b/pallas_call | solution.py:637
  453.3 42.1 %all-to-all-done.7.spectra = f32[32,64,256]{2,1,0:T(8,128)S(1)} async-done(((f32[32,64,256]{2,1,0:T(8,128)}), f32[32,64,256]{2,1,0:T(8,128)S(1)}, u32[]{:S(2)}, u32[]{:S(2)}) %all-to-all-start.7) | async-done | bytes 2097184 | tf_op jit(solution)/shard_map/all_to_all | solution.py:1303
  495.4 7.7 %predicted_rows_a.1 = f32[6,64,2048]{2,1,0:T(8,128)} custom-call(f32[32,64,256]{2,1,0:T(8,128)S(1)} %all-to-all-done.7.spectra, bf16[4,2,2,1024,256]{4,3,2,1,0:T(8,128)(2,1)} %constant.36.clone.table, f32[6,64,2048]{2,1,0:T(8,128)} %predicted_rows_b.1.refs_0_), custom_call_target="tpu_custom_call", output_to_operand_aliasing={{}: (2, {})} | custom-call | tf_op jit(solution)/shard_map/predicted_rows_a/pallas_call | solution.py:637
  (27 shorter events, 0.1 us)
Async XLA Ops:
  1.3 11.0 %copy-start.12 = (s32[1,1,16]{2,1,0:T(1,128)S(1)}, s32[1,1,16]{2,1,0:T(1,128)}, u32[]{:S(2)}) copy-start(s32[1,1,16]{2,1,0:T(1,128)} %param.18) | copy-start | bytes 196
  3.6 57.2 %collective-permute-start.1 = (f32[4,32,2048]{2,1,0:T(8,128)}, f32[4,32,2048]{2,1,0:T(8,128)}, u32[]{:S(2)}, u32[]{:S(2)}) collective-permute-start(f32[4,32,2048]{2,1,0:T(8,128)} %part_spec.3), channel_id=1, source_target_pairs={{0,31},{1,30},{2,29},{3,28},{4,27},{5,26},{6,25},{7,24},{8,23},{9,... | collective-permute-start | bytes 3145736 | tf_op jit(solution)/shard_map/ppermute | solution.py:1329
  11.0 49.8 %collective-permute-start.2 = (f32[12,1,2048]{2,1,0:T(1,128)S(1)}, f32[12,1,2048]{2,1,0:T(1,128)S(1)}, u32[]{:S(2)}, u32[]{:S(2)}) collective-permute-start(f32[12,1,2048]{2,1,0:T(1,128)S(1)} %slice_convert_fusion), channel_id=1, source_target_pairs={{16,0},{17,15},{18,14},{19,13},{20,12},{21,11},{22,10},{23,9},{24,... | collective-permute-start | bytes 294920 | tf_op jit(solution)/shard_map/ppermute | solution.py:1332
  13.0 47.5 %all-to-all-start = ((s32[16,1,1]{2,1,0:T(1,128)}), s32[16,1,1]{2,1,0:T(1,128)S(1)}, u32[]{:S(2)}, u32[]{:S(2)}) async-start(s32[16,1,1]{2,1,0:T(1,128)} %copy.18), calls=%async_computation | async-start | bytes 16384 | tf_op jit(solution)/shard_map/all_to_all | solution.py:1303
  19.7 4.3 copy-start.5
  24.1 2.2 copy-start
  26.3 2.2 copy-start.2
  37.4 1.3 copy-start.8
  60.9 96.9 %all-to-all-start.2 = ((f32[32,64,256]{2,1,0:T(8,128)}), f32[32,64,256]{2,1,0:T(8,128)S(1)}, u32[]{:S(2)}, u32[]{:S(2)}) async-start(f32[32,64,256]{2,1,0:T(8,128)} %copy-done.8), calls=%async_computation.2 | async-start | bytes 4194304 | tf_op jit(solution)/shard_map/all_to_all | solution.py:1303
  63.6 143.0 %copy-start.11 = (s32[2]{0:T(128)S(1)}, s32[2]{0:T(128)}, u32[]{:S(2)}) copy-start(s32[2]{0:T(128)} %add_convert_fusion.flags) | copy-start | bytes 28
  63.6 85.0 %collective-permute-start = (f32[8,32,2048]{2,1,0:T(8,128)}, f32[8,32,2048]{2,1,0:T(8,128)S(1)}, u32[]{:S(2)}, u32[]{:S(2)}) collective-permute-start(f32[8,32,2048]{2,1,0:T(8,128)} %part_spec.2), channel_id=1, source_target_pairs={{0,31},{1,30},{2,29},{3,28},{4,27},{5,26},{6,25},{7,24},{8,23},{9,... | collective-permute-start | bytes 6291464 | tf_op jit(solution)/shard_map/ppermute | solution.py:1331
  148.7 1.4 copy-start.14
  157.7 59.4 %copy-start.13 = (f32[32,64,256]{2,1,0:T(8,128)}, f32[32,64,256]{2,1,0:T(8,128)S(1)}, u32[]{:S(2)}) copy-start(f32[32,64,256]{2,1,0:T(8,128)S(1)} %all-to-all-done.2) | copy-start | bytes 6291460
  157.7 74.9 %all-to-all-start.1 = ((f32[32,64,128]{2,1,0:T(8,128)}), f32[32,64,128]{2,1,0:T(8,128)}, u32[]{:S(2)}, u32[]{:S(2)}) async-start(f32[32,64,128]{2,1,0:T(8,128)} %get-tuple-element.36), calls=%async_computation.1 | async-start | bytes 2097152 | tf_op jit(solution)/shard_map/all_to_all | solution.py:1303
  217.1 15.6 %copy-start.10 = (bf16[512,128]{1,0:T(8,128)(2,1)S(1)}, bf16[512,128]{1,0:T(8,128)(2,1)}, u32[]{:S(2)}) copy-start(bf16[512,128]{1,0:T(8,128)(2,1)} %constant.39.clone.fold) | copy-start | bytes 393220
  242.6 3.6 copy-start.15
  242.6 29.9 %all-to-all-start.3 = ((f32[32,64,128]{2,1,0:T(8,128)}), f32[32,64,128]{2,1,0:T(8,128)S(1)}, u32[]{:S(2)}, u32[]{:S(2)}) async-start(f32[32,64,128]{2,1,0:T(8,128)} %adjoint_columns_b.1), calls=%async_computation.3 | async-start | bytes 2097152 | tf_op jit(solution)/shard_map/all_to_all | solution.py:1303
  281.4 35.9 %copy-start.4 = (f32[1,1,3072,128]{3,2,1,0:T(8,128)S(1)}, f32[1,1,3072,128]{3,2,1,0:T(8,128)}, u32[]{:S(2)}) copy-start(f32[1,1,3072,128]{3,2,1,0:T(8,128)} %param.15) | copy-start | bytes 4718596
  281.4 35.9 %all-to-all-start.4 = ((f32[16,192,128]{2,1,0:T(8,128)}), f32[16,192,128]{2,1,0:T(8,128)S(1)}, u32[]{:S(2)}, u32[]{:S(2)}) async-start(f32[16,192,128]{2,1,0:T(8,128)} %get-tuple-element.49), calls=%async_computation.4 | async-start | bytes 3145728 | tf_op jit(solution)/shard_map/all_to_all | solution.py:1303
  317.3 1.1 copy-start.6
  318.5 46.3 %copy-start.1 = (bf16[8,1024,256]{2,1,0:T(8,128)(2,1)S(1)}, bf16[8,1024,256]{2,1,0:T(8,128)(2,1)}, u32[]{:S(2)}) copy-start(bf16[8,1024,256]{2,1,0:T(8,128)(2,1)} %constant.35.clone.low) | copy-start | bytes 12582916
  318.5 46.3 %copy-start.3 = (bf16[8,1024,256]{2,1,0:T(8,128)(2,1)S(1)}, bf16[8,1024,256]{2,1,0:T(8,128)(2,1)}, u32[]{:S(2)}) copy-start(bf16[8,1024,256]{2,1,0:T(8,128)(2,1)} %constant.34.clone.high) | copy-start | bytes 12582916
  372.7 30.4 %all-to-all-start.6 = ((f32[32,64,128]{2,1,0:T(8,128)}), f32[32,64,128]{2,1,0:T(8,128)}, u32[]{:S(2)}, u32[]{:S(2)}) async-start(f32[32,64,128]{2,1,0:T(8,128)} %model_rows.1), calls=%async_computation.6 | async-start | bytes 2097152 | tf_op jit(solution)/shard_map/all_to_all | solution.py:1303
  376.8 1.1 copy-start.7
  378.0 25.1 %copy-start.9 = (bf16[256,256]{1,0:T(8,128)(2,1)S(1)}, bf16[256,256]{1,0:T(8,128)(2,1)}, u32[]{:S(2)}) copy-start(bf16[256,256]{1,0:T(8,128)(2,1)} %constant.40.clone.spread) | copy-start | bytes 393220
  413.1 29.9 %all-to-all-start.8 = ((f32[32,64,128]{2,1,0:T(8,128)}), f32[32,64,128]{2,1,0:T(8,128)S(1)}, u32[]{:S(2)}, u32[]{:S(2)}) async-start(f32[32,64,128]{2,1,0:T(8,128)} %bitcast.31), calls=%async_computation.8 | async-start | bytes 2097152 | tf_op jit(solution)/shard_map/all_to_all | solution.py:1303
  443.0 52.4 %all-to-all-start.7 = ((f32[32,64,256]{2,1,0:T(8,128)}), f32[32,64,256]{2,1,0:T(8,128)S(1)}, u32[]{:S(2)}, u32[]{:S(2)}) async-start(f32[32,64,256]{2,1,0:T(8,128)} %bitcast.28), calls=%async_computation.7 | async-start | bytes 4194304 | tf_op jit(solution)/shard_map/all_to_all | solution.py:1303
